TPU v7x, 256 devices: a whole 4x4x8 slice. The times are simulated.
256 devices in a mesh: store: 32 (over y, x, core), trainer: 8 (over z).
Axes of the slice: x: 4, y: 4, z: 8, core: 2. Of those that a mesh axis runs over, the one named last changes fastest.
Arguments:
- features: bfloat16 [131072, 768], P('store'), may hold values from -6 to 6
- self_one: bfloat16 [768, 512], replicated, may hold values from -0.21875 to 0.21875
- neigh_one: bfloat16 [768, 512], replicated, may hold values from -0.21875 to 0.21875
- self_two: bfloat16 [512, 153], replicated, may hold values from -0.25 to 0.25
- neigh_two: bfloat16 [512, 153], replicated, may hold values from -0.25 to 0.25
- bucket_counts: int32 [2, 256, 32], P(None, ('store', 'trainer')), may hold values from 4 to 16, as said below
- request_rows: int32 [2, 256, 32, 16], P(None, ('store', 'trainer')), may hold values from 0 to 4095, as said below
- layer_targets: int32 [2, 131072], P(None, ('store', 'trainer')), may hold values from 0 to 511, as said below
- inner_slots: int32 [2, 131072, 10], P(None, ('store', 'trainer')), may hold values from 0 to 511, as said below
- outer_slots: int32 [2, 16384, 15], P(None, ('store', 'trainer')), may hold values from 0 to 511
- outer_degree: int32 [2, 16384], P(None, ('store', 'trainer')), may hold values from 0 to 15
- cotangent: bfloat16 [2, 16384, 153], P(None, ('store', 'trainer')), may hold values from -0.046875 to 0.046875
Outputs:
- logits: float32 [2, 16384, 153], P(None, ('store', 'trainer'))
- grad_self_one: float32 [768, 512], replicated
- grad_neigh_one: float32 [768, 512], replicated
- grad_self_two: float32 [512, 153], replicated
- grad_neigh_two: float32 [512, 153], replicated
Inputs may be any that keep to these rules, and one draw needn't show every extreme that they name: Slots 0 to bucket_counts[b, d, o] - 1 of owner o's bucket are live. In every minibatch one owner's bucket is full (16) from every device, and every other bucket has fewer than 16 live slots. `request_rows`: the 16 rows of one device's bucket for one owner are distinct; some rows of an owner are asked for by many devices. `layer_targets`: every entry is a live frontier slot of its minibatch and device. `inner_slots`: every entry is a frontier slot of its minibatch and device; entries whose slot is not live are padding and take no part in the mean.
All inputs are finite; a program needn't handle non-finite values.
Results may differ from a plain program's by a relative error of at most 0.0041.
Values may be sent and summed in bfloat16 or wider, within the bound.
No kernel may reach another device: no remote copies, remote signals or barrier semaphores. Data moves between devices by JAX's collectives and lax.ppermute only.
A program may use at most 192 MiB of HBM per device.

v0:
```python
import jax
import jax.numpy as jnp
from jax import lax
from jax.sharding import PartitionSpec as P


def contract_rows(left, right):
    return lax.dot_general(
        left, right, (((0,), (0,)), ((), ())), preferred_element_type=jnp.float32
    )


def contract_cols(left, right):
    return lax.dot_general(
        left, right, (((1,), (1,)), ((), ())), preferred_element_type=jnp.float32
    )


def silu_slope(values):
    sigmoid = jax.nn.sigmoid(values)
    return sigmoid * (1.0 + values * (1.0 - sigmoid))


def mean_rows(table, slots, weights):
    picked = table[slots].astype(jnp.float32)
    return jnp.sum(weights[:, :, None] * picked, axis=1)


def sage_pass(
    fetched,
    counts,
    layer_targets,
    inner_slots,
    outer_slots,
    outer_degree,
    cotangent,
    self_one,
    neigh_one,
    self_two,
    neigh_two,
):
    slot_count = fetched.shape[0]
    capacity = slot_count // counts.shape[0]
    live_slots = (
        (jnp.arange(capacity, dtype=jnp.int32)[None, :] < counts[:, None])
        .reshape(slot_count)
        .astype(jnp.float32)
    )
    present = live_slots[inner_slots]
    inner_weight = present / jnp.maximum(jnp.sum(present, axis=1, keepdims=True), 1.0)
    inner_mean = mean_rows(fetched, inner_slots, inner_weight).astype(jnp.bfloat16)
    own_rows = fetched[layer_targets]
    pre_one = jnp.dot(own_rows, self_one, preferred_element_type=jnp.float32) + jnp.dot(
        inner_mean, neigh_one, preferred_element_type=jnp.float32
    )
    hidden_one = jax.nn.silu(pre_one).astype(jnp.bfloat16)
    seed_count = outer_slots.shape[0]
    fanout = outer_slots.shape[1]
    seed_rows = hidden_one[:seed_count]
    outer_present = (jnp.arange(fanout, dtype=jnp.int32)[None, :] < outer_degree[:, None]).astype(
        jnp.float32
    )
    outer_weight = outer_present / jnp.maximum(outer_degree[:, None].astype(jnp.float32), 1.0)
    outer_mean = mean_rows(hidden_one, outer_slots, outer_weight).astype(jnp.bfloat16)
    logits = jnp.dot(seed_rows, self_two, preferred_element_type=jnp.float32) + jnp.dot(
        outer_mean, neigh_two, preferred_element_type=jnp.float32
    )
    grad_self_two = contract_rows(seed_rows, cotangent)
    grad_neigh_two = contract_rows(outer_mean, cotangent)
    back_seed = contract_cols(cotangent, self_two)
    back_mean = contract_cols(cotangent, neigh_two)
    spread = (back_mean[:, None, :] * outer_weight[:, :, None]).reshape(
        seed_count * fanout, back_mean.shape[1]
    )
    back_hidden = (
        jnp.zeros((hidden_one.shape[0], back_mean.shape[1]), jnp.float32)
        .at[outer_slots.reshape(-1)]
        .add(spread)
    )
    back_hidden = back_hidden.at[:seed_count].add(back_seed)
    back_pre = (back_hidden * silu_slope(pre_one)).astype(jnp.bfloat16)
    grad_self_one = contract_rows(own_rows, back_pre)
    grad_neigh_one = contract_rows(inner_mean, back_pre)
    return (logits, (grad_self_one, grad_neigh_one, grad_self_two, grad_neigh_two))


def body(
    features,
    self_one,
    neigh_one,
    self_two,
    neigh_two,
    bucket_counts,
    request_rows,
    layer_targets,
    inner_slots,
    outer_slots,
    outer_degree,
    cotangent,
):
    batch_count = request_rows.shape[0]
    feature_width = features.shape[1]

    def serve(asked):
        return lax.all_to_all(features[asked], "store", split_axis=0, concat_axis=0, tiled=True)

    def fetch(request):
        return serve(lax.all_to_all(request, "store", split_axis=0, concat_axis=0, tiled=True))

    fetched_all = [
        fetch(request_rows[batch, 0]).reshape(-1, feature_width) for batch in range(batch_count)
    ]
    logit_list = []
    summed = None
    for batch in range(batch_count):
        logits, grads = sage_pass(
            fetched_all[batch],
            bucket_counts[batch, 0],
            layer_targets[batch],
            inner_slots[batch],
            outer_slots[batch],
            outer_degree[batch],
            cotangent[batch],
            self_one,
            neigh_one,
            self_two,
            neigh_two,
        )
        logit_list.append(logits)
        summed = grads if batch == 0 else jax.tree.map(jnp.add, summed, grads)
    totals = lax.psum((summed[0], summed[1], summed[2], summed[3]), ("store", "trainer"))
    return (jnp.stack(logit_list), totals[0], totals[1], totals[2], totals[3])


def solution(mesh):
    in_specs = (
        P("store", None),
        P(),
        P(),
        P(),
        P(),
        P(None, ("store", "trainer"), None),
        P(None, ("store", "trainer"), None, None),
        P(None, ("store", "trainer")),
        P(None, ("store", "trainer"), None),
        P(None, ("store", "trainer"), None),
        P(None, ("store", "trainer")),
        P(None, ("store", "trainer"), None),
    )
    out_specs = (P(None, ("store", "trainer"), None), P(), P(), P(), P())
    return jax.shard_map(body, mesh=mesh, in_specs=in_specs, out_specs=out_specs, check_vma=False)
```

profile of v0, /device:TPU:1, one launch (start us, length us, event | category | flops | bytes accessed | tf_op | source)
XLA Modules:
  0.0 587.0 jit_solution(14409965133146304169)
XLA Ops:
  7.2 1.4 fusion.49
  9.2 8.6 %all-to-all-start = ((s32[32,1,16]{2,1,0:T(1,128)}), s32[32,1,16]{2,1,0:T(1,128)}, u32[]{:S(2)}, u32[]{:S(2)}) async-start(s32[32,1,16]{2,1,0:T(1,128)} %bitcast), calls=%async_computation | async-start | bytes 32768 | tf_op jit(solution)/shard_map/all_to_all | solution.py:108
  19.4 1.1 fusion.33
  20.5 1.1 fusion.27
  24.1 0.9 compare_select_fusion.1
  25.3 32.2 %gather_fusion.2 = f32[5120]{0:T(1024)S(1)} fusion(f32[512]{0:T(512)S(1)} %reshape.529, s32[5120]{0:T(1024)S(1)} %broadcast_clamp_fusion.1), kind=kCustom, calls=%fused_computation.2 | custom fusion | bytes 61440 | tf_op jit(solution)/shard_map/gather | solution.py:49
  57.9 0.9 broadcast_divide_fusion.1
  59.3 1.6 mul.99
  60.9 2.8 mul.100
  64.4 1.6 mul.106
  66.0 2.8 mul.107
  68.8 9.3 %scatter_custom_fusion = f32[512,512]{1,0:T(8,128)S(1)} fusion(s32[960]{0:T(1024)S(1)} %bitcast.105, f32[960,512]{1,0:T(8,128)} %mul.100, f32[960]{0:T(1024)S(1)} %div.75, f32[]{:T(128)} %constant.68.clone.1), kind=kCustom, calls=%fused_computation.18 | custom fusion | flops 983040 | bytes 3018756 | tf_op jit(solution)/shard_map/scatter-add | solution.py:78
  78.3 9.7 %scatter_custom_fusion.1 = f32[512,512]{1,0:T(8,128)S(1)} fusion(s32[960]{0:T(1024)S(1)} %bitcast.106, f32[960,512]{1,0:T(8,128)} %mul.107, f32[960]{0:T(1024)S(1)} %div.76, f32[]{:T(128)} %constant.68.clone.1), kind=kCustom, calls=%fused_computation.16 | custom fusion | flops 983040 | bytes 3018756 | tf_op jit(solution)/shard_map/scatter-add | solution.py:78
  90.6 32.2 %gather_fusion.7 = f32[5120]{0:T(1024)S(1)} fusion(f32[512]{0:T(512)S(1)} %reshape.530, s32[5120]{0:T(1024)S(1)} %broadcast_clamp_fusion), kind=kCustom, calls=%fused_computation.7 | custom fusion | bytes 61440 | tf_op jit(solution)/shard_map/gather | solution.py:49
  123.9 7.4 %all-to-all-start.2 = ((s32[32,1,16]{2,1,0:T(1,128)}), s32[32,1,16]{2,1,0:T(1,128)S(1)}, u32[]{:S(2)}, u32[]{:S(2)}) async-start(s32[32,1,16]{2,1,0:T(1,128)} %bitcast.11), calls=%async_computation.2 | async-start | bytes 32768 | tf_op jit(solution)/shard_map/all_to_all | solution.py:108
  132.1 6.7 %gather_fusion = bf16[512,768]{1,0:T(8,128)(2,1)} fusion(bf16[4096,768]{1,0:T(8,128)(2,1)} %param.16, s32[1024]{0:T(1024)S(1)} %pad_clamp_fusion.5), kind=kCustom, calls=%fused_computation | custom fusion | bytes 1574912 | tf_op jit(solution)/shard_map/gather | solution.py:105
  138.8 7.4 %all-to-all-start.1 = ((bf16[32,16,768]{2,1,0:T(8,128)(2,1)}), bf16[32,16,768]{2,1,0:T(8,128)(2,1)S(1)}, u32[]{:S(2)}, u32[]{:S(2)}) async-start(bf16[32,16,768]{2,1,0:T(8,128)(2,1)} %bitcast.2), calls=%async_computation.1 | async-start | bytes 1572864 | tf_op jit(solution)/shard_map/all_to_all | solution.py:105
  147.1 6.7 %gather_fusion.5 = bf16[512,768]{1,0:T(8,128)(2,1)} fusion(bf16[4096,768]{1,0:T(8,128)(2,1)} %param.16, s32[1024]{0:T(1024)S(1)} %pad_clamp_fusion.2), kind=kCustom, calls=%fused_computation.5 | custom fusion | bytes 1574912 | tf_op jit(solution)/shard_map/gather | solution.py:105
  153.8 6.6 %all-to-all-done.1 = bf16[32,16,768]{2,1,0:T(8,128)(2,1)S(1)} async-done(((bf16[32,16,768]{2,1,0:T(8,128)(2,1)}), bf16[32,16,768]{2,1,0:T(8,128)(2,1)S(1)}, u32[]{:S(2)}, u32[]{:S(2)}) %all-to-all-start.1) | async-done | bytes 786464 | tf_op jit(solution)/shard_map/all_to_all | solution.py:105
  160.4 4.1 all-to-all-start.3
  164.6 22.0 %gather_fusion.3 = bf16[5120,768]{1,0:T(8,128)(2,1)} fusion(bf16[512,768]{1,0:T(8,128)(2,1)S(1)} %bitcast.100, s32[5120]{0:T(1024)S(1)} %broadcast_clamp_fusion.1), kind=kCustom, calls=%fused_computation.3 | custom fusion | bytes 15749120 | tf_op jit(solution)/shard_map/gather | solution.py:25
  186.6 16.0 %reshape.635 = f32[512,10,768]{2,1,0:T(8,128)} reshape(bf16[5120,768]{1,0:T(8,128)(2,1)} %gather_fusion.3) | data formatting | bytes 23592960 | tf_op jit(solution)/shard_map/convert_element_type | solution.py:25
  202.6 2.0 gather_fusion.1
  204.6 12.6 %multiply_reduce_fusion.1 = bf16[512,768]{1,0:T(8,128)(2,1)S(1)} fusion(f32[512,10,768]{2,1,0:T(8,128)} %reshape.635, f32[512,10]{1,0:T(8,128)S(1)} %copy-done.19), kind=kLoop, calls=%fused_computation.13 | loop fusion | flops 7471104 | bytes 16535552 | tf_op jit(solution)/shard_map/reduce_sum | solution.py:26
  218.4 0.9 multiply_convert_fusion.1
  219.3 1.7 fusion.54
  221.1 1.7 fusion.53
  222.8 22.0 %gather_fusion.8 = bf16[5120,768]{1,0:T(8,128)(2,1)} fusion(bf16[512,768]{1,0:T(8,128)(2,1)S(1)} %bitcast.98, s32[5120]{0:T(1024)S(1)} %broadcast_clamp_fusion), kind=kCustom, calls=%fused_computation.8 | custom fusion | bytes 15749120 | tf_op jit(solution)/shard_map/gather | solution.py:25
  244.9 16.0 %reshape.637 = f32[512,10,768]{2,1,0:T(8,128)} reshape(bf16[5120,768]{1,0:T(8,128)(2,1)} %gather_fusion.8) | data formatting | bytes 23592960 | tf_op jit(solution)/shard_map/convert_element_type | solution.py:25
  260.8 2.0 gather_fusion.6
  262.9 3.0 fusion.52
  265.9 1.0 fusion.20
  266.9 5.1 gather_fusion.4
  272.0 1.4 reshape.636
  274.5 1.0 fusion.29
  275.5 12.6 %multiply_reduce_fusion = bf16[512,768]{1,0:T(8,128)(2,1)S(1)} fusion(f32[512,10,768]{2,1,0:T(8,128)} %reshape.637, f32[512,10]{1,0:T(8,128)S(1)} %copy-done.20), kind=kLoop, calls=%fused_computation.12 | loop fusion | flops 7471104 | bytes 16535552 | tf_op jit(solution)/shard_map/reduce_sum | solution.py:26
  288.2 1.7 multiply_convert_fusion
  289.9 5.0 gather_fusion.9
  294.9 2.7 reshape.638
  297.6 2.2 multiply_reduce_fusion.2
  299.9 1.7 convolution_add_fusion
  301.7 1.7 convolution_add_fusion.1
  303.5 1.0 convolution_add_fusion.5
  304.4 1.0 convolution_add_fusion.4
  305.4 0.9 copy-done.9
  307.7 267.0 %all-reduce.3.cloned.1.call-done = (f32[768,512]{1,0:T(8,128)}, f32[768,512]{1,0:T(8,128)}, f32[512,153]{0,1:T(8,128)}, f32[512,153]{0,1:T(8,128)}) async-done(((f32[768,512]{1,0:T(8,128)}, f32[768,512]{1,0:T(8,128)}, f32[512,153]{0,1:T(8,128)}, f32[512,153]{0,1:T(8,128)}), (f32[768,512]{1,0:T(8,128)}, f32[768,512]{1,0:T(8,128)}, f32[512,153]{0,1:T(8,128)}, ...) | async-done | bytes 3772432 | tf_op jit(solution)/shard_map/psum | solution.py:131
  574.7 2.8 copy.41
  577.5 1.1 copy.42
  (134 shorter events, 17.4 us)
Async XLA Ops:
  7.2 210.6 %copy-start = (bf16[768,512]{1,0:T(8,128)(2,1)S(1)}, bf16[768,512]{1,0:T(8,128)(2,1)}, u32[]{:S(2)}) copy-start(bf16[768,512]{1,0:T(8,128)(2,1)} %param.18) | copy-start | bytes 2359300
  9.2 114.7 %all-to-all-start = ((s32[32,1,16]{2,1,0:T(1,128)}), s32[32,1,16]{2,1,0:T(1,128)}, u32[]{:S(2)}, u32[]{:S(2)}) async-start(s32[32,1,16]{2,1,0:T(1,128)} %bitcast), calls=%async_computation | async-start | bytes 32768 | tf_op jit(solution)/shard_map/all_to_all | solution.py:108
  58.9 4.8 copy-start.31
  58.9 5.1 copy-start.30
  60.9 2.8 copy-start.35
  68.8 9.3 %copy-start.8 = (bf16[512,153]{0,1:T(8,128)(2,1)S(1)}, bf16[512,153]{0,1:T(8,128)(2,1)}, u32[]{:S(2)}) copy-start(bf16[512,153]{0,1:T(8,128)(2,1)} %param.19) | copy-start | bytes 470020
  68.8 9.3 %copy-start.21 = (bf16[2,64,153]{2,1,0:T(8,128)(2,1)S(1)}, bf16[2,64,153]{2,1,0:T(8,128)(2,1)}, u32[]{:S(2)}) copy-start(bf16[2,64,153]{2,1,0:T(8,128)(2,1)} %param.27) | copy-start | bytes 117508
  78.3 12.3 %copy-start.13 = (f32[512,512]{1,0:T(8,128)}, f32[512,512]{1,0:T(8,128)S(1)}, u32[]{:S(2)}) copy-start(f32[512,512]{1,0:T(8,128)S(1)} %fusion.5) | copy-start | bytes 3145732
  88.2 34.6 %copy-start.15 = (f32[512,512]{1,0:T(8,128)}, f32[512,512]{1,0:T(8,128)S(1)}, u32[]{:S(2)}) copy-start(f32[512,512]{1,0:T(8,128)S(1)} %fusion.4) | copy-start | bytes 3145732
  90.6 32.6 %copy-start.33 = (s32[1,1,32,16]{2,3,1,0:T(8,128)S(1)}, s32[1,1,32,16]{2,3,1,0:T(8,128)}, u32[]{:S(2)}) copy-start(s32[1,1,32,16]{2,3,1,0:T(8,128)} %get-tuple-element.40) | copy-start | bytes 6148
  123.9 14.9 %all-to-all-start.2 = ((s32[32,1,16]{2,1,0:T(1,128)}), s32[32,1,16]{2,1,0:T(1,128)S(1)}, u32[]{:S(2)}, u32[]{:S(2)}) async-start(s32[32,1,16]{2,1,0:T(1,128)} %bitcast.11), calls=%async_computation.2 | async-start | bytes 32768 | tf_op jit(solution)/shard_map/all_to_all | solution.py:108
  138.8 21.6 %all-to-all-start.1 = ((bf16[32,16,768]{2,1,0:T(8,128)(2,1)}), bf16[32,16,768]{2,1,0:T(8,128)(2,1)S(1)}, u32[]{:S(2)}, u32[]{:S(2)}) async-start(bf16[32,16,768]{2,1,0:T(8,128)(2,1)} %bitcast.2), calls=%async_computation.1 | async-start | bytes 1572864 | tf_op jit(solution)/shard_map/all_to_all | solution.py:105
  160.4 62.4 %all-to-all-start.3 = ((bf16[32,16,768]{2,1,0:T(8,128)(2,1)}), bf16[32,16,768]{2,1,0:T(8,128)(2,1)S(1)}, u32[]{:S(2)}, u32[]{:S(2)}) async-start(bf16[32,16,768]{2,1,0:T(8,128)(2,1)} %bitcast.13), calls=%async_computation.3 | async-start | bytes 1572864 | tf_op jit(solution)/shard_map/all_to_all | solution.py:105
  164.5 410.2 %all-reduce.3.cloned.1.call-start = ((), (), s32[]{:S(2)}) async-start(), calls=%async_computation.4 | async-start | bytes 7602176 | tf_op jit(solution)/shard_map/psum | solution.py:131
  202.6 2.0 copy-start.19
  204.6 12.6 %copy-start.7 = (bf16[768,512]{1,0:T(8,128)(2,1)S(1)}, bf16[768,512]{1,0:T(8,128)(2,1)}, u32[]{:S(2)}) copy-start(bf16[768,512]{1,0:T(8,128)(2,1)} %param.17) | copy-start | bytes 2359300
  217.2 1.2 copy-start.14
  244.9 16.0 %copy-start.34 = (s32[1024]{0:T(1024)S(1)}, s32[1024]{0:T(1024)}, u32[]{:S(2)}) copy-start(s32[1024]{0:T(1024)} %pad_clamp_fusion.1) | copy-start | bytes 12292
  262.9 4.0 copy-start.1
  262.9 3.1 copy-start.22
  262.9 4.0 copy-start.27
  272.0 1.4 copy-start.32
  273.4 2.1 copy-start.20
  273.9 0.6 copy-start.24
  275.5 12.6 %copy-start.16 = (f32[512,512]{1,0:T(8,128)S(1)}, f32[512,512]{1,0:T(8,128)}, u32[]{:S(2)}) copy-start(f32[512,512]{1,0:T(8,128)} %copy-done.15) | copy-start | bytes 3145732
  275.5 12.6 %copy-start.23 = (f32[512,512]{1,0:T(8,128)S(1)}, f32[512,512]{1,0:T(8,128)}, u32[]{:S(2)}) copy-start(f32[512,512]{1,0:T(8,128)} %fusion.52) | copy-start | bytes 3145732
  288.1 1.7 copy-start.5
  288.1 1.7 copy-start.26
  294.9 4.9 copy-start.4
  297.6 2.2 copy-start.6
  297.6 2.2 copy-start.11
  299.9 1.8 copy-start.2
  299.9 1.8 copy-start.3
  301.7 1.7 copy-start.17
  301.7 2.7 copy-start.18
  305.4 0.9 copy-start.9
  305.4 1.1 copy-start.10
  305.4 1.1 copy-start.25
  574.7 2.8 copy-start.12
  577.5 1.2 copy-start.29
  577.5 1.9 copy-start.28
Sparse Core Ops, SparseCore 0:
  305.6 269.1 all-reduce.2
where the time goes:
time: 590 us; the launch traced here: 587 us
  waiting for transfers between devices  274 us (46%)
  local copies, waits for them, and re-layouts  196 us (33%)
  other arithmetic  54.8 us (9%)
  starting transfers between devices  27.6 us (5%)
  matrix products  20.2 us (3%)
  between operations  14.6 us (2%)
    psum x1, waiting for transfers between devices, body(): lax.psum((summed[0], summed[1], summed[2], summed[3]), ('store', 'trainer'))  267 us
    gather x4, local copies, waits for them, and re-layouts, sage_pass(): present = live_slots[inner_slots]  64.9 us
    gather x4, local copies, waits for them, and re-layouts, mean_rows(): picked = table[slots].astype(jnp.float32)  54.2 us
    convert_element_type x4, local copies, waits for them, and re-layouts, mean_rows(): picked = table[slots].astype(jnp.float32)  36 us
    reduce_sum x4, other arithmetic, mean_rows(): return jnp.sum(weights[:, :, None] * picked, axis=1)  27.9 us
    scatter-add x2, other arithmetic, sage_pass(): back_hidden = jnp.zeros((hidden_one.shape[0], back_mean.shape[1]), jnp.fl...  19 us
    all_to_all x2, starting transfers between devices, fetch(): lax.all_to_all(request, 'store', split_axis=0, concat_axis=0, tiled=True)  16 us
    gather x2, local copies, waits for them, and re-layouts, serve(): features[asked]  13.4 us
  transfers between devices with their start and end apart: 5, of which 2 were waited for; matrix products, arithmetic and copies ran while one was open for 31% of the time, Pallas kernels for 0%

commit v1 on v0

v1 whole, which is shorter than its diff:
```python
import functools

import jax
import jax.numpy as jnp
from jax import lax
from jax.experimental import pallas as pl
from jax.experimental.pallas import tpu as pltpu
from jax.sharding import Mesh, PartitionSpec as P

BF = jnp.bfloat16
F32 = jnp.float32
VMEM = pl.BlockSpec(memory_space=pltpu.VMEM)
SMEM = pl.BlockSpec(memory_space=pltpu.SMEM)
PARAMS = pltpu.CompilerParams(vmem_limit_bytes=56 * 1024 * 1024)


def nn(left, right):
    return lax.dot_general(left, right, (((1,), (0,)), ((), ())), preferred_element_type=F32)


def nt(left, right):
    return lax.dot_general(left, right, (((1,), (1,)), ((), ())), preferred_element_type=F32)


def tn(left, right):
    return lax.dot_general(left, right, (((0,), (0,)), ((), ())), preferred_element_type=F32)


def struct(shape, dtype):
    return jax.ShapeDtypeStruct(shape, dtype)


def cost(flops, size):
    return pl.CostEstimate(flops=flops, bytes_accessed=size, transcendentals=0)


def plan_kernel(
    counts_ref, targets_ref, inner_ref, outer_ref, degree_ref, cot_ref,
    self_one_ref, neigh_one_ref, self_two_ref, neigh_two_ref,
    own_ref, sum_ref, scale_ref, outer_sel_ref, outer_scale_ref, back_ref, self_t_ref, neigh_t_ref,
):
    batches, owners = counts_ref.shape
    slots, nodes = own_ref.shape[1:]
    fan_in = inner_ref.shape[1]
    fan_out, seeds = outer_ref.shape[1:]
    capacity = slots // owners
    block = 128
    self_t_ref[...] = self_one_ref[...].T
    neigh_t_ref[...] = neigh_one_ref[...].T
    for b in range(batches):
        degree = jnp.zeros((1, nodes), F32)
        for start in range(0, slots, block):
            slot = lax.broadcasted_iota(jnp.int32, (block, nodes), 0) + start
            own = jnp.where(slot == targets_ref[b : b + 1, :], 1.0, 0.0)
            own_ref[b, start : start + block, :] = own.astype(BF)
            total = jnp.zeros((block, nodes), F32)
            for k in range(fan_in):
                total += jnp.where(slot == inner_ref[b, k : k + 1, :], 1.0, 0.0)
            slot_col = lax.broadcasted_iota(jnp.int32, (block, owners), 0) + start
            owner_row = lax.broadcasted_iota(jnp.int32, (block, owners), 1)
            held = jnp.where(
                slot_col // capacity == owner_row, counts_ref[b : b + 1, :].astype(F32), 0.0
            )
            held = jnp.sum(held, axis=1, keepdims=True)
            place = lax.broadcasted_iota(jnp.int32, (block, 1), 0) % capacity
            total = jnp.where(place.astype(F32) < held, total, 0.0)
            degree += jnp.sum(total, axis=0, keepdims=True)
            sum_ref[b, start : start + block, :] = total.astype(BF)
        scale_ref[b, :, :] = 1.0 / jnp.maximum(degree, 1.0)

        seed_degree = degree_ref[b : b + 1, :]
        node = lax.broadcasted_iota(jnp.int32, (nodes, seeds), 0)
        chosen = jnp.zeros((nodes, seeds), F32)
        for k in range(fan_out):
            here = (node == outer_ref[b, k : k + 1, :]) & (seed_degree > k)
            chosen += jnp.where(here, 1.0, 0.0)
        outer_sel = chosen.astype(BF)
        outer_sel_ref[b, :, :] = outer_sel
        outer_scale = 1.0 / jnp.maximum(seed_degree.astype(F32), 1.0)
        outer_scale_ref[b, :, :] = outer_scale
        back_seed = nt(self_two_ref[...], cot_ref[b])
        back_mean = nt(neigh_two_ref[...], cot_ref[b]) * outer_scale
        high = back_mean.astype(BF)
        low = (back_mean - high.astype(F32)).astype(BF)
        back_ref[b, :, :] = nt(high, outer_sel) + nt(low, outer_sel)
        back_ref[b, :, 0:seeds] = back_ref[b, :, 0:seeds] + back_seed


def plan(counts, targets, inner, outer, degree, cot, self_one, neigh_one, self_two, neigh_two):
    batches, owners = counts.shape
    nodes = targets.shape[1]
    seeds = outer.shape[2]
    width, hidden = self_one.shape
    slots = nodes
    return pl.pallas_call(
        plan_kernel,
        out_shape=(
            struct((batches, slots, nodes), BF),
            struct((batches, slots, nodes), BF),
            struct((batches, 1, nodes), F32),
            struct((batches, nodes, seeds), BF),
            struct((batches, 1, seeds), F32),
            struct((batches, hidden, nodes), F32),
            struct((hidden, width), BF),
            struct((hidden, width), BF),
        ),
        in_specs=[VMEM] * 10,
        out_specs=[VMEM] * 8,
        compiler_params=PARAMS,
        cost_estimate=cost(200_000_000, 10_000_000),
        name="plan",
    )(counts, targets, inner, outer, degree, cot, self_one, neigh_one, self_two, neigh_two)


def serve_kernel(asked_ref, rows_ref, out_ref, wide, hot, total):
    step = pl.program_id(0)
    count = out_ref.shape[0]
    depth = rows_ref.shape[0]

    @pl.when(step == 0)
    def _():
        for start in range(0, count, 128):
            line = jnp.broadcast_to(asked_ref[:, start : start + 128], (128, 128))
            wide[start : start + 128, :] = line.T

    for start in range(0, depth, 128):
        place = lax.broadcasted_iota(jnp.int32, (count, 128), 1) + (step * depth + start)
        hot[:, start : start + 128] = jnp.where(wide[...] == place, 1.0, 0.0).astype(BF)
    part = nn(hot[...], rows_ref[...])

    @pl.when(step == 0)
    def _():
        total[...] = part

    @pl.when(step > 0)
    def _():
        total[...] += part

    @pl.when(step == pl.num_programs(0) - 1)
    def _():
        out_ref[...] = total[...].astype(BF)


def serve(asked, features):
    count = asked.shape[1]
    rows, width = features.shape
    depth = 1024
    return pl.pallas_call(
        serve_kernel,
        out_shape=struct((count, width), BF),
        grid=(rows // depth,),
        in_specs=[
            pl.BlockSpec((1, count), lambda i: (0, 0)),
            pl.BlockSpec((depth, width), lambda i: (i, 0)),
        ],
        out_specs=pl.BlockSpec((count, width), lambda i: (0, 0)),
        scratch_shapes=[
            pltpu.VMEM((count, 128), jnp.int32),
            pltpu.VMEM((count, depth), BF),
            pltpu.VMEM((count, width), F32),
        ],
        compiler_params=PARAMS,
        cost_estimate=cost(2 * count * rows * width, 10_000_000),
        name="serve",
    )(asked, features)


def pass_kernel(
    core_ref, fetched_ref, own_sel_ref, sum_sel_ref, scale_ref, outer_sel_ref, outer_scale_ref,
    back_ref, cot_ref, self_t_ref, neigh_t_ref, self_two_ref, neigh_two_ref,
    logits_ref, keep_ref, send_ref, own_t, mean_t, first, second, back_t,
):
    batches = fetched_ref.shape[1]
    slots = own_sel_ref.shape[1]
    width = self_t_ref.shape[1]
    hidden = self_t_ref.shape[0]
    seeds, classes = logits_ref.shape[1:]
    second[...] = jnp.zeros_like(second)
    for b in range(batches):
        table = fetched_ref[:, b].reshape(slots, width).T
        own_t[...] = nn(table, own_sel_ref[b]).astype(BF)
        mean_t[...] = (nn(table, sum_sel_ref[b]) * scale_ref[b]).astype(BF)
        pre = nn(self_t_ref[...], own_t[...]) + nn(neigh_t_ref[...], mean_t[...])
        gate = 1.0 / (1.0 + jnp.exp(-pre))
        hidden_t = (pre * gate).astype(BF)
        back_t[...] = (back_ref[b] * (gate * (1.0 + pre * (1.0 - gate)))).astype(BF)
        outer_t = (nn(hidden_t, outer_sel_ref[b]) * outer_scale_ref[b]).astype(BF)
        seed_t = hidden_t[:, 0:seeds]
        logits_ref[b, :, :] = tn(seed_t, self_two_ref[...]) + tn(outer_t, neigh_two_ref[...])
        self_grad = nn(seed_t, cot_ref[b])
        neigh_grad = nn(outer_t, cot_ref[b])
        half = hidden // 2
        for h in range(2):
            second[h, :, 0:classes] += self_grad[h * half : (h + 1) * half, :]
            second[h, :, half : half + classes] += neigh_grad[h * half : (h + 1) * half, :]
        if b == 0:
            first[0] = nt(own_t[...], back_t[...])
            first[1] = nt(mean_t[...], back_t[...])
        else:
            first[0] += nt(own_t[...], back_t[...])
            first[1] += nt(mean_t[...], back_t[...])
    core = core_ref[0]
    keep_ref[0:width, :] = first[core]
    keep_ref[width:, :] = second[core]
    send_ref[0:width, :] = first[1 - core].astype(BF)
    send_ref[width:, :] = second[1 - core].astype(BF)


def both_passes(core, fetched, planned, cot, self_two, neigh_two, logit_shape):
    own_sel, sum_sel, scale, outer_sel, outer_scale, back, self_t, neigh_t = planned
    batches = fetched.shape[1]
    hidden, width = self_t.shape
    nodes = own_sel.shape[2]
    half_rows = width + hidden // 2
    return pl.pallas_call(
        pass_kernel,
        out_shape=(
            struct(logit_shape, F32),
            struct((half_rows, hidden), F32),
            struct((half_rows, hidden), BF),
        ),
        in_specs=[SMEM] + [VMEM] * 12,
        out_specs=[VMEM] * 3,
        scratch_shapes=[
            pltpu.VMEM((width, nodes), BF),
            pltpu.VMEM((width, nodes), BF),
            pltpu.VMEM((2, width, hidden), F32),
            pltpu.VMEM((2, hidden // 2, hidden), F32),
            pltpu.VMEM((hidden, nodes), BF),
        ],
        compiler_params=PARAMS,
        cost_estimate=cost(6_000_000_000, 20_000_000),
        name="both_passes",
    )(
        core, fetched, own_sel, sum_sel, scale, outer_sel, outer_scale, back, cot,
        self_t, neigh_t, self_two, neigh_two,
    )


def add_kernel(keep_ref, got_ref, out_ref):
    out_ref[...] = (keep_ref[...] + got_ref[...].astype(F32)).astype(BF)


def add_pair(keep, got):
    return pl.pallas_call(
        add_kernel,
        out_shape=struct(keep.shape, BF),
        in_specs=[VMEM] * 2,
        out_specs=VMEM,
        compiler_params=PARAMS,
        cost_estimate=cost(keep.size, keep.size * 8),
        name="add_pair",
    )(keep, got)


def sum_kernel(parts_ref, out_ref):
    total = parts_ref[0].astype(F32)
    for i in range(1, parts_ref.shape[0]):
        total += parts_ref[i].astype(F32)
    total = total.astype(BF)
    for i in range(out_ref.shape[0]):
        out_ref[i] = total


def sum_parts(parts, copies):
    return pl.pallas_call(
        sum_kernel,
        out_shape=struct((copies,) + parts.shape[1:], BF),
        in_specs=[VMEM],
        out_specs=VMEM,
        compiler_params=PARAMS,
        cost_estimate=cost(parts.size, parts.size * 4),
        name="sum_parts",
    )(parts)


def unpack_kernel(core_ref, mine_ref, other_ref, self_one_ref, neigh_one_ref, self_two_ref, neigh_two_ref):
    width = self_one_ref.shape[0]
    half = mine_ref.shape[0] - width
    classes = self_two_ref.shape[1]

    def place(ref, one_ref, h):
        one_ref[...] = ref[0:width, :].astype(F32)
        tail = ref[width:, :].astype(F32)
        self_two_ref[h * half : (h + 1) * half, :] = tail[:, 0:classes]
        neigh_two_ref[h * half : (h + 1) * half, :] = tail[:, half : half + classes]

    @pl.when(core_ref[0] == 0)
    def _():
        place(mine_ref, self_one_ref, 0)
        place(other_ref, neigh_one_ref, 1)

    @pl.when(core_ref[0] != 0)
    def _():
        place(mine_ref, neigh_one_ref, 1)
        place(other_ref, self_one_ref, 0)


def unpack(core, mine, other, one_shape, two_shape):
    return pl.pallas_call(
        unpack_kernel,
        out_shape=(
            struct(one_shape, F32),
            struct(one_shape, F32),
            struct(two_shape, F32),
            struct(two_shape, F32),
        ),
        in_specs=[SMEM, VMEM, VMEM],
        out_specs=[VMEM] * 4,
        compiler_params=PARAMS,
        cost_estimate=cost(mine.size, mine.size * 12),
        name="unpack",
    )(core, mine, other)


def exchange(value, axes):
    return lax.all_to_all(value, axes, split_axis=0, concat_axis=0, tiled=True)


def swap_cores(value):
    return lax.ppermute(value, "core", [(0, 1), (1, 0)])


def body(
    chips, trainers,
    features, self_one, neigh_one, self_two, neigh_two, bucket_counts, request_rows,
    layer_targets, inner_slots, outer_slots, outer_degree, cotangent,
):
    batches, _, owners, capacity = request_rows.shape
    width, hidden = self_one.shape
    core = lax.axis_index("core").reshape(1).astype(jnp.int32)
    wanted = request_rows[:, 0].transpose(1, 0, 2).reshape(owners, batches * capacity)
    asked = exchange(wanted, ("chip", "core"))
    planned = plan(
        bucket_counts[:, 0],
        layer_targets,
        inner_slots.transpose(0, 2, 1),
        outer_slots.transpose(0, 2, 1),
        outer_degree,
        cotangent,
        self_one,
        neigh_one,
        self_two,
        neigh_two,
    )
    rows = serve(asked.reshape(1, -1), features)
    fetched = exchange(rows.reshape(owners, batches, capacity, width), ("chip", "core"))
    logits, keep, send = both_passes(
        core, fetched, planned, cotangent, self_two, neigh_two, cotangent.shape
    )
    half = add_pair(keep, swap_cores(send))
    piece = half.shape[0] // chips
    parts = exchange(half.reshape(chips, piece, hidden), "chip")
    parts = exchange(sum_parts(parts, trainers), "trainer")
    mine = exchange(sum_parts(parts, chips), "chip").reshape(chips * piece, hidden)
    grads = unpack(core, mine, swap_cores(mine), self_one.shape, self_two.shape)
    return (logits,) + tuple(grads)


def solution(mesh):
    stores, trainers = mesh.shape["store"], mesh.shape["trainer"]
    split = Mesh(
        mesh.devices.reshape(stores // 2, 2, trainers), ("chip", "core", "trainer")
    )
    store = ("chip", "core")
    every = ("chip", "core", "trainer")
    in_specs = (
        P(store, None),
        P(),
        P(),
        P(),
        P(),
        P(None, every, None),
        P(None, every, None, None),
        P(None, every),
        P(None, every, None),
        P(None, every, None),
        P(None, every),
        P(None, every, None),
    )
    out_specs = (P(None, every, None), P(), P(), P(), P())
    return jax.shard_map(
        functools.partial(body, stores // 2, trainers),
        mesh=split,
        in_specs=in_specs,
        out_specs=out_specs,
        check_vma=False,
    )
```

time: 590 us -> 161 us (0.27)
  waiting for transfers between devices: 274 us -> 15.9 us
  local copies, waits for them, and re-layouts: 196 us -> 11.9 us
  blocking collectives: 0 us -> 77.6 us
  other arithmetic: 54.8 us -> 0.69 us
  Pallas kernels: 0 us -> 42.4 us
  matrix products: 20.2 us -> 0 us
  starting transfers between devices: 27.6 us -> 10.8 us
  between operations: 14.6 us -> 0.69 us
    psum x1 -> x0, waiting for transfers between devices: 267 us -> none  [body(): lax.psum((summed[0], summed[1], summed[2], summed[3]), ('store', 'trainer'))]
    gather x12 -> x0, local copies, waits for them, and re-layouts: 136 us -> none  [the longest x4 64.9 us: sage_pass(): present = live_slots[inner_slots]]
    all_to_all x0 -> x4, blocking collectives: none -> 77.6 us  [exchange(): return lax.all_to_all(value, axes, split_axis=0, concat_axis=0, tiled=True)]
    pallas_call x0 -> x7, Pallas kernels: none -> 42.4 us  [the longest x1 11.8 us: both_passes(): pl.pallas_call(pass_kernel, out_shape=(struct(logit_shape, F32), struct((...]
    convert_element_type x6 -> x0, local copies, waits for them, and re-layouts: 36.2 us -> none  [the longest x4 36 us: mean_rows(): picked = table[slots].astype(jnp.float32)]
    reduce_sum x6 -> x0, other arithmetic: 28.2 us -> none  [the longest x4 27.9 us: mean_rows(): return jnp.sum(weights[:, :, None] * picked, axis=1)]
    all_to_all x4 -> x1, starting transfers between devices: 27.5 us -> 4.43 us  [exchange(): return lax.all_to_all(value, axes, split_axis=0, concat_axis=0, tiled=True)]
    dot_general x20 -> x0, matrix products: 20.2 us -> none  [the longest x8 10.8 us: contract_rows(): lax.dot_general(left, right, (((0,), (0,)), ((), ())), preferred_element_...]
  transfers between devices with their start and end apart: 5 -> 3, of which waited for: 2 -> 3; matrix products, arithmetic and copies ran while one was open for 31% -> 2% of each run, Pallas kernels for 0% -> 5%
where the time goes in v1:
time: 161 us; the launch traced here: 160 us
  blocking collectives  77.6 us (48%)
  Pallas kernels  42.4 us (26%)
  waiting for transfers between devices  15.9 us (10%)
  local copies, waits for them, and re-layouts  11.9 us (7%)
  starting transfers between devices  10.8 us (7%)
    all_to_all x4, blocking collectives, exchange(): return lax.all_to_all(value, axes, split_axis=0, concat_axis=0, tiled=True)  77.6 us
    pallas_call x1, Pallas kernels, both_passes(): pl.pallas_call(pass_kernel, out_shape=(struct(logit_shape, F32), struct((...  11.8 us
    pallas_call x1, Pallas kernels, serve(): pl.pallas_call(serve_kernel, out_shape=struct((count, width), BF), grid=(...  11.4 us
    all_to_all x1, waiting for transfers between devices, exchange(): return lax.all_to_all(value, axes, split_axis=0, concat_axis=0, tiled=True)  11.1 us
    unnamed x22, local copies, waits for them, and re-layouts  9.94 us
    pallas_call x1, Pallas kernels, plan(): pl.pallas_call(plan_kernel, out_shape=(struct((batches, slots, nodes), BF...  8.09 us
    ppermute x2, starting transfers between devices, swap_cores(): return lax.ppermute(value, 'core', [(0, 1), (1, 0)])  6.36 us
    ppermute x2, waiting for transfers between devices, swap_cores(): return lax.ppermute(value, 'core', [(0, 1), (1, 0)])  4.78 us
  transfers between devices with their start and end apart: 3, of which 3 were waited for; matrix products, arithmetic and copies ran while one was open for 2% of the time, Pallas kernels for 5%

profile of v1, /device:TPU:1, one launch (start us, length us, event | category | flops | bytes accessed | tf_op | source)
XLA Modules:
  0.0 159.9 jit_solution(3615605055880712148)
XLA Ops:
  0.6 0.8 copy.35
  1.4 15.3 %all_to_all.29 = s32[32,1,32]{2,1,0:T(1,128)S(1)} all-to-all(s32[32,1,32]{2,1,0:T(1,128)S(1)} %copy.35), channel_id=1, replica_groups=mesh['chip'=16,'core'=2,'trainer'=8] {'chip','core'}, dimensions={0} | all-to-all | bytes 8192 | tf_op jit(solution)/shard_map/all_to_all | solution.py:317
  16.7 0.5 broadcast.3
  17.3 0.7 reduce.3
  17.9 0.7 reshape.31.asked_ref
  18.6 11.4 %serve.1 = bf16[1024,768]{1,0:T(8,128)(2,1)} custom-call(s32[1,1024]{1,0:T(1,128)} %reshape.31.asked_ref, bf16[4096,768]{1,0:T(8,128)(2,1)} %rows_ref.1), custom_call_target="tpu_custom_call" | custom-call | flops 6442450944 | bytes 10000000 | tf_op jit(solution)/shard_map/serve/pallas_call | solution.py:148
  30.0 0.0 copy-start.7
  30.0 0.0 copy-start.6
  30.0 0.0 copy-start.4
  30.0 0.0 copy-start.5
  30.0 4.4 %all-to-all-start.1 = ((bf16[32,2,16,768]{3,2,1,0:T(8,128)(2,1)}), bf16[32,2,16,768]{3,2,1,0:T(8,128)(2,1)S(1)}, u32[]{:S(2)}, u32[]{:S(2)}) async-start(bf16[32,2,16,768]{3,2,1,0:T(8,128)(2,1)} %bitcast.19), calls=%async_computation.1 | async-start | bytes 3145728 | tf_op jit(solution)/shard_map/all_to_all | solution.py:317
  34.5 0.0 copy-done.7
  34.5 0.6 copy.47
  35.1 0.0 copy-done.6
  35.1 0.6 copy.46
  35.7 0.0 copy-done.4
  35.7 0.8 copy.38.self_two_ref
  36.6 0.0 copy-done.5
  36.6 0.8 copy.39.neigh_two_ref
  37.4 8.1 %plan.1 = (bf16[2,512,512]{2,1,0:T(8,128)(2,1)}, bf16[2,512,512]{2,1,0:T(8,128)(2,1)}, f32[2,1,512]{2,1,0:T(1,128)}, bf16[2,512,64]{2,1,0:T(8,128)(2,1)}, f32[2,...) custom-call(s32[2,32]{1,0:T(2,128)} %bitcast.23, ...), custom_call_target="tpu_custom_call" | custom-call | flops 200000000 | bytes 10000000 | tf_op jit(solution)/shard_map/plan/pallas_call | solution.py:95
  45.5 11.1 %all-to-all-done.1.fetched_ref = bf16[32,2,16,768]{3,2,1,0:T(8,128)(2,1)S(1)} async-done(((bf16[32,2,16,768]{3,2,1,0:T(8,128)(2,1)}), bf16[32,2,16,768]{3,2,1,0:T(8,128)(2,1)S(1)}, u32[]{:S(2)}, u32[]{:S(2)}) %all-to-all-start.1) | async-done | bytes 1572896 | tf_op jit(solution)/shard_map/all_to_all | solution.py:317
  56.6 0.0 copy-start.1
  56.6 1.1 copy-done.1
  57.8 11.8 %both_passes.1 = (f32[2,64,153]{2,1,0:T(8,128)}, f32[1024,512]{1,0:T(8,128)}, bf16[1024,512]{1,0:T(8,128)(2,1)}) custom-call(s32[1]{0:T(128)} %bitcast.core_ref, bf16[32,2,16,768]{3,2,1,0:T(8,128)(2,1)} %copy-done.1, bf16[2,512,512]{2,1,0:T(8,128)(2,1)} %get-tuple-element.20.own_sel_ref, bf16[2,512,512]{2,1,0:T(8,128)(2,1)} %get-tuple-element.21.sum_sel_ref, ...), custom_call_target="tpu_custom_call" | custom-call | flops 6000000000 | bytes 20000000 | tf_op jit(solution)/shard_map/both_passes/pallas_call | solution.py:215
  69.5 2.1 %collective-permute-start = (bf16[1024,512]{1,0:T(8,128)(2,1)}, bf16[1024,512]{1,0:T(8,128)(2,1)S(1)}, u32[]{:S(2)}, u32[]{:S(2)}) collective-permute-start(bf16[1024,512]{1,0:T(8,128)(2,1)} %get-tuple-element.30), channel_id=1, source_target_pairs={{0,8},{8,0},{1,9},{9,1},{2,10},{10,2},{3,11},{11,3},{4,12},{12,4},... | collective-permute-start | bytes 3145736 | tf_op jit(solution)/shard_map/ppermute | solution.py:321
  71.7 2.5 %collective-permute-done.got_ref = bf16[1024,512]{1,0:T(8,128)(2,1)S(1)} collective-permute-done((bf16[1024,512]{1,0:T(8,128)(2,1)}, bf16[1024,512]{1,0:T(8,128)(2,1)S(1)}, u32[]{:S(2)}, u32[]{:S(2)}) %collective-permute-start) | collective-permute-done | bytes 1048608 | tf_op jit(solution)/shard_map/ppermute | solution.py:321
  74.2 0.0 copy-start.3
  74.2 1.0 copy-done.3
  75.2 3.0 %add_pair.1 = bf16[1024,512]{1,0:T(8,128)(2,1)} custom-call(f32[1024,512]{1,0:T(8,128)} %get-tuple-element.29.keep_ref, bf16[1024,512]{1,0:T(8,128)(2,1)} %copy-done.3), custom_call_target="tpu_custom_call" | custom-call | flops 524288 | bytes 4194304 | tf_op jit(solution)/shard_map/add_pair/pallas_call | solution.py:245
  78.1 21.0 %all_to_all.30.parts_ref = bf16[16,64,512]{2,1,0:T(8,128)(2,1)} all-to-all(bf16[16,64,512]{2,1,0:T(8,128)(2,1)} %bitcast.18), channel_id=1, replica_groups=mesh['chip'=16,'core'=2,'trainer'=8] {'chip'}, dimensions={0} | all-to-all | bytes 2097152 | tf_op jit(solution)/shard_map/all_to_all | solution.py:317
  99.1 2.2 %sum_parts.2 = bf16[8,64,512]{2,1,0:T(8,128)(2,1)} custom-call(bf16[16,64,512]{2,1,0:T(8,128)(2,1)} %all_to_all.30.parts_ref), custom_call_target="tpu_custom_call" | custom-call | flops 524288 | bytes 2097152 | tf_op jit(solution)/shard_map/sum_parts/pallas_call | solution.py:266
  101.3 23.1 %all_to_all.31.parts_ref = bf16[8,64,512]{2,1,0:T(8,128)(2,1)} all-to-all(bf16[8,64,512]{2,1,0:T(8,128)(2,1)} %sum_parts.2), channel_id=1, replica_groups=mesh['chip'=16,'core'=2,'trainer'=8] {'trainer'}, dimensions={0} | all-to-all | bytes 1048576 | tf_op jit(solution)/shard_map/all_to_all | solution.py:317
  124.4 2.1 %sum_parts.3 = bf16[16,64,512]{2,1,0:T(8,128)(2,1)} custom-call(bf16[8,64,512]{2,1,0:T(8,128)(2,1)} %all_to_all.31.parts_ref), custom_call_target="tpu_custom_call" | custom-call | flops 262144 | bytes 1048576 | tf_op jit(solution)/shard_map/sum_parts/pallas_call | solution.py:266
  126.5 18.2 %all_to_all.32 = bf16[16,64,512]{2,1,0:T(8,128)(2,1)S(1)} all-to-all(bf16[16,64,512]{2,1,0:T(8,128)(2,1)} %sum_parts.3), channel_id=1, replica_groups=mesh['chip'=16,'core'=2,'trainer'=8] {'chip'}, dimensions={0} | all-to-all | bytes 2097152 | tf_op jit(solution)/shard_map/all_to_all | solution.py:317
  144.7 0.0 copy-start
  144.7 4.2 %collective-permute-start.1 = (bf16[1024,512]{1,0:T(8,128)(2,1)S(1)}, bf16[1024,512]{1,0:T(8,128)(2,1)S(1)}, u32[]{:S(2)}, u32[]{:S(2)}) collective-permute-start(bf16[1024,512]{1,0:T(8,128)(2,1)S(1)} %bitcast.16), channel_id=1, source_target_pairs={{0,8},{8,0},{1,9},{9,1},{2,10},{10,2},{3,11},{11,3},{4,12},{12,4},... | collective-permute-start | bytes 3145736 | tf_op jit(solution)/shard_map/ppermute | solution.py:321
  148.9 2.3 %collective-permute-done.1.other_ref = bf16[1024,512]{1,0:T(8,128)(2,1)S(1)} collective-permute-done((bf16[1024,512]{1,0:T(8,128)(2,1)S(1)}, bf16[1024,512]{1,0:T(8,128)(2,1)S(1)}, u32[]{:S(2)}, u32[]{:S(2)}) %collective-permute-start.1) | collective-permute-done | bytes 1048608 | tf_op jit(solution)/shard_map/ppermute | solution.py:321
  151.2 0.0 copy-done
  151.2 0.0 copy-start.2
  151.2 1.0 copy-done.2
  152.2 3.8 %unpack.1 = (f32[768,512]{1,0:T(8,128)}, f32[768,512]{1,0:T(8,128)}, f32[512,153]{1,0:T(8,128)}, f32[512,153]{1,0:T(8,128)}) custom-call(s32[1]{0:T(128)} %bitcast.core_ref, bf16[1024,512]{1,0:T(8,128)(2,1)} %bitcast.17, bf16[1024,512]{1,0:T(8,128)(2,1)} %copy-done.2), custom_call_target="tpu_custom_call" | custom-call | flops 524288 | bytes 6291456 | tf_op jit(solution)/shard_map/unpack/pallas_call | solution.py:300
  156.0 1.9 %copy.42 = f32[512,153]{0,1:T(8,128)} copy(f32[512,153]{1,0:T(8,128)} %get-tuple-element.48) | data formatting | bytes 626688
  158.0 1.9 %copy.43 = f32[512,153]{0,1:T(8,128)} copy(f32[512,153]{1,0:T(8,128)} %get-tuple-element.49) | data formatting | bytes 626688
Async XLA Ops:
  30.0 4.5 %copy-start.7 = (s32[2,64,15]{1,0,2:T(2,128)S(1)}, s32[2,64,15]{1,0,2:T(2,128)}, u32[]{:S(2)}) copy-start(s32[2,64,15]{1,0,2:T(2,128)} %param.21) | copy-start | bytes 23044
  30.0 5.1 %copy-start.6 = (s32[2,512,10]{1,0,2:T(2,128)S(1)}, s32[2,512,10]{1,0,2:T(2,128)}, u32[]{:S(2)}) copy-start(s32[2,512,10]{1,0,2:T(2,128)} %param.20) | copy-start | bytes 122884
  30.0 5.7 %copy-start.4 = (bf16[512,153]{0,1:T(8,128)(2,1)S(1)}, bf16[512,153]{0,1:T(8,128)(2,1)}, u32[]{:S(2)}) copy-start(bf16[512,153]{0,1:T(8,128)(2,1)} %param.15) | copy-start | bytes 470020
  30.0 6.5 %copy-start.5 = (bf16[512,153]{0,1:T(8,128)(2,1)S(1)}, bf16[512,153]{0,1:T(8,128)(2,1)}, u32[]{:S(2)}) copy-start(bf16[512,153]{0,1:T(8,128)(2,1)} %param.16) | copy-start | bytes 470020
  30.0 26.6 %all-to-all-start.1 = ((bf16[32,2,16,768]{3,2,1,0:T(8,128)(2,1)}), bf16[32,2,16,768]{3,2,1,0:T(8,128)(2,1)S(1)}, u32[]{:S(2)}, u32[]{:S(2)}) async-start(bf16[32,2,16,768]{3,2,1,0:T(8,128)(2,1)} %bitcast.19), calls=%async_computation.1 | async-start | bytes 3145728 | tf_op jit(solution)/shard_map/all_to_all | solution.py:317
  56.6 1.1 copy-start.1
  69.5 4.6 %collective-permute-start = (bf16[1024,512]{1,0:T(8,128)(2,1)}, bf16[1024,512]{1,0:T(8,128)(2,1)S(1)}, u32[]{:S(2)}, u32[]{:S(2)}) collective-permute-start(bf16[1024,512]{1,0:T(8,128)(2,1)} %get-tuple-element.30), channel_id=1, source_target_pairs={{0,8},{8,0},{1,9},{9,1},{2,10},{10,2},{3,11},{11,3},{4,12},{12,4},... | collective-permute-start | bytes 3145736 | tf_op jit(solution)/shard_map/ppermute | solution.py:321
  74.2 1.0 copy-start.3
  144.7 6.5 %copy-start = (bf16[16,64,512]{2,1,0:T(8,128)(2,1)}, bf16[16,64,512]{2,1,0:T(8,128)(2,1)S(1)}, u32[]{:S(2)}) copy-start(bf16[16,64,512]{2,1,0:T(8,128)(2,1)S(1)} %all_to_all.32) | copy-start | bytes 3145732
  144.7 6.5 %collective-permute-start.1 = (bf16[1024,512]{1,0:T(8,128)(2,1)S(1)}, bf16[1024,512]{1,0:T(8,128)(2,1)S(1)}, u32[]{:S(2)}, u32[]{:S(2)}) collective-permute-start(bf16[1024,512]{1,0:T(8,128)(2,1)S(1)} %bitcast.16), channel_id=1, source_target_pairs={{0,8},{8,0},{1,9},{9,1},{2,10},{10,2},{3,11},{11,3},{4,12},{12,4},... | collective-permute-start | bytes 3145736 | tf_op jit(solution)/shard_map/ppermute | solution.py:321
  151.2 1.0 copy-start.2

commit v2 on v1

v2 whole, which is shorter than its diff:
```python
import jax
import jax.numpy as jnp
from jax import lax
from jax.experimental import pallas as pl
from jax.experimental.pallas import tpu as pltpu
from jax.sharding import Mesh, PartitionSpec as P

BF = jnp.bfloat16
F32 = jnp.float32
VMEM = pl.BlockSpec(memory_space=pltpu.VMEM)
SMEM = pl.BlockSpec(memory_space=pltpu.SMEM)
LANES = 128
SUBLANES = 8


def nn(left, right):
    return lax.dot_general(left, right, (((1,), (0,)), ((), ())), preferred_element_type=F32)


def nt(left, right):
    return lax.dot_general(left, right, (((1,), (1,)), ((), ())), preferred_element_type=F32)


def tn(left, right):
    return lax.dot_general(left, right, (((0,), (0,)), ((), ())), preferred_element_type=F32)


def struct(shape, dtype):
    return jax.ShapeDtypeStruct(shape, dtype)


def params(mebibytes):
    return pltpu.CompilerParams(vmem_limit_bytes=mebibytes * 1024 * 1024)


def cost(flops, size):
    return pl.CostEstimate(flops=flops, bytes_accessed=size, transcendentals=0)


def plan_kernel(
    counts_ref, targets_ref, inner_ref, outer_ref, degree_ref, cot_ref,
    self_one_ref, neigh_one_ref, self_two_ref, neigh_two_ref,
    own_ref, sum_ref, scale_ref, outer_sel_ref, outer_scale_ref, back_ref, self_t_ref, neigh_t_ref,
    cot_t_ref,
):
    batches, owners = counts_ref.shape
    slots, nodes = own_ref.shape[1:]
    fan_in = inner_ref.shape[1]
    fan_out, seeds = outer_ref.shape[1:]
    capacity = slots // owners
    block = 128
    self_t_ref[...] = self_one_ref[...].T
    neigh_t_ref[...] = neigh_one_ref[...].T
    for b in range(batches):
        degree = jnp.zeros((1, nodes), F32)
        for start in range(0, slots, block):
            slot = lax.broadcasted_iota(jnp.int32, (block, nodes), 0) + start
            own = jnp.where(slot == targets_ref[b : b + 1, :], 1.0, 0.0)
            own_ref[b, start : start + block, :] = own.astype(BF)
            total = jnp.zeros((block, nodes), F32)
            for k in range(fan_in):
                total += jnp.where(slot == inner_ref[b, k : k + 1, :], 1.0, 0.0)
            slot_col = lax.broadcasted_iota(jnp.int32, (block, owners), 0) + start
            owner_row = lax.broadcasted_iota(jnp.int32, (block, owners), 1)
            held = jnp.where(
                slot_col // capacity == owner_row, counts_ref[b : b + 1, :].astype(F32), 0.0
            )
            held = jnp.sum(held, axis=1, keepdims=True)
            place = lax.broadcasted_iota(jnp.int32, (block, 1), 0) % capacity
            total = jnp.where(place.astype(F32) < held, total, 0.0)
            degree += jnp.sum(total, axis=0, keepdims=True)
            sum_ref[b, start : start + block, :] = total.astype(BF)
        scale_ref[b, :, :] = 1.0 / jnp.maximum(degree, 1.0)

        seed_degree = degree_ref[b : b + 1, :]
        node = lax.broadcasted_iota(jnp.int32, (nodes, seeds), 0)
        chosen = jnp.zeros((nodes, seeds), F32)
        for k in range(fan_out):
            here = (node == outer_ref[b, k : k + 1, :]) & (seed_degree > k)
            chosen += jnp.where(here, 1.0, 0.0)
        outer_sel = chosen.astype(BF)
        outer_sel_ref[b, :, :] = outer_sel
        outer_scale = 1.0 / jnp.maximum(seed_degree.astype(F32), 1.0)
        outer_scale_ref[b, :, :] = outer_scale
        cot_t = cot_ref[b].T
        cot_t_ref[b, :, :] = cot_t
        back_seed = tn(self_two_ref[...], cot_t)
        back_mean = tn(neigh_two_ref[...], cot_t) * outer_scale
        high = back_mean.astype(BF)
        low = (back_mean - high.astype(F32)).astype(BF)
        back_ref[b, :, :] = nt(high, outer_sel) + nt(low, outer_sel)
        back_ref[b, :, 0:seeds] = back_ref[b, :, 0:seeds] + back_seed


def plan(counts, targets, inner, outer, degree, cot, self_one, neigh_one, self_two, neigh_two):
    batches, owners = counts.shape
    nodes = targets.shape[1]
    seeds, classes = cot.shape[1:]
    width, hidden = self_one.shape
    slots = nodes
    return pl.pallas_call(
        plan_kernel,
        out_shape=(
            struct((batches, slots, nodes), BF),
            struct((batches, slots, nodes), BF),
            struct((batches, 1, nodes), F32),
            struct((batches, nodes, seeds), BF),
            struct((batches, 1, seeds), F32),
            struct((batches, hidden, nodes), F32),
            struct((hidden, width), BF),
            struct((hidden, width), BF),
            struct((batches, classes, seeds), BF),
        ),
        in_specs=[VMEM] * 10,
        out_specs=[VMEM] * 9,
        compiler_params=params(24),
        cost_estimate=cost(200_000_000, 10_000_000),
        name="plan",
    )(counts, targets, inner, outer, degree, cot, self_one, neigh_one, self_two, neigh_two)


def widen_kernel(rows_ref, out_ref):
    rows, width = rows_ref.shape
    for j in range(width // LANES):
        piece = rows_ref[:, j * LANES : (j + 1) * LANES]
        out_ref[pl.ds(j, rows, stride=SUBLANES), :] = piece.astype(F32)


def widen(features):
    rows, width = features.shape
    block = rows // 8
    return pl.pallas_call(
        widen_kernel,
        out_shape=struct((rows * SUBLANES, LANES), F32),
        grid=(rows // block,),
        in_specs=[pl.BlockSpec((block, width), lambda i: (i, 0))],
        out_specs=pl.BlockSpec((block * SUBLANES, LANES), lambda i: (i, 0)),
        compiler_params=params(10),
        cost_estimate=cost(rows * width, rows * width * 6),
        name="widen",
    )(features)


def serve_kernel(asked_ref, rows_ref, out_ref, picked):
    askers, each = asked_ref.shape
    count, width = out_ref.shape

    def one_asker(p, carry):
        for q in range(each):
            source = pl.multiple_of(asked_ref[p, q] * SUBLANES, SUBLANES)
            target = pl.multiple_of((p * each + q) * SUBLANES, SUBLANES)
            picked[pl.ds(target, SUBLANES), :] = rows_ref[pl.ds(source, SUBLANES), :]
        return carry

    lax.fori_loop(0, askers, one_asker, 0)
    for j in range(width // LANES):
        piece = picked[pl.ds(j, count, stride=SUBLANES), :]
        out_ref[:, j * LANES : (j + 1) * LANES] = piece.astype(BF)


def serve(asked, wide, width):
    count = asked.size
    return pl.pallas_call(
        serve_kernel,
        out_shape=struct((count, width), BF),
        in_specs=[SMEM, VMEM],
        out_specs=VMEM,
        scratch_shapes=[pltpu.VMEM((count * SUBLANES, LANES), F32)],
        compiler_params=params(26),
        cost_estimate=cost(count * width, count * width * 10),
        name="serve",
    )(asked, wide)


def pass_kernel(
    core_ref, fetched_ref, own_sel_ref, sum_sel_ref, scale_ref, outer_sel_ref, outer_scale_ref,
    back_ref, self_t_ref, neigh_t_ref, cot_t_ref, self_two_ref, neigh_two_ref,
    logits_ref, keep_ref, send_ref, own_t, mean_t, back_t, first, second,
):
    batches = fetched_ref.shape[1]
    slots = own_sel_ref.shape[1]
    width = self_t_ref.shape[1]
    hidden = self_t_ref.shape[0]
    seeds, classes = logits_ref.shape[1:]
    nodes = own_sel_ref.shape[2]
    second[:, classes:, :] = jnp.zeros((2, second.shape[1] - classes, hidden), F32)
    for b in range(batches):
        here = slice(b * nodes, (b + 1) * nodes)
        table = fetched_ref[:, b].reshape(slots, width).T
        own_t[:, here] = nn(table, own_sel_ref[b]).astype(BF)
        mean_t[:, here] = (nn(table, sum_sel_ref[b]) * scale_ref[b]).astype(BF)
        pre = nn(self_t_ref[...], own_t[:, here]) + nn(neigh_t_ref[...], mean_t[:, here])
        gate = 1.0 / (1.0 + jnp.exp(-pre))
        hidden_t = (pre * gate).astype(BF)
        back_t[:, here] = (back_ref[b] * (gate * (1.0 + pre * (1.0 - gate)))).astype(BF)
        outer_t = (nn(hidden_t, outer_sel_ref[b]) * outer_scale_ref[b]).astype(BF)
        seed_t = hidden_t[:, 0:seeds]
        logits_ref[b, :, :] = (nn(self_two_ref[...], seed_t) + nn(neigh_two_ref[...], outer_t)).T
        self_grad = nt(cot_t_ref[b], seed_t)
        neigh_grad = nt(cot_t_ref[b], outer_t)
        if b == 0:
            second[0, 0:classes, :] = self_grad
            second[1, 0:classes, :] = neigh_grad
        else:
            second[0, 0:classes, :] += self_grad
            second[1, 0:classes, :] += neigh_grad
    first[0] = nt(own_t[...], back_t[...])
    first[1] = nt(mean_t[...], back_t[...])
    core = core_ref[0]
    keep_ref[0:width, :] = first[core]
    keep_ref[width:, :] = second[core]
    send_ref[0:width, :] = first[1 - core].astype(BF)
    send_ref[width:, :] = second[1 - core].astype(BF)


def both_passes(core, fetched, planned, self_two, neigh_two, logit_shape):
    batches = fetched.shape[1]
    width = fetched.shape[3]
    hidden = self_two.shape[1]
    nodes = planned[0].shape[2]
    tail = hidden // 2
    return pl.pallas_call(
        pass_kernel,
        out_shape=(
            struct(logit_shape, F32),
            struct((width + tail, hidden), F32),
            struct((width + tail, hidden), BF),
        ),
        in_specs=[SMEM] + [VMEM] * 12,
        out_specs=[VMEM] * 3,
        scratch_shapes=[
            pltpu.VMEM((width, batches * nodes), BF),
            pltpu.VMEM((width, batches * nodes), BF),
            pltpu.VMEM((hidden, batches * nodes), BF),
            pltpu.VMEM((2, width, hidden), F32),
            pltpu.VMEM((2, tail, hidden), F32),
        ],
        compiler_params=params(32),
        cost_estimate=cost(6_000_000_000, 20_000_000),
        name="both_passes",
    )(core, fetched, *planned, self_two, neigh_two)


def add_kernel(keep_ref, got_ref, out_ref):
    out_ref[...] = (keep_ref[...] + got_ref[...].astype(F32)).astype(BF)


def add_pair(keep, got):
    return pl.pallas_call(
        add_kernel,
        out_shape=struct(keep.shape, BF),
        in_specs=[VMEM] * 2,
        out_specs=VMEM,
        compiler_params=params(6),
        cost_estimate=cost(keep.size, keep.size * 8),
        name="add_pair",
    )(keep, got)


def sum_kernel(parts_ref, out_ref):
    total = parts_ref[0].astype(F32)
    for i in range(1, parts_ref.shape[0]):
        total += parts_ref[i].astype(F32)
    out_ref[...] = total.astype(BF)


def sum_parts(parts):
    return pl.pallas_call(
        sum_kernel,
        out_shape=struct(parts.shape[1:], BF),
        in_specs=[VMEM],
        out_specs=VMEM,
        compiler_params=params(3),
        cost_estimate=cost(parts.size, parts.size * 4),
        name="sum_parts",
    )(parts)


def total_kernel(own_ref, next_ref, across_ref, last_ref, out_ref):
    near = own_ref[...].astype(F32) + across_ref[...].astype(F32)
    far = next_ref[...].astype(F32) + last_ref[...].astype(F32)
    total = (near + far).astype(BF)
    for i in range(out_ref.shape[0]):
        out_ref[i] = total


def total_copies(own, got, copies):
    return pl.pallas_call(
        total_kernel,
        out_shape=struct((copies,) + own.shape, BF),
        in_specs=[VMEM] * 4,
        out_specs=VMEM,
        compiler_params=params(3),
        cost_estimate=cost(own.size * copies, own.size * copies * 2),
        name="total_copies",
    )(own, *got)


def unpack_kernel(
    core_ref, mine_ref, other_ref, mine_tail_ref, other_tail_ref,
    self_one_ref, neigh_one_ref, self_two_ref, neigh_two_ref,
):
    classes = self_two_ref.shape[0]

    def place(mine, other, mine_tail, other_tail):
        mine[...] = mine_ref[...].astype(F32)
        other[...] = other_ref[...].astype(F32)

        @pl.when(pl.program_id(0) == 0)
        def _():
            mine_tail[...] = mine_tail_ref[0:classes, :].astype(F32)
            other_tail[...] = other_tail_ref[0:classes, :].astype(F32)

    @pl.when(core_ref[0] == 0)
    def _():
        place(self_one_ref, neigh_one_ref, self_two_ref, neigh_two_ref)

    @pl.when(core_ref[0] != 0)
    def _():
        place(neigh_one_ref, self_one_ref, neigh_two_ref, self_two_ref)


def unpack(core, mine, other, one_shape, two_shape):
    width, hidden = one_shape
    tail = mine.shape[0] - width
    steps = 4
    head = pl.BlockSpec((width // steps, hidden), lambda i: (i, 0))
    last = pl.BlockSpec((tail, hidden), lambda i: (width // tail, 0))
    two = pl.BlockSpec(two_shape, lambda i: (0, 0))
    return pl.pallas_call(
        unpack_kernel,
        out_shape=(
            struct(one_shape, F32),
            struct(one_shape, F32),
            struct(two_shape, F32),
            struct(two_shape, F32),
        ),
        grid=(steps,),
        in_specs=[SMEM, head, head, last, last],
        out_specs=[head, head, two, two],
        compiler_params=params(8),
        cost_estimate=cost(mine.size, mine.size * 12),
        name="unpack",
    )(core, mine, other, mine, other)


def exchange(value, axes):
    return lax.all_to_all(value, axes, split_axis=0, concat_axis=0, tiled=True)


def swap_cores(value):
    return lax.ppermute(value, "core", [(0, 1), (1, 0)])


def body(
    features, self_one, neigh_one, self_two, neigh_two, bucket_counts, request_rows,
    layer_targets, inner_slots, outer_slots, outer_degree, cotangent,
):
    batches, _, owners, capacity = request_rows.shape
    width, hidden = self_one.shape
    core = lax.axis_index("core").reshape(1).astype(jnp.int32)
    wanted = request_rows[:, 0].transpose(1, 0, 2).reshape(owners, batches * capacity)
    asked = exchange(wanted, ("chip", "core"))
    wide = widen(features)
    planned = plan(
        bucket_counts[:, 0],
        layer_targets,
        inner_slots.transpose(0, 2, 1),
        outer_slots.transpose(0, 2, 1),
        outer_degree,
        cotangent,
        self_one,
        neigh_one,
        self_two.T,
        neigh_two.T,
    )
    rows = serve(asked, wide, width)
    fetched = exchange(rows.reshape(owners, batches, capacity, width), ("chip", "core"))
    logits, keep, send = both_passes(
        core, fetched, planned, self_two.T, neigh_two.T, cotangent.shape
    )
    half = add_pair(keep, swap_cores(send))
    plane = ("chip", "near")
    parties = lax.axis_size(plane)
    far = lax.axis_size("far")
    piece = half.shape[0] // parties
    own = sum_parts(exchange(half.reshape(parties, piece, hidden), plane))
    got = [
        lax.ppermute(own, "far", [(i, (i + shift) % far) for i in range(far)])
        for shift in range(1, far)
    ]
    mine = exchange(total_copies(own, got, parties), plane).reshape(half.shape)
    grads = unpack(core, mine, swap_cores(mine), self_one.shape, self_two.T.shape)
    return (logits, grads[0], grads[1], grads[2].T, grads[3].T)


def solution(mesh):
    stores, trainers = mesh.shape["store"], mesh.shape["trainer"]
    split = Mesh(
        mesh.devices.reshape(stores // 2, 2, trainers // 2, 2), ("chip", "core", "far", "near")
    )
    store = ("chip", "core")
    every = ("chip", "core", "far", "near")
    in_specs = (
        P(store, None),
        P(),
        P(),
        P(),
        P(),
        P(None, every, None),
        P(None, every, None, None),
        P(None, every),
        P(None, every, None),
        P(None, every, None),
        P(None, every),
        P(None, every, None),
    )
    out_specs = (P(None, every, None), P(), P(), P(), P())
    return jax.shard_map(
        body, mesh=split, in_specs=in_specs, out_specs=out_specs, check_vma=False
    )
```

time: 161 us -> 143 us (0.89)
  blocking collectives: 77.6 us -> 39 us
  starting transfers between devices: 10.8 us -> 32.1 us
  local copies, waits for them, and re-layouts: 11.9 us -> 33 us
  Pallas kernels: 42.4 us -> 21.5 us
    all_to_all x4 -> x2, blocking collectives: 77.6 us -> 39 us  [exchange(): return lax.all_to_all(value, axes, split_axis=0, concat_axis=0, tiled=True)]
    unnamed x22 -> x56, local copies, waits for them, and re-layouts: 9.94 us -> 31.6 us
    all_to_all x1 -> x2, starting transfers between devices: 4.43 us -> 16.1 us  [exchange(): return lax.all_to_all(value, axes, split_axis=0, concat_axis=0, tiled=True)]
    ppermute x0 -> x3, starting transfers between devices: none -> 9.84 us  [body(): lax.ppermute(own, 'far', [(i, (i + shift) % far) for i in range(far)])]
    pallas_call x3 -> x4, Pallas kernels: 15.7 us -> 7.48 us  [the longest x1 3.93 us: serve(): pl.pallas_call(serve_kernel, out_shape=struct((count, width), BF), in_spe...]
    pallas_call x1, Pallas kernels: 11.8 us -> 7.36 us  [both_passes(): pl.pallas_call(pass_kernel, out_shape=(struct(logit_shape, F32), struct((...]
    pallas_call x1, Pallas kernels: 8.09 us -> 4.12 us  [plan(): pl.pallas_call(plan_kernel, out_shape=(struct((batches, slots, nodes), BF...]
    pallas_call x1, Pallas kernels: 3 us -> 0.17 us  [add_pair(): pl.pallas_call(add_kernel, out_shape=struct(keep.shape, BF), in_specs=[VM...]
  transfers between devices with their start and end apart: 3 -> 7, of which waited for: 3 -> 5; matrix products, arithmetic and copies ran while one was open for 2% -> 1% of each run, Pallas kernels for 5% -> 5%
where the time goes in v2:
time: 143 us
  blocking collectives  39 us (27%)
  local copies, waits for them, and re-layouts  33 us (23%)
  starting transfers between devices  32.1 us (22%)
  Pallas kernels  21.5 us (15%)
  waiting for transfers between devices  16.1 us (11%)
    all_to_all x2, blocking collectives, exchange(): return lax.all_to_all(value, axes, split_axis=0, concat_axis=0, tiled=True)  39 us
    unnamed x56, local copies, waits for them, and re-layouts  31.6 us
    all_to_all x2, starting transfers between devices, exchange(): return lax.all_to_all(value, axes, split_axis=0, concat_axis=0, tiled=True)  16.1 us
    ppermute x3, starting transfers between devices, body(): lax.ppermute(own, 'far', [(i, (i + shift) % far) for i in range(far)])  9.84 us
    all_to_all x2, waiting for transfers between devices, exchange(): return lax.all_to_all(value, axes, split_axis=0, concat_axis=0, tiled=True)  9.49 us
    pallas_call x1, Pallas kernels, both_passes(): pl.pallas_call(pass_kernel, out_shape=(struct(logit_shape, F32), struct((...  7.36 us
    ppermute x2, starting transfers between devices, swap_cores(): return lax.ppermute(value, 'core', [(0, 1), (1, 0)])  6.13 us
    ppermute x2, waiting for transfers between devices, swap_cores(): return lax.ppermute(value, 'core', [(0, 1), (1, 0)])  4.57 us
  transfers between devices with their start and end apart: 7, of which 5 were waited for; matrix products, arithmetic and copies ran while one was open for 1% of the time, Pallas kernels for 5%

profile of v2, /device:TPU:1, one launch (start us, length us, event | category | flops | bytes accessed | tf_op | source)
XLA Modules:
  0.0 142.5 jit_solution(17661781745711165639)
XLA Ops:
  0.6 1.4 copy.23
  2.0 8.6 %all-to-all-start = ((s32[32,1,32]{2,1,0:T(1,128)}), s32[32,1,32]{2,1,0:T(1,128)S(1)}, u32[]{:S(2)}, u32[]{:S(2)}) async-start(s32[32,1,32]{2,1,0:T(1,128)} %copy.23), calls=%async_computation | async-start | bytes 32768 | tf_op jit(solution)/shard_map/all_to_all | solution.py:348
  10.6 0.0 copy-start.2
  10.6 2.8 %copy-done.2 = bf16[4096,768]{1,0:T(8,128)(2,1)S(1)} copy-done((bf16[4096,768]{1,0:T(8,128)(2,1)S(1)}, bf16[4096,768]{1,0:T(8,128)(2,1)}, u32[]{:S(2)}) %copy-start.2) | copy-done | bytes 6291480
  13.4 3.3 %widen.1.rows_ref = f32[32768,128]{1,0:T(8,128)S(1)} custom-call(bf16[4096,768]{1,0:T(8,128)(2,1)S(1)} %copy-done.2), custom_call_target="tpu_custom_call" | custom-call | flops 3145728 | bytes 18874368 | tf_op jit(solution)/shard_map/widen/pallas_call | solution.py:132
  16.7 5.7 %copy-done = f32[32768,128]{1,0:T(8,128)} copy-done((f32[32768,128]{1,0:T(8,128)}, f32[32768,128]{1,0:T(8,128)S(1)}, u32[]{:S(2)}) %copy-start) | copy-done | bytes 16777240
  22.5 5.8 %copy-done.1 = f32[32768,128]{1,0:T(8,128)S(1)} copy-done((f32[32768,128]{1,0:T(8,128)S(1)}, f32[32768,128]{1,0:T(8,128)}, u32[]{:S(2)}) %copy-start.1) | copy-done | bytes 16777240
  28.2 3.9 %serve.1 = bf16[1024,768]{1,0:T(8,128)(2,1)} custom-call(s32[32,32]{1,0:T(8,128)S(1)} %bitcast.31, f32[32768,128]{1,0:T(8,128)S(1)} %copy-done.1), custom_call_target="tpu_custom_call" | custom-call | flops 786432 | bytes 7864320 | tf_op jit(solution)/shard_map/serve/pallas_call | solution.py:163
  32.2 0.0 copy-start.7
  32.2 0.0 copy-start.9
  32.2 0.0 copy-start.10
  32.2 7.5 %all-to-all-start.1 = ((bf16[32,2,16,768]{3,2,1,0:T(8,128)(2,1)}), bf16[32,2,16,768]{3,2,1,0:T(8,128)(2,1)S(1)}, u32[]{:S(2)}, u32[]{:S(2)}) async-start(bf16[32,2,16,768]{3,2,1,0:T(8,128)(2,1)} %bitcast.5), calls=%async_computation.1 | async-start | bytes 3145728 | tf_op jit(solution)/shard_map/all_to_all | solution.py:348
  39.8 0.8 copy.28
  40.6 0.7 copy.29
  41.3 4.1 %plan.1 = (bf16[2,512,512]{2,1,0:T(8,128)(2,1)S(1)}, bf16[2,512,512]{2,1,0:T(8,128)(2,1)S(1)}, f32[2,1,512]{2,1,0:T(1,128)S(1)}, bf16[2,512,64]{2,1,0:T(8,128)(2...) custom-call(s32[2,32]{1,0:T(2,128)S(1)} %bitcast.32, ...), custom_call_target="tpu_custom_call" | custom-call | flops 200000000 | bytes 10000000 | tf_op jit(solution)/shard_map/plan/pallas_call | solution.py:101
  45.5 1.4 copy-done.11
  46.8 1.0 copy-done.13
  47.8 1.0 copy-done.15
  48.8 0.9 copy-done.17
  49.7 0.9 copy-done.19
  50.6 0.7 copy-done.21
  51.3 0.6 copy-done.23
  51.9 0.6 copy-done.25
  52.5 9.5 %all-to-all-done.1.fetched_ref = bf16[32,2,16,768]{3,2,1,0:T(8,128)(2,1)S(1)} async-done(((bf16[32,2,16,768]{3,2,1,0:T(8,128)(2,1)}), bf16[32,2,16,768]{3,2,1,0:T(8,128)(2,1)S(1)}, u32[]{:S(2)}, u32[]{:S(2)}) %all-to-all-start.1) | async-done | bytes 1572896 | tf_op jit(solution)/shard_map/all_to_all | solution.py:348
  61.9 1.6 %copy-done.12 = f32[2,512,512]{2,1,0:T(8,128)S(1)} copy-done((f32[2,512,512]{2,1,0:T(8,128)S(1)}, f32[2,512,512]{2,1,0:T(8,128)}, u32[]{:S(2)}) %copy-start.12) | copy-done | bytes 2097176
  63.5 1.2 copy-done.14
  64.8 1.2 copy-done.16
  66.0 1.1 copy-done.18
  67.1 1.1 copy-done.20
  68.3 0.9 copy-done.22
  69.2 0.9 copy-done.24
  70.1 0.7 copy-done.26
  70.8 7.4 %both_passes.1 = (f32[2,64,153]{2,1,0:T(8,128)}, f32[1024,512]{1,0:T(8,128)S(1)}, bf16[1024,512]{1,0:T(8,128)(2,1)S(1)}) custom-call(s32[1]{0:T(128)} %bitcast.core_ref, bf16[32,2,16,768]{3,2,1,0:T(8,128)(2,1)S(1)} %all-to-all-done.1.fetched_ref, bf16[2,512,512]{2,1,0:T(8,128)(2,1)S(1)} %copy-done.14, bf16[2,512,512]{2,1,0:T(8,128)(2,1)S(1)} %copy-done.16, ...), custom_call_target="tpu_custom_call" | custom-call | flops 6000000000 | bytes 20000000 | tf_op jit(solution)/shard_map/both_passes/pallas_call | solution.py:222
  78.1 2.0 %collective-permute-start = (bf16[1024,512]{1,0:T(8,128)(2,1)S(1)}, bf16[1024,512]{1,0:T(8,128)(2,1)S(1)}, u32[]{:S(2)}, u32[]{:S(2)}) collective-permute-start(bf16[1024,512]{1,0:T(8,128)(2,1)S(1)} %get-tuple-element.32), channel_id=1, source_target_pairs={{0,8},{8,0},{1,9},{9,1},{2,10},{10,2},{3,11},{11,3},{4,12},{12,4},... | collective-permute-start | bytes 3145736 | tf_op jit(solution)/shard_map/ppermute | solution.py:352
  80.1 2.3 %collective-permute-done.got_ref = bf16[1024,512]{1,0:T(8,128)(2,1)S(1)} collective-permute-done((bf16[1024,512]{1,0:T(8,128)(2,1)S(1)}, bf16[1024,512]{1,0:T(8,128)(2,1)S(1)}, u32[]{:S(2)}, u32[]{:S(2)}) %collective-permute-start) | collective-permute-done | bytes 1048608 | tf_op jit(solution)/shard_map/ppermute | solution.py:352
  82.4 0.2 add_pair.1
  82.6 21.2 %all_to_all.26.parts_ref = bf16[32,32,512]{2,1,0:T(8,128)(2,1)S(1)} all-to-all(bf16[32,32,512]{2,1,0:T(8,128)(2,1)S(1)} %bitcast.24), channel_id=1, replica_groups=mesh['chip'=16,'core'=2,'far'=4,'near'=2] {'chip','near'}, dimensions={0} | all-to-all | bytes 2097152 | tf_op jit(solution)/shard_map/all_to_all | solution.py:348
  103.8 0.1 sum_parts.1.own_ref
  103.9 3.2 %collective-permute-start.1 = (bf16[32,512]{1,0:T(8,128)(2,1)S(1)}, bf16[32,512]{1,0:T(8,128)(2,1)S(1)}, u32[]{:S(2)}, u32[]{:S(2)}) collective-permute-start(bf16[32,512]{1,0:T(8,128)(2,1)S(1)} %sum_parts.1.own_ref), channel_id=1, source_target_pairs={{0,2},{2,4},{4,6},{6,0},{1,3},{3,5},{5,7},{7,1},{8,10},{10,12},{12... | collective-permute-start | bytes 98312 | tf_op jit(solution)/shard_map/ppermute | solution.py:389
  107.2 4.2 %collective-permute-start.2 = (bf16[32,512]{1,0:T(8,128)(2,1)S(1)}, bf16[32,512]{1,0:T(8,128)(2,1)S(1)}, u32[]{:S(2)}, u32[]{:S(2)}) collective-permute-start(bf16[32,512]{1,0:T(8,128)(2,1)S(1)} %sum_parts.1.own_ref), channel_id=1, source_target_pairs={{0,4},{2,6},{4,0},{6,2},{1,5},{3,7},{5,1},{7,3},{8,12},{10,14},{12... | collective-permute-start | bytes 98312 | tf_op jit(solution)/shard_map/ppermute | solution.py:389
  111.4 2.4 %collective-permute-start.3 = (bf16[32,512]{1,0:T(8,128)(2,1)S(1)}, bf16[32,512]{1,0:T(8,128)(2,1)S(1)}, u32[]{:S(2)}, u32[]{:S(2)}) collective-permute-start(bf16[32,512]{1,0:T(8,128)(2,1)S(1)} %sum_parts.1.own_ref), channel_id=1, source_target_pairs={{0,6},{2,0},{4,2},{6,4},{1,7},{3,1},{5,3},{7,5},{8,14},{10,8},{12,... | collective-permute-start | bytes 98312 | tf_op jit(solution)/shard_map/ppermute | solution.py:389
  113.8 0.4 collective-permute-done.2.across_ref
  114.2 1.6 %collective-permute-done.3.last_ref = bf16[32,512]{1,0:T(8,128)(2,1)S(1)} collective-permute-done((bf16[32,512]{1,0:T(8,128)(2,1)S(1)}, bf16[32,512]{1,0:T(8,128)(2,1)S(1)}, u32[]{:S(2)}, u32[]{:S(2)}) %collective-permute-start.3) | collective-permute-done | bytes 32800 | tf_op jit(solution)/shard_map/ppermute | solution.py:389
  115.8 0.1 total_copies.1
  115.9 17.7 %all_to_all.27 = bf16[32,32,512]{2,1,0:T(8,128)(2,1)S(1)} all-to-all(bf16[32,32,512]{2,1,0:T(8,128)(2,1)S(1)} %total_copies.1), channel_id=1, replica_groups=mesh['chip'=16,'core'=2,'far'=4,'near'=2] {'chip','near'}, dimensions={0} | all-to-all | bytes 2097152 | tf_op jit(solution)/shard_map/all_to_all | solution.py:348
  133.7 4.1 %collective-permute-start.4 = (bf16[1024,512]{1,0:T(8,128)(2,1)S(1)}, bf16[1024,512]{1,0:T(8,128)(2,1)S(1)}, u32[]{:S(2)}, u32[]{:S(2)}) collective-permute-start(bf16[1024,512]{1,0:T(8,128)(2,1)S(1)} %bitcast.21), channel_id=1, source_target_pairs={{0,8},{8,0},{1,9},{9,1},{2,10},{10,2},{3,11},{11,3},{4,12},{12,4},... | collective-permute-start | bytes 3145736 | tf_op jit(solution)/shard_map/ppermute | solution.py:352
  137.8 2.3 %collective-permute-done.4.other_ref.other_tail_ref = bf16[1024,512]{1,0:T(8,128)(2,1)S(1)} collective-permute-done((bf16[1024,512]{1,0:T(8,128)(2,1)S(1)}, bf16[1024,512]{1,0:T(8,128)(2,1)S(1)}, u32[]{:S(2)}, u32[]{:S(2)}) %collective-permute-start.4) | collective-permute-done | bytes 1048608 | tf_op jit(solution)/shard_map/ppermute | solution.py:352
  140.1 2.4 %unpack.1 = (f32[768,512]{1,0:T(8,128)}, f32[768,512]{1,0:T(8,128)}, f32[153,512]{1,0:T(8,128)}, f32[153,512]{1,0:T(8,128)}) custom-call(s32[1]{0:T(128)} %bitcast.core_ref, bf16[1024,512]{1,0:T(8,128)(2,1)S(1)} %bitcast.22, bf16[1024,512]{1,0:T(8,128)(2,1)S(1)} %collective-permute-done.4.other_ref.other_tail_ref, bf16[1024,512]{1,0:T(8,128)(2,1)S(1)} %bitcast.23, ...), custom_call_target="tpu_custom_call" | custom-call | flops 524288 | bytes 6291456 | tf_op jit(solution)/shard_map/unpack/pallas_call | solution.py:330
  (33 shorter events, 0.1 us)
Async XLA Ops:
  2.0 20.4 %all-to-all-start = ((s32[32,1,32]{2,1,0:T(1,128)}), s32[32,1,32]{2,1,0:T(1,128)S(1)}, u32[]{:S(2)}, u32[]{:S(2)}) async-start(s32[32,1,32]{2,1,0:T(1,128)} %copy.23), calls=%async_computation | async-start | bytes 32768 | tf_op jit(solution)/shard_map/all_to_all | solution.py:348
  10.6 2.8 %copy-start.2 = (bf16[4096,768]{1,0:T(8,128)(2,1)S(1)}, bf16[4096,768]{1,0:T(8,128)(2,1)}, u32[]{:S(2)}) copy-start(bf16[4096,768]{1,0:T(8,128)(2,1)} %rows_ref.1) | copy-start | bytes 18874372
  16.7 5.8 %copy-start = (f32[32768,128]{1,0:T(8,128)}, f32[32768,128]{1,0:T(8,128)S(1)}, u32[]{:S(2)}) copy-start(f32[32768,128]{1,0:T(8,128)S(1)} %widen.1.rows_ref) | copy-start | bytes 50331652
  22.5 5.8 %copy-start.1 = (f32[32768,128]{1,0:T(8,128)S(1)}, f32[32768,128]{1,0:T(8,128)}, u32[]{:S(2)}) copy-start(f32[32768,128]{1,0:T(8,128)} %copy-done) | copy-start | bytes 50331652
  32.2 9.1 %copy-start.3 = (bf16[768,512]{1,0:T(8,128)(2,1)S(1)}, bf16[768,512]{1,0:T(8,128)(2,1)}, u32[]{:S(2)}) copy-start(bf16[768,512]{1,0:T(8,128)(2,1)} %self_one_ref.1) | copy-start | bytes 2359300
  32.2 9.1 %copy-start.4 = (bf16[768,512]{1,0:T(8,128)(2,1)S(1)}, bf16[768,512]{1,0:T(8,128)(2,1)}, u32[]{:S(2)}) copy-start(bf16[768,512]{1,0:T(8,128)(2,1)} %neigh_one_ref.1) | copy-start | bytes 2359300
  32.2 9.1 %copy-start.5 = (bf16[512,153]{0,1:T(8,128)(2,1)S(1)}, bf16[512,153]{0,1:T(8,128)(2,1)}, u32[]{:S(2)}) copy-start(bf16[512,153]{0,1:T(8,128)(2,1)} %param.15) | copy-start | bytes 470020
  32.2 9.1 %copy-start.6 = (bf16[512,153]{0,1:T(8,128)(2,1)S(1)}, bf16[512,153]{0,1:T(8,128)(2,1)}, u32[]{:S(2)}) copy-start(bf16[512,153]{0,1:T(8,128)(2,1)} %param.16) | copy-start | bytes 470020
  32.2 9.1 %copy-start.7 = (bf16[2,64,153]{2,1,0:T(8,128)(2,1)S(1)}, bf16[2,64,153]{2,1,0:T(8,128)(2,1)}, u32[]{:S(2)}) copy-start(bf16[2,64,153]{2,1,0:T(8,128)(2,1)} %cot_ref.1) | copy-start | bytes 117508
  32.2 9.1 %copy-start.8 = (s32[2,512]{1,0:T(2,128)S(1)}, s32[2,512]{1,0:T(2,128)}, u32[]{:S(2)}) copy-start(s32[2,512]{1,0:T(2,128)} %targets_ref.1) | copy-start | bytes 12292
  32.2 9.1 %copy-start.9 = (s32[2,1,32]{2,1,0:T(1,128)S(1)}, s32[2,1,32]{2,1,0:T(1,128)}, u32[]{:S(2)}) copy-start(s32[2,1,32]{2,1,0:T(1,128)} %param.17) | copy-start | bytes 772
  32.2 9.1 %copy-start.10 = (s32[2,64]{1,0:T(2,128)S(1)}, s32[2,64]{1,0:T(2,128)}, u32[]{:S(2)}) copy-start(s32[2,64]{1,0:T(2,128)} %degree_ref.1) | copy-start | bytes 1540
  32.2 29.7 %all-to-all-start.1 = ((bf16[32,2,16,768]{3,2,1,0:T(8,128)(2,1)}), bf16[32,2,16,768]{3,2,1,0:T(8,128)(2,1)S(1)}, u32[]{:S(2)}, u32[]{:S(2)}) async-start(bf16[32,2,16,768]{3,2,1,0:T(8,128)(2,1)} %bitcast.5), calls=%async_computation.1 | async-start | bytes 3145728 | tf_op jit(solution)/shard_map/all_to_all | solution.py:348
  45.5 1.4 copy-start.11
  46.8 1.0 copy-start.13
  47.8 1.0 copy-start.15
  48.8 0.9 copy-start.17
  49.7 0.9 copy-start.19
  50.6 0.7 copy-start.21
  51.3 0.6 copy-start.23
  51.9 0.6 copy-start.25
  61.9 1.6 %copy-start.12 = (f32[2,512,512]{2,1,0:T(8,128)S(1)}, f32[2,512,512]{2,1,0:T(8,128)}, u32[]{:S(2)}) copy-start(f32[2,512,512]{2,1,0:T(8,128)} %copy-done.11) | copy-start | bytes 6291460
  63.5 1.2 copy-start.14
  64.8 1.2 copy-start.16
  66.0 1.1 copy-start.18
  67.1 1.1 copy-start.20
  68.3 0.9 copy-start.22
  69.2 0.9 copy-start.24
  70.1 0.7 copy-start.26
  78.1 4.3 %collective-permute-start = (bf16[1024,512]{1,0:T(8,128)(2,1)S(1)}, bf16[1024,512]{1,0:T(8,128)(2,1)S(1)}, u32[]{:S(2)}, u32[]{:S(2)}) collective-permute-start(bf16[1024,512]{1,0:T(8,128)(2,1)S(1)} %get-tuple-element.32), channel_id=1, source_target_pairs={{0,8},{8,0},{1,9},{9,1},{2,10},{10,2},{3,11},{11,3},{4,12},{12,4},... | collective-permute-start | bytes 3145736 | tf_op jit(solution)/shard_map/ppermute | solution.py:352
  103.9 9.8 %collective-permute-start.1 = (bf16[32,512]{1,0:T(8,128)(2,1)S(1)}, bf16[32,512]{1,0:T(8,128)(2,1)S(1)}, u32[]{:S(2)}, u32[]{:S(2)}) collective-permute-start(bf16[32,512]{1,0:T(8,128)(2,1)S(1)} %sum_parts.1.own_ref), channel_id=1, source_target_pairs={{0,2},{2,4},{4,6},{6,0},{1,3},{3,5},{5,7},{7,1},{8,10},{10,12},{12... | collective-permute-start | bytes 98312 | tf_op jit(solution)/shard_map/ppermute | solution.py:389
  107.2 7.0 %collective-permute-start.2 = (bf16[32,512]{1,0:T(8,128)(2,1)S(1)}, bf16[32,512]{1,0:T(8,128)(2,1)S(1)}, u32[]{:S(2)}, u32[]{:S(2)}) collective-permute-start(bf16[32,512]{1,0:T(8,128)(2,1)S(1)} %sum_parts.1.own_ref), channel_id=1, source_target_pairs={{0,4},{2,6},{4,0},{6,2},{1,5},{3,7},{5,1},{7,3},{8,12},{10,14},{12... | collective-permute-start | bytes 98312 | tf_op jit(solution)/shard_map/ppermute | solution.py:389
  111.4 4.4 %collective-permute-start.3 = (bf16[32,512]{1,0:T(8,128)(2,1)S(1)}, bf16[32,512]{1,0:T(8,128)(2,1)S(1)}, u32[]{:S(2)}, u32[]{:S(2)}) collective-permute-start(bf16[32,512]{1,0:T(8,128)(2,1)S(1)} %sum_parts.1.own_ref), channel_id=1, source_target_pairs={{0,6},{2,0},{4,2},{6,4},{1,7},{3,1},{5,3},{7,5},{8,14},{10,8},{12,... | collective-permute-start | bytes 98312 | tf_op jit(solution)/shard_map/ppermute | solution.py:389
  133.7 6.4 %collective-permute-start.4 = (bf16[1024,512]{1,0:T(8,128)(2,1)S(1)}, bf16[1024,512]{1,0:T(8,128)(2,1)S(1)}, u32[]{:S(2)}, u32[]{:S(2)}) collective-permute-start(bf16[1024,512]{1,0:T(8,128)(2,1)S(1)} %bitcast.21), channel_id=1, source_target_pairs={{0,8},{8,0},{1,9},{9,1},{2,10},{10,2},{3,11},{11,3},{4,12},{12,4},... | collective-permute-start | bytes 3145736 | tf_op jit(solution)/shard_map/ppermute | solution.py:352

commit v3 on v2

--- a/solution.py
+++ b/solution.py
@@ -9,6 +9,7 @@
 F32 = jnp.float32
 VMEM = pl.BlockSpec(memory_space=pltpu.VMEM)
 SMEM = pl.BlockSpec(memory_space=pltpu.SMEM)
+ANY = pl.BlockSpec(memory_space=pl.ANY)
 LANES = 128
 SUBLANES = 8
 
@@ -27,6 +28,10 @@
 
 def struct(shape, dtype):
     return jax.ShapeDtypeStruct(shape, dtype)
+
+
+def in_hbm(value):
+    return pltpu.with_memory_space_constraint(value, pltpu.HBM)
 
 
 def params(mebibytes):
@@ -101,15 +106,15 @@
     return pl.pallas_call(
         plan_kernel,
         out_shape=(
-            struct((batches, slots, nodes), BF),
-            struct((batches, slots, nodes), BF),
-            struct((batches, 1, nodes), F32),
-            struct((batches, nodes, seeds), BF),
-            struct((batches, 1, seeds), F32),
-            struct((batches, hidden, nodes), F32),
-            struct((hidden, width), BF),
-            struct((hidden, width), BF),
-            struct((batches, classes, seeds), BF),
+            pltpu.HBM((batches, slots, nodes), BF),
+            pltpu.HBM((batches, slots, nodes), BF),
+            pltpu.HBM((batches, 1, nodes), F32),
+            pltpu.HBM((batches, nodes, seeds), BF),
+            pltpu.HBM((batches, 1, seeds), F32),
+            pltpu.HBM((batches, hidden, nodes), F32),
+            pltpu.HBM((hidden, width), BF),
+            pltpu.HBM((hidden, width), BF),
+            pltpu.HBM((batches, classes, seeds), BF),
         ),
         in_specs=[VMEM] * 10,
         out_specs=[VMEM] * 9,
@@ -119,80 +124,131 @@
     )(counts, targets, inner, outer, degree, cot, self_one, neigh_one, self_two, neigh_two)
 
 
-def widen_kernel(rows_ref, out_ref):
+def serve_kernel(asked_ref, rows_ref, out_ref, landed, wide, sems):
+    askers, each = asked_ref.shape
     rows, width = rows_ref.shape
-    for j in range(width // LANES):
-        piece = rows_ref[:, j * LANES : (j + 1) * LANES]
-        out_ref[pl.ds(j, rows, stride=SUBLANES), :] = piece.astype(F32)
-
-
-def widen(features):
+    chunks = sems.shape[0]
+    block = rows // chunks
+    pieces = width // LANES
+
+    def load(c):
+        here = pl.ds(c * block, block)
+        return pltpu.make_async_copy(rows_ref.at[here, :], landed.at[here, :], sems.at[c])
+
+    for c in range(chunks):
+        load(c).start()
+    for c in range(chunks):
+        load(c).wait()
+        for j in range(pieces):
+            piece = landed[pl.ds(c * block, block), j * LANES : (j + 1) * LANES]
+            wide[j, pl.ds(SUBLANES + c * block, block), :] = piece.astype(F32)
+
+    line = lax.broadcasted_iota(jnp.int32, (SUBLANES, LANES), 0)
+
+    def one_asker(p, carry):
+        for first in range(0, each, 2 * SUBLANES):
+            tiles = []
+            for half in range(2):
+                base = first + half * SUBLANES
+                starts = [asked_ref[p, base + i] + (SUBLANES - i) for i in range(SUBLANES)]
+                for j in range(pieces):
+                    tile = wide[j, pl.ds(starts[0], SUBLANES), :]
+                    for i in range(1, SUBLANES):
+                        tile = jnp.where(line == i, wide[j, pl.ds(starts[i], SUBLANES), :], tile)
+                    tiles.append(tile)
+            target = pl.ds(pl.multiple_of(p * each + first, 2 * SUBLANES), 2 * SUBLANES)
+            for j in range(pieces):
+                pair = jnp.concatenate([tiles[j], tiles[pieces + j]], axis=0)
+                out_ref[target, j * LANES : (j + 1) * LANES] = pair.astype(BF)
+        return carry
+
+    lax.fori_loop(0, askers, one_asker, 0)
+
+
+def serve(asked, features):
+    count = asked.size
     rows, width = features.shape
-    block = rows // 8
-    return pl.pallas_call(
-        widen_kernel,
-        out_shape=struct((rows * SUBLANES, LANES), F32),
-        grid=(rows // block,),
-        in_specs=[pl.BlockSpec((block, width), lambda i: (i, 0))],
-        out_specs=pl.BlockSpec((block * SUBLANES, LANES), lambda i: (i, 0)),
-        compiler_params=params(10),
-        cost_estimate=cost(rows * width, rows * width * 6),
-        name="widen",
-    )(features)
-
-
-def serve_kernel(asked_ref, rows_ref, out_ref, picked):
-    askers, each = asked_ref.shape
-    count, width = out_ref.shape
-
-    def one_asker(p, carry):
-        for q in range(each):
-            source = pl.multiple_of(asked_ref[p, q] * SUBLANES, SUBLANES)
-            target = pl.multiple_of((p * each + q) * SUBLANES, SUBLANES)
-            picked[pl.ds(target, SUBLANES), :] = rows_ref[pl.ds(source, SUBLANES), :]
-        return carry
-
-    lax.fori_loop(0, askers, one_asker, 0)
-    for j in range(width // LANES):
-        piece = picked[pl.ds(j, count, stride=SUBLANES), :]
-        out_ref[:, j * LANES : (j + 1) * LANES] = piece.astype(BF)
-
-
-def serve(asked, wide, width):
-    count = asked.size
+    chunks = 8
     return pl.pallas_call(
         serve_kernel,
         out_shape=struct((count, width), BF),
-        in_specs=[SMEM, VMEM],
+        in_specs=[SMEM, ANY],
         out_specs=VMEM,
-        scratch_shapes=[pltpu.VMEM((count * SUBLANES, LANES), F32)],
-        compiler_params=params(26),
-        cost_estimate=cost(count * width, count * width * 10),
+        scratch_shapes=[
+            pltpu.VMEM((rows, width), BF),
+            pltpu.VMEM((width // LANES, rows + 2 * SUBLANES, LANES), F32),
+            pltpu.SemaphoreType.DMA((chunks,)),
+        ],
+        compiler_params=params(28),
+        cost_estimate=cost(count * width, rows * width * 6),
         name="serve",
-    )(asked, wide)
+    )(asked, in_hbm(features))
 
 
 def pass_kernel(
-    core_ref, fetched_ref, own_sel_ref, sum_sel_ref, scale_ref, outer_sel_ref, outer_scale_ref,
-    back_ref, self_t_ref, neigh_t_ref, cot_t_ref, self_two_ref, neigh_two_ref,
-    logits_ref, keep_ref, send_ref, own_t, mean_t, back_t, first, second,
+    core_ref, fetched_ref, own_sel_hbm, sum_sel_hbm, scale_hbm, outer_sel_hbm, outer_scale_hbm,
+    back_hbm, self_t_hbm, neigh_t_hbm, cot_t_hbm, self_two_ref, neigh_two_ref,
+    logits_ref, send_ref, inputs_t, back_t, second,
+    own_sel_ref, sum_sel_ref, scale_ref, outer_sel_ref, outer_scale_ref, back_ref,
+    self_t_ref, neigh_t_ref, cot_t_ref, sems,
 ):
     batches = fetched_ref.shape[1]
-    slots = own_sel_ref.shape[1]
-    width = self_t_ref.shape[1]
-    hidden = self_t_ref.shape[0]
+    slots, nodes = own_sel_ref.shape[1:]
+    hidden, width = self_t_ref.shape
     seeds, classes = logits_ref.shape[1:]
-    nodes = own_sel_ref.shape[2]
+    loads = []
+
+    def load(source, target):
+        copy = pltpu.make_async_copy(source, target, sems.at[len(loads)])
+        loads.append(copy)
+        return copy
+
+    early = [
+        [load(source.at[b], target.at[b]) for b in range(batches)]
+        for source, target in (
+            (own_sel_hbm, own_sel_ref), (sum_sel_hbm, sum_sel_ref), (back_hbm, back_ref),
+        )
+    ]
+    scale = load(scale_hbm, scale_ref)
+    weights = [load(self_t_hbm, self_t_ref), load(neigh_t_hbm, neigh_t_ref)]
+    outer = [
+        load(outer_sel_hbm, outer_sel_ref), load(outer_scale_hbm, outer_scale_ref),
+        load(cot_t_hbm, cot_t_ref),
+    ]
+    early[0][0].start()
+    early[1][0].start()
+    scale.start()
+    for copy in weights:
+        copy.start()
     second[:, classes:, :] = jnp.zeros((2, second.shape[1] - classes, hidden), F32)
     for b in range(batches):
         here = slice(b * nodes, (b + 1) * nodes)
         table = fetched_ref[:, b].reshape(slots, width).T
-        own_t[:, here] = nn(table, own_sel_ref[b]).astype(BF)
-        mean_t[:, here] = (nn(table, sum_sel_ref[b]) * scale_ref[b]).astype(BF)
-        pre = nn(self_t_ref[...], own_t[:, here]) + nn(neigh_t_ref[...], mean_t[:, here])
+        early[0][b].wait()
+        own_t = nn(table, own_sel_ref[b]).astype(BF)
+        inputs_t[0, :, here] = own_t
+        if b == 0:
+            early[2][0].start()
+            for copy in outer:
+                copy.start()
+            scale.wait()
+        early[1][b].wait()
+        mean_t = (nn(table, sum_sel_ref[b]) * scale_ref[b]).astype(BF)
+        inputs_t[1, :, here] = mean_t
+        if b == 0:
+            for later in range(1, batches):
+                for copies in early:
+                    copies[later].start()
+            for copy in weights:
+                copy.wait()
+        pre = nn(self_t_ref[...], own_t) + nn(neigh_t_ref[...], mean_t)
         gate = 1.0 / (1.0 + jnp.exp(-pre))
         hidden_t = (pre * gate).astype(BF)
+        early[2][b].wait()
         back_t[:, here] = (back_ref[b] * (gate * (1.0 + pre * (1.0 - gate)))).astype(BF)
+        if b == 0:
+            for copy in outer:
+                copy.wait()
         outer_t = (nn(hidden_t, outer_sel_ref[b]) * outer_scale_ref[b]).astype(BF)
         seed_t = hidden_t[:, 0:seeds]
         logits_ref[b, :, :] = (nn(self_two_ref[...], seed_t) + nn(neigh_two_ref[...], outer_t)).T
@@ -204,13 +260,9 @@
         else:
             second[0, 0:classes, :] += self_grad
             second[1, 0:classes, :] += neigh_grad
-    first[0] = nt(own_t[...], back_t[...])
-    first[1] = nt(mean_t[...], back_t[...])
-    core = core_ref[0]
-    keep_ref[0:width, :] = first[core]
-    keep_ref[width:, :] = second[core]
-    send_ref[0:width, :] = first[1 - core].astype(BF)
-    send_ref[width:, :] = second[1 - core].astype(BF)
+    sent = 1 - core_ref[0]
+    send_ref[0:width, :] = nt(inputs_t[sent], back_t[...]).astype(BF)
+    send_ref[width:, :] = second[sent].astype(BF)
 
 
 def both_passes(core, fetched, planned, self_two, neigh_two, logit_shape):
@@ -223,22 +275,40 @@
         pass_kernel,
         out_shape=(
             struct(logit_shape, F32),
-            struct((width + tail, hidden), F32),
             struct((width + tail, hidden), BF),
+            struct((2, width, batches * nodes), BF),
+            struct((hidden, batches * nodes), BF),
+            struct((2, tail, hidden), F32),
         ),
-        in_specs=[SMEM] + [VMEM] * 12,
-        out_specs=[VMEM] * 3,
-        scratch_shapes=[
-            pltpu.VMEM((width, batches * nodes), BF),
-            pltpu.VMEM((width, batches * nodes), BF),
-            pltpu.VMEM((hidden, batches * nodes), BF),
-            pltpu.VMEM((2, width, hidden), F32),
-            pltpu.VMEM((2, tail, hidden), F32),
-        ],
-        compiler_params=params(32),
-        cost_estimate=cost(6_000_000_000, 20_000_000),
+        in_specs=[SMEM, VMEM] + [ANY] * len(planned) + [VMEM] * 2,
+        out_specs=[VMEM] * 5,
+        scratch_shapes=[pltpu.VMEM(value.shape, value.dtype) for value in planned]
+        + [pltpu.SemaphoreType.DMA((len(planned) + 3 * (batches - 1),))],
+        compiler_params=params(40),
+        cost_estimate=cost(4_500_000_000, 20_000_000),
         name="both_passes",
-    )(core, fetched, *planned, self_two, neigh_two)
+    )(core, fetched, *[in_hbm(value) for value in planned], self_two, neigh_two)
+
+
+def keep_kernel(core_ref, inputs_t, back_t, second, keep_ref):
+    core = core_ref[0]
+    width = inputs_t.shape[1]
+    keep_ref[0:width, :] = nt(inputs_t[core], back_t[...])
+    keep_ref[width:, :] = second[core]
+
+
+def keep_half(core, inputs_t, back_t, second):
+    width, nodes = inputs_t.shape[1:]
+    tail, hidden = second.shape[1:]
+    return pl.pallas_call(
+        keep_kernel,
+        out_shape=struct((width + tail, hidden), F32),
+        in_specs=[SMEM] + [VMEM] * 3,
+        out_specs=VMEM,
+        compiler_params=params(16),
+        cost_estimate=cost(2 * width * hidden * nodes, 5_000_000),
+        name="keep_half",
+    )(core, inputs_t, back_t, second)
 
 
 def add_kernel(keep_ref, got_ref, out_ref):
@@ -296,52 +366,51 @@
     )(own, *got)
 
 
-def unpack_kernel(
-    core_ref, mine_ref, other_ref, mine_tail_ref, other_tail_ref,
-    self_one_ref, neigh_one_ref, self_two_ref, neigh_two_ref,
-):
-    classes = self_two_ref.shape[0]
-
-    def place(mine, other, mine_tail, other_tail):
-        mine[...] = mine_ref[...].astype(F32)
-        other[...] = other_ref[...].astype(F32)
-
-        @pl.when(pl.program_id(0) == 0)
-        def _():
-            mine_tail[...] = mine_tail_ref[0:classes, :].astype(F32)
-            other_tail[...] = other_tail_ref[0:classes, :].astype(F32)
-
-    @pl.when(core_ref[0] == 0)
+def unpack_kernel(slot_ref, half_ref, *refs):
+    self_one, neigh_one, self_two, neigh_two, head, tail, sems = refs[-7:]
+    width = head.shape[0]
+    classes = tail.shape[0]
+    parts = sems.shape[0] - 1
+    block = width // parts
+
+    def place(one, two):
+        copies = []
+        for i in range(parts):
+            here = slice(i * block, (i + 1) * block)
+            head[here, :] = half_ref[here, :].astype(F32)
+            copies.append(pltpu.make_async_copy(head.at[here], one.at[here], sems.at[i]))
+            copies[-1].start()
+        tail[...] = half_ref[width : width + classes, :].astype(F32)
+        copies.append(pltpu.make_async_copy(tail, two, sems.at[parts]))
+        copies[-1].start()
+        for copy in copies:
+            copy.wait()
+
+    @pl.when(slot_ref[0] == 0)
     def _():
-        place(self_one_ref, neigh_one_ref, self_two_ref, neigh_two_ref)
-
-    @pl.when(core_ref[0] != 0)
+        place(self_one, self_two)
+
+    @pl.when(slot_ref[0] != 0)
     def _():
-        place(neigh_one_ref, self_one_ref, neigh_two_ref, self_two_ref)
-
-
-def unpack(core, mine, other, one_shape, two_shape):
-    width, hidden = one_shape
-    tail = mine.shape[0] - width
-    steps = 4
-    head = pl.BlockSpec((width // steps, hidden), lambda i: (i, 0))
-    last = pl.BlockSpec((tail, hidden), lambda i: (width // tail, 0))
-    two = pl.BlockSpec(two_shape, lambda i: (0, 0))
+        place(neigh_one, neigh_two)
+
+
+def unpack(slot, half, one_shape, two_shape, placed=()):
     return pl.pallas_call(
         unpack_kernel,
-        out_shape=(
-            struct(one_shape, F32),
-            struct(one_shape, F32),
-            struct(two_shape, F32),
-            struct(two_shape, F32),
-        ),
-        grid=(steps,),
-        in_specs=[SMEM, head, head, last, last],
-        out_specs=[head, head, two, two],
-        compiler_params=params(8),
-        cost_estimate=cost(mine.size, mine.size * 12),
+        out_shape=tuple(pltpu.HBM(shape, F32) for shape in (one_shape,) * 2 + (two_shape,) * 2),
+        in_specs=[SMEM, VMEM] + [ANY] * len(placed),
+        out_specs=[ANY] * 4,
+        scratch_shapes=[
+            pltpu.VMEM(one_shape, F32),
+            pltpu.VMEM(two_shape, F32),
+            pltpu.SemaphoreType.DMA((5,)),
+        ],
+        input_output_aliases={2 + i: i for i in range(len(placed))},
+        compiler_params=params(5),
+        cost_estimate=cost(half.size, half.size * 6),
         name="unpack",
-    )(core, mine, other, mine, other)
+    )(slot, half, *[in_hbm(value) for value in placed])
 
 
 def exchange(value, axes):
@@ -361,7 +430,6 @@
     core = lax.axis_index("core").reshape(1).astype(jnp.int32)
     wanted = request_rows[:, 0].transpose(1, 0, 2).reshape(owners, batches * capacity)
     asked = exchange(wanted, ("chip", "core"))
-    wide = widen(features)
     planned = plan(
         bucket_counts[:, 0],
         layer_targets,
@@ -374,12 +442,13 @@
         self_two.T,
         neigh_two.T,
     )
-    rows = serve(asked, wide, width)
+    rows = serve(asked, features)
     fetched = exchange(rows.reshape(owners, batches, capacity, width), ("chip", "core"))
-    logits, keep, send = both_passes(
+    logits, send, inputs_t, back_t, second = both_passes(
         core, fetched, planned, self_two.T, neigh_two.T, cotangent.shape
     )
-    half = add_pair(keep, swap_cores(send))
+    got = swap_cores(send)
+    half = add_pair(keep_half(core, inputs_t, back_t, second), got)
     plane = ("chip", "near")
     parties = lax.axis_size(plane)
     far = lax.axis_size("far")
@@ -390,7 +459,9 @@
         for shift in range(1, far)
     ]
     mine = exchange(total_copies(own, got, parties), plane).reshape(half.shape)
-    grads = unpack(core, mine, swap_cores(mine), self_one.shape, self_two.T.shape)
+    other = swap_cores(mine)
+    shapes = (self_one.shape, self_two.T.shape)
+    grads = unpack(1 - core, other, *shapes, unpack(core, mine, *shapes))
     return (logits, grads[0], grads[1], grads[2].T, grads[3].T)
 
 

time: 143 us -> 123 us (0.86)
  local copies, waits for them, and re-layouts: 33 us -> 5.2 us
  blocking collectives: 39 us -> 54.3 us
  starting transfers between devices: 32.1 us -> 20.5 us
  Pallas kernels: 21.5 us -> 25.9 us
    unnamed x56 -> x18, local copies, waits for them, and re-layouts: 31.6 us -> 4.41 us
    all_to_all x2 -> x3, blocking collectives: 39 us -> 54.3 us  [exchange(): return lax.all_to_all(value, axes, split_axis=0, concat_axis=0, tiled=True)]
    all_to_all x2 -> x1, starting transfers between devices: 16.1 us -> 4.42 us  [exchange(): return lax.all_to_all(value, axes, split_axis=0, concat_axis=0, tiled=True)]
    pallas_call x1, Pallas kernels: 3.93 us -> 6.86 us  [serve(): pl.pallas_call(serve_kernel, out_shape=struct((count, width), BF), in_spe...]
    ppermute x2, waiting for transfers between devices: 4.57 us -> 2.24 us  [swap_cores(): return lax.ppermute(value, 'core', [(0, 1), (1, 0)])]
    all_to_all x2 -> x1, waiting for transfers between devices: 9.49 us -> 11.7 us  [exchange(): return lax.all_to_all(value, axes, split_axis=0, concat_axis=0, tiled=True)]
    pallas_call x1, Pallas kernels: 7.36 us -> 8.79 us  [both_passes(): pl.pallas_call(pass_kernel, out_shape=(struct(logit_shape, F32), struct((...]
    pallas_call x3 -> x4, Pallas kernels: 9.79 us -> 9.8 us  [the longest x1 6.17 us: plan(): pl.pallas_call(plan_kernel, out_shape=(pltpu.HBM((batches, slots, nodes),...]
  transfers between devices with their start and end apart: 7 -> 6, of which waited for: 5 -> 5; matrix products, arithmetic and copies ran while one was open for 1% -> 1% of each run, Pallas kernels for 5% -> 7%
where the time goes in v3:
time: 123 us
  blocking collectives  54.3 us (44%)
  Pallas kernels  25.9 us (21%)
  starting transfers between devices  20.5 us (17%)
  waiting for transfers between devices  15.9 us (13%)
  local copies, waits for them, and re-layouts  5.2 us (4%)
    all_to_all x3, blocking collectives, exchange(): return lax.all_to_all(value, axes, split_axis=0, concat_axis=0, tiled=True)  54.3 us
    all_to_all x1, waiting for transfers between devices, exchange(): return lax.all_to_all(value, axes, split_axis=0, concat_axis=0, tiled=True)  11.7 us
    ppermute x3, starting transfers between devices, body(): lax.ppermute(own, 'far', [(i, (i + shift) % far) for i in range(far)])  9.65 us
    pallas_call x1, Pallas kernels, both_passes(): pl.pallas_call(pass_kernel, out_shape=(struct(logit_shape, F32), struct((...  8.79 us
    pallas_call x1, Pallas kernels, serve(): pl.pallas_call(serve_kernel, out_shape=struct((count, width), BF), in_spe...  6.86 us
    ppermute x2, starting transfers between devices, swap_cores(): return lax.ppermute(value, 'core', [(0, 1), (1, 0)])  6.43 us
    pallas_call x1, Pallas kernels, plan(): pl.pallas_call(plan_kernel, out_shape=(pltpu.HBM((batches, slots, nodes),...  6.17 us
    all_to_all x1, starting transfers between devices, exchange(): return lax.all_to_all(value, axes, split_axis=0, concat_axis=0, tiled=True)  4.42 us
  transfers between devices with their start and end apart: 6, of which 5 were waited for; matrix products, arithmetic and copies ran while one was open for 1% of the time, Pallas kernels for 7%

profile of v3, /device:TPU:1, one launch (start us, length us, event | category | flops | bytes accessed | tf_op | source)
XLA Modules:
  0.0 122.7 jit_solution(1993268921792752181)
XLA Ops:
  0.6 0.8 copy.27
  1.4 15.3 %all_to_all.26 = s32[32,1,32]{2,1,0:T(1,128)S(1)} all-to-all(s32[32,1,32]{2,1,0:T(1,128)S(1)} %copy.27), channel_id=1, replica_groups=mesh['chip'=16,'core'=2,'far'=4,'near'=2] {'chip','core'}, dimensions={0} | all-to-all | bytes 8192 | tf_op jit(solution)/shard_map/all_to_all | solution.py:417
  16.7 6.9 %serve.1 = bf16[1024,768]{1,0:T(8,128)(2,1)} custom-call(s32[32,32]{1,0:T(8,128)S(1)} %bitcast.30, bf16[4096,768]{1,0:T(8,128)(2,1)} %rows_ref.1), custom_call_target="tpu_custom_call" | custom-call | flops 786432 | bytes 18874368 | tf_op jit(solution)/shard_map/serve/pallas_call | solution.py:172
  23.6 0.0 copy-start
  23.6 0.0 copy-start.1
  23.6 0.0 copy-start.2
  23.6 0.0 copy-start.3
  23.7 4.4 %all-to-all-start.1 = ((bf16[32,2,16,768]{3,2,1,0:T(8,128)(2,1)}), bf16[32,2,16,768]{3,2,1,0:T(8,128)(2,1)S(1)}, u32[]{:S(2)}, u32[]{:S(2)}) async-start(bf16[32,2,16,768]{3,2,1,0:T(8,128)(2,1)} %bitcast.5), calls=%async_computation.1 | async-start | bytes 3145728 | tf_op jit(solution)/shard_map/all_to_all | solution.py:417
  28.1 0.8 copy.32
  28.9 0.7 copy.33
  29.6 0.0 copy-done
  29.6 0.0 copy-done.1
  29.6 0.0 copy-done.2
  29.6 0.0 copy-done.3
  29.6 0.0 copy-start.4
  29.6 0.8 copy-done.4
  30.5 0.0 copy-start.5
  30.5 0.7 copy-done.5
  31.2 0.0 copy-start.6
  31.2 0.7 copy-done.6
  31.8 0.0 copy-start.7
  31.8 0.7 copy-done.7
  32.5 6.2 %plan.1 = (bf16[2,512,512]{2,1,0:T(8,128)(2,1)}, bf16[2,512,512]{2,1,0:T(8,128)(2,1)}, f32[2,1,512]{2,1,0:T(1,128)}, bf16[2,512,64]{2,1,0:T(8,128)(2,1)}, f32[2,...) custom-call(s32[2,32]{1,0:T(2,128)S(1)} %bitcast.31, ...), custom_call_target="tpu_custom_call" | custom-call | flops 200000000 | bytes 10000000 | tf_op jit(solution)/shard_map/plan/pallas_call | solution.py:106
  38.7 11.7 %all-to-all-done.1.fetched_ref = bf16[32,2,16,768]{3,2,1,0:T(8,128)(2,1)S(1)} async-done(((bf16[32,2,16,768]{3,2,1,0:T(8,128)(2,1)}), bf16[32,2,16,768]{3,2,1,0:T(8,128)(2,1)S(1)}, u32[]{:S(2)}, u32[]{:S(2)}) %all-to-all-start.1) | async-done | bytes 1572896 | tf_op jit(solution)/shard_map/all_to_all | solution.py:417
  50.4 8.8 %both_passes.1 = (f32[2,64,153]{2,1,0:T(8,128)}, bf16[1024,512]{1,0:T(8,128)(2,1)S(1)}, bf16[2,768,1024]{2,1,0:T(8,128)(2,1)S(1)}, bf16[512,1024]{1,0:T(8,128)(2,1)S(1)}, f32[2,256,512]{2,1,0:T(8,128)S(1)}) custom-call(s32[1]{0:T(128)} %bitcast.core_ref.slot_ref, bf16[32,2,16,768]{3,2,1,0:T(8,128)(2,1)S(1)} %all-to-all-done.1.fetched_ref, ...), custom_call_target="tpu_custom_call" | custom-call | flops 4499999744 | bytes 20000000 | tf_op jit(solution)/shard_map/both_passes/pallas_call | solution.py:274
  59.2 2.3 %collective-permute-start = (bf16[1024,512]{1,0:T(8,128)(2,1)S(1)}, bf16[1024,512]{1,0:T(8,128)(2,1)S(1)}, u32[]{:S(2)}, u32[]{:S(2)}) collective-permute-start(bf16[1024,512]{1,0:T(8,128)(2,1)S(1)} %get-tuple-element.40), channel_id=1, source_target_pairs={{0,8},{8,0},{1,9},{9,1},{2,10},{10,2},{3,11},{11,3},{4,12},{12,4},... | collective-permute-start | bytes 3145736 | tf_op jit(solution)/shard_map/ppermute | solution.py:421
  61.4 1.0 keep_half.1.keep_ref
  62.5 1.3 %collective-permute-done.got_ref = bf16[1024,512]{1,0:T(8,128)(2,1)S(1)} collective-permute-done((bf16[1024,512]{1,0:T(8,128)(2,1)S(1)}, bf16[1024,512]{1,0:T(8,128)(2,1)S(1)}, u32[]{:S(2)}, u32[]{:S(2)}) %collective-permute-start) | collective-permute-done | bytes 1048608 | tf_op jit(solution)/shard_map/ppermute | solution.py:421
  63.7 0.2 add_pair.1
  63.9 21.2 %all_to_all.27.parts_ref = bf16[32,32,512]{2,1,0:T(8,128)(2,1)S(1)} all-to-all(bf16[32,32,512]{2,1,0:T(8,128)(2,1)S(1)} %bitcast.23), channel_id=1, replica_groups=mesh['chip'=16,'core'=2,'far'=4,'near'=2] {'chip','near'}, dimensions={0} | all-to-all | bytes 2097152 | tf_op jit(solution)/shard_map/all_to_all | solution.py:417
  85.1 0.1 sum_parts.1.own_ref
  85.3 3.1 %collective-permute-start.1 = (bf16[32,512]{1,0:T(8,128)(2,1)S(1)}, bf16[32,512]{1,0:T(8,128)(2,1)S(1)}, u32[]{:S(2)}, u32[]{:S(2)}) collective-permute-start(bf16[32,512]{1,0:T(8,128)(2,1)S(1)} %sum_parts.1.own_ref), channel_id=1, source_target_pairs={{0,2},{2,4},{4,6},{6,0},{1,3},{3,5},{5,7},{7,1},{8,10},{10,12},{12... | collective-permute-start | bytes 98312 | tf_op jit(solution)/shard_map/ppermute | solution.py:458
  88.3 4.2 %collective-permute-start.2 = (bf16[32,512]{1,0:T(8,128)(2,1)S(1)}, bf16[32,512]{1,0:T(8,128)(2,1)S(1)}, u32[]{:S(2)}, u32[]{:S(2)}) collective-permute-start(bf16[32,512]{1,0:T(8,128)(2,1)S(1)} %sum_parts.1.own_ref), channel_id=1, source_target_pairs={{0,4},{2,6},{4,0},{6,2},{1,5},{3,7},{5,1},{7,3},{8,12},{10,14},{12... | collective-permute-start | bytes 98312 | tf_op jit(solution)/shard_map/ppermute | solution.py:458
  92.5 2.4 %collective-permute-start.3 = (bf16[32,512]{1,0:T(8,128)(2,1)S(1)}, bf16[32,512]{1,0:T(8,128)(2,1)S(1)}, u32[]{:S(2)}, u32[]{:S(2)}) collective-permute-start(bf16[32,512]{1,0:T(8,128)(2,1)S(1)} %sum_parts.1.own_ref), channel_id=1, source_target_pairs={{0,6},{2,0},{4,2},{6,4},{1,7},{3,1},{5,3},{7,5},{8,14},{10,8},{12,... | collective-permute-start | bytes 98312 | tf_op jit(solution)/shard_map/ppermute | solution.py:458
  94.9 0.0 collective-permute-done.1.next_ref
  94.9 0.4 collective-permute-done.2.across_ref
  95.3 1.6 %collective-permute-done.3.last_ref = bf16[32,512]{1,0:T(8,128)(2,1)S(1)} collective-permute-done((bf16[32,512]{1,0:T(8,128)(2,1)S(1)}, bf16[32,512]{1,0:T(8,128)(2,1)S(1)}, u32[]{:S(2)}, u32[]{:S(2)}) %collective-permute-start.3) | collective-permute-done | bytes 32800 | tf_op jit(solution)/shard_map/ppermute | solution.py:458
  96.9 0.1 total_copies.1
  97.1 17.7 %all_to_all.28 = bf16[32,32,512]{2,1,0:T(8,128)(2,1)S(1)} all-to-all(bf16[32,32,512]{2,1,0:T(8,128)(2,1)S(1)} %total_copies.1), channel_id=1, replica_groups=mesh['chip'=16,'core'=2,'far'=4,'near'=2] {'chip','near'}, dimensions={0} | all-to-all | bytes 2097152 | tf_op jit(solution)/shard_map/all_to_all | solution.py:417
  114.8 4.1 %collective-permute-start.4 = (bf16[1024,512]{1,0:T(8,128)(2,1)S(1)}, bf16[1024,512]{1,0:T(8,128)(2,1)S(1)}, u32[]{:S(2)}, u32[]{:S(2)}) collective-permute-start(bf16[1024,512]{1,0:T(8,128)(2,1)S(1)} %bitcast.21), channel_id=1, source_target_pairs={{0,8},{8,0},{1,9},{9,1},{2,10},{10,2},{3,11},{11,3},{4,12},{12,4},... | collective-permute-start | bytes 3145736 | tf_op jit(solution)/shard_map/ppermute | solution.py:421
  119.0 1.3 %unpack.2 = (f32[768,512]{1,0:T(8,128)}, f32[768,512]{1,0:T(8,128)}, f32[153,512]{1,0:T(8,128)}, f32[153,512]{1,0:T(8,128)}) custom-call(s32[1]{0:T(128)} %bitcast.core_ref.slot_ref, bf16[1024,512]{1,0:T(8,128)(2,1)S(1)} %bitcast.22), custom_call_target="tpu_custom_call" | custom-call | flops 524288 | bytes 3145728 | tf_op jit(solution)/shard_map/unpack/pallas_call | solution.py:399
  120.3 1.0 collective-permute-done.4.half_ref
  121.2 1.3 %unpack.3 = (f32[768,512]{1,0:T(8,128)}, f32[768,512]{1,0:T(8,128)}, f32[153,512]{1,0:T(8,128)}, f32[153,512]{1,0:T(8,128)}) custom-call(s32[1]{0:T(128)S(6)} %sub.3.slot_ref, bf16[1024,512]{1,0:T(8,128)(2,1)S(1)} %collective-permute-done.4.half_ref, ...), custom_call_target="tpu_custom_call", output_to_operand_aliasing={{0}: (2, {}), {1}: (3, {}), {2}: (4, {}), {3}: (5, {})} | custom-call | flops 524288 | bytes 3145728 | tf_op jit(solution)/shard_map/unpack/pallas_call | solution.py:399
Async XLA Ops:
  23.6 6.0 %copy-start = (bf16[768,512]{1,0:T(8,128)(2,1)S(1)}, bf16[768,512]{1,0:T(8,128)(2,1)}, u32[]{:S(2)}) copy-start(bf16[768,512]{1,0:T(8,128)(2,1)} %self_one_ref.1) | copy-start | bytes 2359300
  23.6 6.0 %copy-start.1 = (bf16[768,512]{1,0:T(8,128)(2,1)S(1)}, bf16[768,512]{1,0:T(8,128)(2,1)}, u32[]{:S(2)}) copy-start(bf16[768,512]{1,0:T(8,128)(2,1)} %neigh_one_ref.1) | copy-start | bytes 2359300
  23.6 6.0 %copy-start.2 = (bf16[512,153]{0,1:T(8,128)(2,1)S(1)}, bf16[512,153]{0,1:T(8,128)(2,1)}, u32[]{:S(2)}) copy-start(bf16[512,153]{0,1:T(8,128)(2,1)} %param.15) | copy-start | bytes 470020
  23.6 6.0 %copy-start.3 = (bf16[512,153]{0,1:T(8,128)(2,1)S(1)}, bf16[512,153]{0,1:T(8,128)(2,1)}, u32[]{:S(2)}) copy-start(bf16[512,153]{0,1:T(8,128)(2,1)} %param.16) | copy-start | bytes 470020
  23.7 26.7 %all-to-all-start.1 = ((bf16[32,2,16,768]{3,2,1,0:T(8,128)(2,1)}), bf16[32,2,16,768]{3,2,1,0:T(8,128)(2,1)S(1)}, u32[]{:S(2)}, u32[]{:S(2)}) async-start(bf16[32,2,16,768]{3,2,1,0:T(8,128)(2,1)} %bitcast.5), calls=%async_computation.1 | async-start | bytes 3145728 | tf_op jit(solution)/shard_map/all_to_all | solution.py:417
  29.6 0.8 copy-start.4
  30.5 0.7 copy-start.5
  31.2 0.7 copy-start.6
  31.8 0.7 copy-start.7
  59.2 4.6 %collective-permute-start = (bf16[1024,512]{1,0:T(8,128)(2,1)S(1)}, bf16[1024,512]{1,0:T(8,128)(2,1)S(1)}, u32[]{:S(2)}, u32[]{:S(2)}) collective-permute-start(bf16[1024,512]{1,0:T(8,128)(2,1)S(1)} %get-tuple-element.40), channel_id=1, source_target_pairs={{0,8},{8,0},{1,9},{9,1},{2,10},{10,2},{3,11},{11,3},{4,12},{12,4},... | collective-permute-start | bytes 3145736 | tf_op jit(solution)/shard_map/ppermute | solution.py:421
  85.3 9.7 %collective-permute-start.1 = (bf16[32,512]{1,0:T(8,128)(2,1)S(1)}, bf16[32,512]{1,0:T(8,128)(2,1)S(1)}, u32[]{:S(2)}, u32[]{:S(2)}) collective-permute-start(bf16[32,512]{1,0:T(8,128)(2,1)S(1)} %sum_parts.1.own_ref), channel_id=1, source_target_pairs={{0,2},{2,4},{4,6},{6,0},{1,3},{3,5},{5,7},{7,1},{8,10},{10,12},{12... | collective-permute-start | bytes 98312 | tf_op jit(solution)/shard_map/ppermute | solution.py:458
  88.3 7.0 %collective-permute-start.2 = (bf16[32,512]{1,0:T(8,128)(2,1)S(1)}, bf16[32,512]{1,0:T(8,128)(2,1)S(1)}, u32[]{:S(2)}, u32[]{:S(2)}) collective-permute-start(bf16[32,512]{1,0:T(8,128)(2,1)S(1)} %sum_parts.1.own_ref), channel_id=1, source_target_pairs={{0,4},{2,6},{4,0},{6,2},{1,5},{3,7},{5,1},{7,3},{8,12},{10,14},{12... | collective-permute-start | bytes 98312 | tf_op jit(solution)/shard_map/ppermute | solution.py:458
  92.5 4.4 %collective-permute-start.3 = (bf16[32,512]{1,0:T(8,128)(2,1)S(1)}, bf16[32,512]{1,0:T(8,128)(2,1)S(1)}, u32[]{:S(2)}, u32[]{:S(2)}) collective-permute-start(bf16[32,512]{1,0:T(8,128)(2,1)S(1)} %sum_parts.1.own_ref), channel_id=1, source_target_pairs={{0,6},{2,0},{4,2},{6,4},{1,7},{3,1},{5,3},{7,5},{8,14},{10,8},{12,... | collective-permute-start | bytes 98312 | tf_op jit(solution)/shard_map/ppermute | solution.py:458
  114.8 6.4 %collective-permute-start.4 = (bf16[1024,512]{1,0:T(8,128)(2,1)S(1)}, bf16[1024,512]{1,0:T(8,128)(2,1)S(1)}, u32[]{:S(2)}, u32[]{:S(2)}) collective-permute-start(bf16[1024,512]{1,0:T(8,128)(2,1)S(1)} %bitcast.21), channel_id=1, source_target_pairs={{0,8},{8,0},{1,9},{9,1},{2,10},{10,2},{3,11},{11,3},{4,12},{12,4},... | collective-permute-start | bytes 3145736 | tf_op jit(solution)/shard_map/ppermute | solution.py:421

commit v4 on v3

--- a/solution.py
+++ b/solution.py
@@ -124,7 +124,7 @@
     )(counts, targets, inner, outer, degree, cot, self_one, neigh_one, self_two, neigh_two)
 
 
-def serve_kernel(asked_ref, rows_ref, out_ref, landed, wide, sems):
+def serve_kernel(asked_ref, rows_ref, out_ref, landed, wide, found, sems, out_sems):
     askers, each = asked_ref.shape
     rows, width = rows_ref.shape
     chunks = sems.shape[0]
@@ -159,10 +159,19 @@
             target = pl.ds(pl.multiple_of(p * each + first, 2 * SUBLANES), 2 * SUBLANES)
             for j in range(pieces):
                 pair = jnp.concatenate([tiles[j], tiles[pieces + j]], axis=0)
-                out_ref[target, j * LANES : (j + 1) * LANES] = pair.astype(BF)
+                found[target, j * LANES : (j + 1) * LANES] = pair.astype(BF)
         return carry
 
-    lax.fori_loop(0, askers, one_asker, 0)
+    parts = out_sems.shape[0]
+    count = askers // parts
+    stores = []
+    for part in range(parts):
+        lax.fori_loop(part * count, (part + 1) * count, one_asker, 0)
+        here = pl.ds(part * count * each, count * each)
+        stores.append(pltpu.make_async_copy(found.at[here, :], out_ref.at[here, :], out_sems.at[part]))
+        stores[-1].start()
+    for store in stores:
+        store.wait()
 
 
 def serve(asked, features):
@@ -171,13 +180,15 @@
     chunks = 8
     return pl.pallas_call(
         serve_kernel,
-        out_shape=struct((count, width), BF),
+        out_shape=pltpu.HBM((count, width), BF),
         in_specs=[SMEM, ANY],
-        out_specs=VMEM,
+        out_specs=ANY,
         scratch_shapes=[
             pltpu.VMEM((rows, width), BF),
             pltpu.VMEM((width // LANES, rows + 2 * SUBLANES, LANES), F32),
+            pltpu.VMEM((count, width), BF),
             pltpu.SemaphoreType.DMA((chunks,)),
+            pltpu.SemaphoreType.DMA((4,)),
         ],
         compiler_params=params(28),
         cost_estimate=cost(count * width, rows * width * 6),
@@ -190,65 +201,59 @@
     back_hbm, self_t_hbm, neigh_t_hbm, cot_t_hbm, self_two_ref, neigh_two_ref,
     logits_ref, send_ref, inputs_t, back_t, second,
     own_sel_ref, sum_sel_ref, scale_ref, outer_sel_ref, outer_scale_ref, back_ref,
-    self_t_ref, neigh_t_ref, cot_t_ref, sems,
+    self_t_ref, neigh_t_ref, cot_t_ref, table_t, sems,
 ):
     batches = fetched_ref.shape[1]
     slots, nodes = own_sel_ref.shape[1:]
     hidden, width = self_t_ref.shape
     seeds, classes = logits_ref.shape[1:]
-    loads = []
-
-    def load(source, target):
-        copy = pltpu.make_async_copy(source, target, sems.at[len(loads)])
-        loads.append(copy)
-        return copy
-
-    early = [
-        [load(source.at[b], target.at[b]) for b in range(batches)]
-        for source, target in (
-            (own_sel_hbm, own_sel_ref), (sum_sel_hbm, sum_sel_ref), (back_hbm, back_ref),
-        )
+    pairs = (
+        (own_sel_hbm, own_sel_ref), (sum_sel_hbm, sum_sel_ref), (back_hbm, back_ref),
+        (scale_hbm, scale_ref), (self_t_hbm, self_t_ref), (neigh_t_hbm, neigh_t_ref),
+        (outer_sel_hbm, outer_sel_ref), (outer_scale_hbm, outer_scale_ref),
+        (cot_t_hbm, cot_t_ref),
+    )
+    split = [
+        (source.at[b], target.at[b]) for b in range(batches) for source, target in pairs[:3]
     ]
-    scale = load(scale_hbm, scale_ref)
-    weights = [load(self_t_hbm, self_t_ref), load(neigh_t_hbm, neigh_t_ref)]
-    outer = [
-        load(outer_sel_hbm, outer_sel_ref), load(outer_scale_hbm, outer_scale_ref),
-        load(cot_t_hbm, cot_t_ref),
+    loads = [
+        pltpu.make_async_copy(source, target, sems.at[i])
+        for i, (source, target) in enumerate(split + list(pairs[3:]))
     ]
-    early[0][0].start()
-    early[1][0].start()
-    scale.start()
-    for copy in weights:
+    count = len(split)
+    first = loads[0:2] + loads[count : count + 3]
+    rest = loads[2:count] + loads[count + 3 :]
+    for copy in first + rest:
         copy.start()
     second[:, classes:, :] = jnp.zeros((2, second.shape[1] - classes, hidden), F32)
     for b in range(batches):
-        here = slice(b * nodes, (b + 1) * nodes)
-        table = fetched_ref[:, b].reshape(slots, width).T
-        early[0][b].wait()
-        own_t = nn(table, own_sel_ref[b]).astype(BF)
-        inputs_t[0, :, here] = own_t
+        table_t[b] = fetched_ref[:, b].reshape(slots, width).T
+
+    def inputs(b):
         if b == 0:
-            early[2][0].start()
-            for copy in outer:
-                copy.start()
-            scale.wait()
-        early[1][b].wait()
-        mean_t = (nn(table, sum_sel_ref[b]) * scale_ref[b]).astype(BF)
-        inputs_t[1, :, here] = mean_t
+            first[0].wait()
+        own_t = nn(table_t[b], own_sel_ref[b]).astype(BF)
         if b == 0:
-            for later in range(1, batches):
-                for copies in early:
-                    copies[later].start()
-            for copy in weights:
-                copy.wait()
-        pre = nn(self_t_ref[...], own_t) + nn(neigh_t_ref[...], mean_t)
+            first[1].wait()
+            first[2].wait()
+        mean_t = (nn(table_t[b], sum_sel_ref[b]) * scale_ref[b]).astype(BF)
+        inputs_t[0, :, b * nodes : (b + 1) * nodes] = own_t
+        inputs_t[1, :, b * nodes : (b + 1) * nodes] = mean_t
+        if b == 0:
+            first[3].wait()
+            first[4].wait()
+        return nn(self_t_ref[...], own_t) + nn(neigh_t_ref[...], mean_t)
+
+    pre = inputs(0)
+    for copy in rest:
+        copy.wait()
+    for b in range(batches):
+        if b > 0:
+            pre = inputs(b)
         gate = 1.0 / (1.0 + jnp.exp(-pre))
         hidden_t = (pre * gate).astype(BF)
-        early[2][b].wait()
-        back_t[:, here] = (back_ref[b] * (gate * (1.0 + pre * (1.0 - gate)))).astype(BF)
-        if b == 0:
-            for copy in outer:
-                copy.wait()
+        slope = back_ref[b] * (gate * (1.0 + pre * (1.0 - gate)))
+        back_t[:, b * nodes : (b + 1) * nodes] = slope.astype(BF)
         outer_t = (nn(hidden_t, outer_sel_ref[b]) * outer_scale_ref[b]).astype(BF)
         seed_t = hidden_t[:, 0:seeds]
         logits_ref[b, :, :] = (nn(self_two_ref[...], seed_t) + nn(neigh_two_ref[...], outer_t)).T
@@ -265,17 +270,17 @@
     send_ref[width:, :] = second[sent].astype(BF)
 
 
-def both_passes(core, fetched, planned, self_two, neigh_two, logit_shape):
+def both_passes(core, fetched, planned, self_two, neigh_two, logit_shape, half_rows):
     batches = fetched.shape[1]
     width = fetched.shape[3]
     hidden = self_two.shape[1]
     nodes = planned[0].shape[2]
-    tail = hidden // 2
+    tail = half_rows - width
     return pl.pallas_call(
         pass_kernel,
         out_shape=(
             struct(logit_shape, F32),
-            struct((width + tail, hidden), BF),
+            struct((half_rows, hidden), BF),
             struct((2, width, batches * nodes), BF),
             struct((hidden, batches * nodes), BF),
             struct((2, tail, hidden), F32),
@@ -283,7 +288,10 @@
         in_specs=[SMEM, VMEM] + [ANY] * len(planned) + [VMEM] * 2,
         out_specs=[VMEM] * 5,
         scratch_shapes=[pltpu.VMEM(value.shape, value.dtype) for value in planned]
-        + [pltpu.SemaphoreType.DMA((len(planned) + 3 * (batches - 1),))],
+        + [
+            pltpu.VMEM((batches, width, nodes), BF),
+            pltpu.SemaphoreType.DMA((len(planned) + 3 * (batches - 1),)),
+        ],
         compiler_params=params(40),
         cost_estimate=cost(4_500_000_000, 20_000_000),
         name="both_passes",
@@ -312,13 +320,15 @@
 
 
 def add_kernel(keep_ref, got_ref, out_ref):
-    out_ref[...] = (keep_ref[...] + got_ref[...].astype(F32)).astype(BF)
+    total = (keep_ref[...] + got_ref[...].astype(F32)).astype(BF)
+    for j in range(out_ref.shape[0]):
+        out_ref[j] = total[:, j * LANES : (j + 1) * LANES]
 
 
 def add_pair(keep, got):
     return pl.pallas_call(
         add_kernel,
-        out_shape=struct(keep.shape, BF),
+        out_shape=struct((keep.shape[1] // LANES, keep.shape[0], LANES), BF),
         in_specs=[VMEM] * 2,
         out_specs=VMEM,
         compiler_params=params(6),
@@ -372,15 +382,19 @@
     classes = tail.shape[0]
     parts = sems.shape[0] - 1
     block = width // parts
+    columns = half_ref.shape[0]
 
     def place(one, two):
         copies = []
         for i in range(parts):
             here = slice(i * block, (i + 1) * block)
-            head[here, :] = half_ref[here, :].astype(F32)
+            for j in range(columns):
+                head[here, j * LANES : (j + 1) * LANES] = half_ref[j, here, :].astype(F32)
             copies.append(pltpu.make_async_copy(head.at[here], one.at[here], sems.at[i]))
             copies[-1].start()
-        tail[...] = half_ref[width : width + classes, :].astype(F32)
+        for j in range(columns):
+            piece = half_ref[j, width : width + classes, :].astype(F32)
+            tail[:, j * LANES : (j + 1) * LANES] = piece
         copies.append(pltpu.make_async_copy(tail, two, sems.at[parts]))
         copies[-1].start()
         for copy in copies:
@@ -444,16 +458,17 @@
     )
     rows = serve(asked, features)
     fetched = exchange(rows.reshape(owners, batches, capacity, width), ("chip", "core"))
+    plane = ("chip", "near")
+    parties = lax.axis_size(plane)
+    far = lax.axis_size("far")
+    unit = parties * SUBLANES * LANES // hidden
+    half_rows = -(-(width + cotangent.shape[2]) // unit) * unit
     logits, send, inputs_t, back_t, second = both_passes(
-        core, fetched, planned, self_two.T, neigh_two.T, cotangent.shape
+        core, fetched, planned, self_two.T, neigh_two.T, cotangent.shape, half_rows
     )
     got = swap_cores(send)
     half = add_pair(keep_half(core, inputs_t, back_t, second), got)
-    plane = ("chip", "near")
-    parties = lax.axis_size(plane)
-    far = lax.axis_size("far")
-    piece = half.shape[0] // parties
-    own = sum_parts(exchange(half.reshape(parties, piece, hidden), plane))
+    own = sum_parts(exchange(half.reshape(parties, -1, LANES), plane))
     got = [
         lax.ppermute(own, "far", [(i, (i + shift) % far) for i in range(far)])
         for shift in range(1, far)

time: 123 us -> 121 us (0.984)
  blocking collectives: 54.3 us -> 52.9 us
    all_to_all x3, blocking collectives: 54.3 us -> 52.9 us  [exchange(): return lax.all_to_all(value, axes, split_axis=0, concat_axis=0, tiled=True)]
where the time goes in v4:
time: 121 us; the launch traced here: 120 us
  blocking collectives  52.9 us (44%)
  Pallas kernels  24.9 us (21%)
  starting transfers between devices  20.5 us (17%)
  waiting for transfers between devices  15.7 us (13%)
  local copies, waits for them, and re-layouts  5.2 us (4%)
    all_to_all x3, blocking collectives, exchange(): return lax.all_to_all(value, axes, split_axis=0, concat_axis=0, tiled=True)  52.9 us
    all_to_all x1, waiting for transfers between devices, exchange(): return lax.all_to_all(value, axes, split_axis=0, concat_axis=0, tiled=True)  11.7 us
    ppermute x3, starting transfers between devices, body(): lax.ppermute(own, 'far', [(i, (i + shift) % far) for i in range(far)])  9.83 us
    pallas_call x1, Pallas kernels, both_passes(): pl.pallas_call(pass_kernel, out_shape=(struct(logit_shape, F32), struct((...  8.07 us
    pallas_call x1, Pallas kernels, serve(): pl.pallas_call(serve_kernel, out_shape=pltpu.HBM((count, width), BF), in_...  6.5 us
    ppermute x2, starting transfers between devices, swap_cores(): return lax.ppermute(value, 'core', [(0, 1), (1, 0)])  6.22 us
    pallas_call x1, Pallas kernels, plan(): pl.pallas_call(plan_kernel, out_shape=(pltpu.HBM((batches, slots, nodes),...  6.17 us
    all_to_all x1, starting transfers between devices, exchange(): return lax.all_to_all(value, axes, split_axis=0, concat_axis=0, tiled=True)  4.44 us
  transfers between devices with their start and end apart: 6, of which 5 were waited for; matrix products, arithmetic and copies ran while one was open for 1% of the time, Pallas kernels for 7%

profile of v4, /device:TPU:1, one launch (start us, length us, event | category | flops | bytes accessed | tf_op | source)
XLA Modules:
  0.0 120.1 jit_solution(16841067743639401393)
XLA Ops:
  0.6 0.8 copy.27
  1.4 15.3 %all_to_all.26 = s32[32,1,32]{2,1,0:T(1,128)S(1)} all-to-all(s32[32,1,32]{2,1,0:T(1,128)S(1)} %copy.27), channel_id=1, replica_groups=mesh['chip'=16,'core'=2,'far'=4,'near'=2] {'chip','core'}, dimensions={0} | all-to-all | bytes 8192 | tf_op jit(solution)/shard_map/all_to_all | solution.py:431
  16.7 6.5 %serve.1 = bf16[1024,768]{1,0:T(8,128)(2,1)} custom-call(s32[32,32]{1,0:T(8,128)S(1)} %bitcast.30, bf16[4096,768]{1,0:T(8,128)(2,1)} %rows_ref.1), custom_call_target="tpu_custom_call" | custom-call | flops 786432 | bytes 18874368 | tf_op jit(solution)/shard_map/serve/pallas_call | solution.py:181
  23.3 0.0 copy-start
  23.3 0.0 copy-start.1
  23.3 0.0 copy-start.2
  23.3 0.0 copy-start.3
  23.3 4.4 %all-to-all-start.1 = ((bf16[32,2,16,768]{3,2,1,0:T(8,128)(2,1)}), bf16[32,2,16,768]{3,2,1,0:T(8,128)(2,1)S(1)}, u32[]{:S(2)}, u32[]{:S(2)}) async-start(bf16[32,2,16,768]{3,2,1,0:T(8,128)(2,1)} %bitcast.32), calls=%async_computation.1 | async-start | bytes 3145728 | tf_op jit(solution)/shard_map/all_to_all | solution.py:431
  27.8 0.8 copy.32
  28.5 0.7 copy.33
  29.3 0.0 copy-done
  29.3 0.0 copy-done.1
  29.3 0.0 copy-done.2
  29.3 0.0 copy-done.3
  29.3 0.0 copy-start.4
  29.3 0.8 copy-done.4
  30.1 0.0 copy-start.5
  30.1 0.7 copy-done.5
  30.8 0.0 copy-start.6
  30.8 0.7 copy-done.6
  31.5 0.0 copy-start.7
  31.5 0.7 copy-done.7
  32.2 6.2 %plan.1 = (bf16[2,512,512]{2,1,0:T(8,128)(2,1)}, bf16[2,512,512]{2,1,0:T(8,128)(2,1)}, f32[2,1,512]{2,1,0:T(1,128)}, bf16[2,512,64]{2,1,0:T(8,128)(2,1)}, f32[2,...) custom-call(s32[2,32]{1,0:T(2,128)S(1)} %bitcast.31, ...), custom_call_target="tpu_custom_call" | custom-call | flops 200000000 | bytes 10000000 | tf_op jit(solution)/shard_map/plan/pallas_call | solution.py:106
  38.3 11.7 %all-to-all-done.1.fetched_ref = bf16[32,2,16,768]{3,2,1,0:T(8,128)(2,1)S(1)} async-done(((bf16[32,2,16,768]{3,2,1,0:T(8,128)(2,1)}), bf16[32,2,16,768]{3,2,1,0:T(8,128)(2,1)S(1)}, u32[]{:S(2)}, u32[]{:S(2)}) %all-to-all-start.1) | async-done | bytes 1572896 | tf_op jit(solution)/shard_map/all_to_all | solution.py:431
  50.0 8.1 %both_passes.1 = (f32[2,64,153]{2,1,0:T(8,128)}, bf16[960,512]{1,0:T(8,128)(2,1)S(1)}, bf16[2,768,1024]{2,1,0:T(8,128)(2,1)S(1)}, bf16[512,1024]{1,0:T(8,128)(2,1)S(1)}, f32[2,192,512]{2,1,0:T(8,128)S(1)}) custom-call(s32[1]{0:T(128)} %bitcast.core_ref.slot_ref, bf16[32,2,16,768]{3,2,1,0:T(8,128)(2,1)S(1)} %all-to-all-done.1.fetched_ref, ...), custom_call_target="tpu_custom_call" | custom-call | flops 4499999744 | bytes 20000000 | tf_op jit(solution)/shard_map/both_passes/pallas_call | solution.py:279
  58.1 2.1 %collective-permute-start = (bf16[960,512]{1,0:T(8,128)(2,1)S(1)}, bf16[960,512]{1,0:T(8,128)(2,1)S(1)}, u32[]{:S(2)}, u32[]{:S(2)}) collective-permute-start(bf16[960,512]{1,0:T(8,128)(2,1)S(1)} %get-tuple-element.40), channel_id=1, source_target_pairs={{0,8},{8,0},{1,9},{9,1},{2,10},{10,2},{3,11},{11,3},{4,12},{12,4},... | collective-permute-start | bytes 2949128 | tf_op jit(solution)/shard_map/ppermute | solution.py:435
  60.2 1.0 keep_half.1.keep_ref
  61.2 1.2 collective-permute-done.got_ref
  62.4 0.3 add_pair.1
  62.7 20.5 %all_to_all.27.parts_ref = bf16[32,120,128]{2,1,0:T(8,128)(2,1)S(1)} all-to-all(bf16[32,120,128]{2,1,0:T(8,128)(2,1)S(1)} %bitcast.23), channel_id=1, replica_groups=mesh['chip'=16,'core'=2,'far'=4,'near'=2] {'chip','near'}, dimensions={0} | all-to-all | bytes 1966080 | tf_op jit(solution)/shard_map/all_to_all | solution.py:431
  83.2 0.1 sum_parts.1.own_ref
  83.4 3.2 %collective-permute-start.1 = (bf16[120,128]{1,0:T(8,128)(2,1)S(1)}, bf16[120,128]{1,0:T(8,128)(2,1)S(1)}, u32[]{:S(2)}, u32[]{:S(2)}) collective-permute-start(bf16[120,128]{1,0:T(8,128)(2,1)S(1)} %sum_parts.1.own_ref), channel_id=1, source_target_pairs={{0,2},{2,4},{4,6},{6,0},{1,3},{3,5},{5,7},{7,1},{8,10},{10,12},{12... | collective-permute-start | bytes 92168 | tf_op jit(solution)/shard_map/ppermute | solution.py:473
  86.6 4.2 %collective-permute-start.2 = (bf16[120,128]{1,0:T(8,128)(2,1)S(1)}, bf16[120,128]{1,0:T(8,128)(2,1)S(1)}, u32[]{:S(2)}, u32[]{:S(2)}) collective-permute-start(bf16[120,128]{1,0:T(8,128)(2,1)S(1)} %sum_parts.1.own_ref), channel_id=1, source_target_pairs={{0,4},{2,6},{4,0},{6,2},{1,5},{3,7},{5,1},{7,3},{8,12},{10,14},{12... | collective-permute-start | bytes 92168 | tf_op jit(solution)/shard_map/ppermute | solution.py:473
  90.8 2.4 %collective-permute-start.3 = (bf16[120,128]{1,0:T(8,128)(2,1)S(1)}, bf16[120,128]{1,0:T(8,128)(2,1)S(1)}, u32[]{:S(2)}, u32[]{:S(2)}) collective-permute-start(bf16[120,128]{1,0:T(8,128)(2,1)S(1)} %sum_parts.1.own_ref), channel_id=1, source_target_pairs={{0,6},{2,0},{4,2},{6,4},{1,7},{3,1},{5,3},{7,5},{8,14},{10,8},{12,... | collective-permute-start | bytes 92168 | tf_op jit(solution)/shard_map/ppermute | solution.py:473
  93.2 0.0 collective-permute-done.1.next_ref
  93.2 0.4 collective-permute-done.2.across_ref
  93.6 1.6 %collective-permute-done.3.last_ref = bf16[120,128]{1,0:T(8,128)(2,1)S(1)} collective-permute-done((bf16[120,128]{1,0:T(8,128)(2,1)S(1)}, bf16[120,128]{1,0:T(8,128)(2,1)S(1)}, u32[]{:S(2)}, u32[]{:S(2)}) %collective-permute-start.3) | collective-permute-done | bytes 30752 | tf_op jit(solution)/shard_map/ppermute | solution.py:473
  95.1 0.1 total_copies.1
  95.2 17.1 %all_to_all.28 = bf16[32,120,128]{2,1,0:T(8,128)(2,1)S(1)} all-to-all(bf16[32,120,128]{2,1,0:T(8,128)(2,1)S(1)} %total_copies.1), channel_id=1, replica_groups=mesh['chip'=16,'core'=2,'far'=4,'near'=2] {'chip','near'}, dimensions={0} | all-to-all | bytes 1966080 | tf_op jit(solution)/shard_map/all_to_all | solution.py:431
  112.3 4.1 %collective-permute-start.4 = (bf16[4,960,128]{2,1,0:T(8,128)(2,1)S(1)}, bf16[4,960,128]{2,1,0:T(8,128)(2,1)S(1)}, u32[]{:S(2)}, u32[]{:S(2)}) collective-permute-start(bf16[4,960,128]{2,1,0:T(8,128)(2,1)S(1)} %bitcast.21), channel_id=1, source_target_pairs={{0,8},{8,0},{1,9},{9,1},{2,10},{10,2},{3,11},{11,3},{4,12},{12,4},... | collective-permute-start | bytes 2949128 | tf_op jit(solution)/shard_map/ppermute | solution.py:435
  116.4 1.3 %unpack.2 = (f32[768,512]{1,0:T(8,128)}, f32[768,512]{1,0:T(8,128)}, f32[153,512]{1,0:T(8,128)}, f32[153,512]{1,0:T(8,128)}) custom-call(s32[1]{0:T(128)} %bitcast.core_ref.slot_ref, bf16[4,960,128]{2,1,0:T(8,128)(2,1)S(1)} %bitcast.22), custom_call_target="tpu_custom_call" | custom-call | flops 491520 | bytes 2949120 | tf_op jit(solution)/shard_map/unpack/pallas_call | solution.py:413
  117.7 0.9 collective-permute-done.4.half_ref
  118.6 1.3 %unpack.3 = (f32[768,512]{1,0:T(8,128)}, f32[768,512]{1,0:T(8,128)}, f32[153,512]{1,0:T(8,128)}, f32[153,512]{1,0:T(8,128)}) custom-call(s32[1]{0:T(128)S(6)} %sub.3.slot_ref, bf16[4,960,128]{2,1,0:T(8,128)(2,1)S(1)} %collective-permute-done.4.half_ref, ...), custom_call_target="tpu_custom_call", output_to_operand_aliasing={{0}: (2, {}), {1}: (3, {}), {2}: (4, {}), {3}: (5, {})} | custom-call | flops 491520 | bytes 2949120 | tf_op jit(solution)/shard_map/unpack/pallas_call | solution.py:413
Async XLA Ops:
  23.3 6.0 %copy-start = (bf16[768,512]{1,0:T(8,128)(2,1)S(1)}, bf16[768,512]{1,0:T(8,128)(2,1)}, u32[]{:S(2)}) copy-start(bf16[768,512]{1,0:T(8,128)(2,1)} %self_one_ref.1) | copy-start | bytes 2359300
  23.3 6.0 %copy-start.1 = (bf16[768,512]{1,0:T(8,128)(2,1)S(1)}, bf16[768,512]{1,0:T(8,128)(2,1)}, u32[]{:S(2)}) copy-start(bf16[768,512]{1,0:T(8,128)(2,1)} %neigh_one_ref.1) | copy-start | bytes 2359300
  23.3 6.0 %copy-start.2 = (bf16[512,153]{0,1:T(8,128)(2,1)S(1)}, bf16[512,153]{0,1:T(8,128)(2,1)}, u32[]{:S(2)}) copy-start(bf16[512,153]{0,1:T(8,128)(2,1)} %param.15) | copy-start | bytes 470020
  23.3 6.0 %copy-start.3 = (bf16[512,153]{0,1:T(8,128)(2,1)S(1)}, bf16[512,153]{0,1:T(8,128)(2,1)}, u32[]{:S(2)}) copy-start(bf16[512,153]{0,1:T(8,128)(2,1)} %param.16) | copy-start | bytes 470020
  23.3 26.7 %all-to-all-start.1 = ((bf16[32,2,16,768]{3,2,1,0:T(8,128)(2,1)}), bf16[32,2,16,768]{3,2,1,0:T(8,128)(2,1)S(1)}, u32[]{:S(2)}, u32[]{:S(2)}) async-start(bf16[32,2,16,768]{3,2,1,0:T(8,128)(2,1)} %bitcast.32), calls=%async_computation.1 | async-start | bytes 3145728 | tf_op jit(solution)/shard_map/all_to_all | solution.py:431
  29.3 0.8 copy-start.4
  30.1 0.7 copy-start.5
  30.8 0.7 copy-start.6
  31.5 0.7 copy-start.7
  58.1 4.3 %collective-permute-start = (bf16[960,512]{1,0:T(8,128)(2,1)S(1)}, bf16[960,512]{1,0:T(8,128)(2,1)S(1)}, u32[]{:S(2)}, u32[]{:S(2)}) collective-permute-start(bf16[960,512]{1,0:T(8,128)(2,1)S(1)} %get-tuple-element.40), channel_id=1, source_target_pairs={{0,8},{8,0},{1,9},{9,1},{2,10},{10,2},{3,11},{11,3},{4,12},{12,4},... | collective-permute-start | bytes 2949128 | tf_op jit(solution)/shard_map/ppermute | solution.py:435
  83.4 9.8 %collective-permute-start.1 = (bf16[120,128]{1,0:T(8,128)(2,1)S(1)}, bf16[120,128]{1,0:T(8,128)(2,1)S(1)}, u32[]{:S(2)}, u32[]{:S(2)}) collective-permute-start(bf16[120,128]{1,0:T(8,128)(2,1)S(1)} %sum_parts.1.own_ref), channel_id=1, source_target_pairs={{0,2},{2,4},{4,6},{6,0},{1,3},{3,5},{5,7},{7,1},{8,10},{10,12},{12... | collective-permute-start | bytes 92168 | tf_op jit(solution)/shard_map/ppermute | solution.py:473
  86.6 7.0 %collective-permute-start.2 = (bf16[120,128]{1,0:T(8,128)(2,1)S(1)}, bf16[120,128]{1,0:T(8,128)(2,1)S(1)}, u32[]{:S(2)}, u32[]{:S(2)}) collective-permute-start(bf16[120,128]{1,0:T(8,128)(2,1)S(1)} %sum_parts.1.own_ref), channel_id=1, source_target_pairs={{0,4},{2,6},{4,0},{6,2},{1,5},{3,7},{5,1},{7,3},{8,12},{10,14},{12... | collective-permute-start | bytes 92168 | tf_op jit(solution)/shard_map/ppermute | solution.py:473
  90.8 4.3 %collective-permute-start.3 = (bf16[120,128]{1,0:T(8,128)(2,1)S(1)}, bf16[120,128]{1,0:T(8,128)(2,1)S(1)}, u32[]{:S(2)}, u32[]{:S(2)}) collective-permute-start(bf16[120,128]{1,0:T(8,128)(2,1)S(1)} %sum_parts.1.own_ref), channel_id=1, source_target_pairs={{0,6},{2,0},{4,2},{6,4},{1,7},{3,1},{5,3},{7,5},{8,14},{10,8},{12,... | collective-permute-start | bytes 92168 | tf_op jit(solution)/shard_map/ppermute | solution.py:473
  112.3 6.3 %collective-permute-start.4 = (bf16[4,960,128]{2,1,0:T(8,128)(2,1)S(1)}, bf16[4,960,128]{2,1,0:T(8,128)(2,1)S(1)}, u32[]{:S(2)}, u32[]{:S(2)}) collective-permute-start(bf16[4,960,128]{2,1,0:T(8,128)(2,1)S(1)} %bitcast.21), channel_id=1, source_target_pairs={{0,8},{8,0},{1,9},{9,1},{2,10},{10,2},{3,11},{11,3},{4,12},{12,4},... | collective-permute-start | bytes 2949128 | tf_op jit(solution)/shard_map/ppermute | solution.py:435

commit v5 on v4

--- a/solution.py
+++ b/solution.py
@@ -10,6 +10,8 @@
 VMEM = pl.BlockSpec(memory_space=pltpu.VMEM)
 SMEM = pl.BlockSpec(memory_space=pltpu.SMEM)
 ANY = pl.BlockSpec(memory_space=pl.ANY)
+STORE = ("y", "x", "core")
+PLANE = ("x", "near", "y")
 LANES = 128
 SUBLANES = 8
 
@@ -443,7 +445,7 @@
     width, hidden = self_one.shape
     core = lax.axis_index("core").reshape(1).astype(jnp.int32)
     wanted = request_rows[:, 0].transpose(1, 0, 2).reshape(owners, batches * capacity)
-    asked = exchange(wanted, ("chip", "core"))
+    asked = exchange(wanted, STORE)
     planned = plan(
         bucket_counts[:, 0],
         layer_targets,
@@ -457,8 +459,8 @@
         neigh_two.T,
     )
     rows = serve(asked, features)
-    fetched = exchange(rows.reshape(owners, batches, capacity, width), ("chip", "core"))
-    plane = ("chip", "near")
+    fetched = exchange(rows.reshape(owners, batches, capacity, width), STORE)
+    plane = PLANE
     parties = lax.axis_size(plane)
     far = lax.axis_size("far")
     unit = parties * SUBLANES * LANES // hidden
@@ -482,13 +484,14 @@
 
 def solution(mesh):
     stores, trainers = mesh.shape["store"], mesh.shape["trainer"]
+    chips = stores // 2
+    side = int(chips**0.5)
     split = Mesh(
-        mesh.devices.reshape(stores // 2, 2, trainers // 2, 2), ("chip", "core", "far", "near")
+        mesh.devices.reshape(chips // side, side, 2, trainers // 2, 2), STORE + ("far", "near")
     )
-    store = ("chip", "core")
-    every = ("chip", "core", "far", "near")
+    every = STORE + ("far", "near")
     in_specs = (
-        P(store, None),
+        P(STORE, None),
         P(),
         P(),
         P(),

time: 121 us -> 119 us (0.983)
  no operation moved by 1% of the time
where the time goes in v5:
time: 119 us
  blocking collectives  51.9 us (44%)
  Pallas kernels  24.9 us (21%)
  starting transfers between devices  19.8 us (17%)
  waiting for transfers between devices  15.9 us (13%)
  local copies, waits for them, and re-layouts  5.2 us (4%)
    all_to_all x3, blocking collectives, exchange(): return lax.all_to_all(value, axes, split_axis=0, concat_axis=0, tiled=True)  51.9 us
    all_to_all x1, waiting for transfers between devices, exchange(): return lax.all_to_all(value, axes, split_axis=0, concat_axis=0, tiled=True)  11.7 us
    ppermute x3, starting transfers between devices, body(): lax.ppermute(own, 'far', [(i, (i + shift) % far) for i in range(far)])  9.85 us
    pallas_call x1, Pallas kernels, both_passes(): pl.pallas_call(pass_kernel, out_shape=(struct(logit_shape, F32), struct((...  8.08 us
    pallas_call x1, Pallas kernels, serve(): pl.pallas_call(serve_kernel, out_shape=pltpu.HBM((count, width), BF), in_...  6.5 us
    pallas_call x1, Pallas kernels, plan(): pl.pallas_call(plan_kernel, out_shape=(pltpu.HBM((batches, slots, nodes),...  6.17 us
    ppermute x2, starting transfers between devices, swap_cores(): return lax.ppermute(value, 'core', [(0, 1), (1, 0)])  5.48 us
    all_to_all x1, starting transfers between devices, exchange(): return lax.all_to_all(value, axes, split_axis=0, concat_axis=0, tiled=True)  4.44 us
  transfers between devices with their start and end apart: 6, of which 5 were waited for; matrix products, arithmetic and copies ran while one was open for 1% of the time, Pallas kernels for 7%

profile of v5, /device:TPU:1, one launch (start us, length us, event | category | flops | bytes accessed | tf_op | source)
XLA Modules:
  0.0 118.6 jit_solution(16092699135727340356)
XLA Ops:
  0.6 0.8 copy.27
  1.4 15.3 %all_to_all.26 = s32[32,1,32]{2,1,0:T(1,128)S(1)} all-to-all(s32[32,1,32]{2,1,0:T(1,128)S(1)} %copy.27), channel_id=1, replica_groups=mesh['y'=4,'x'=4,'core'=2,'far'=4,'near'=2] {'y','x','core'}, dimensions={0} | all-to-all | bytes 8192 | tf_op jit(solution)/shard_map/all_to_all | solution.py:433
  16.7 6.5 %serve.1 = bf16[1024,768]{1,0:T(8,128)(2,1)} custom-call(s32[32,32]{1,0:T(8,128)S(1)} %bitcast.30, bf16[4096,768]{1,0:T(8,128)(2,1)} %rows_ref.1), custom_call_target="tpu_custom_call" | custom-call | flops 786432 | bytes 18874368 | tf_op jit(solution)/shard_map/serve/pallas_call | solution.py:183
  23.2 0.0 copy-start
  23.3 0.0 copy-start.1
  23.3 0.0 copy-start.2
  23.3 0.0 copy-start.3
  23.3 4.4 %all-to-all-start.1 = ((bf16[32,2,16,768]{3,2,1,0:T(8,128)(2,1)}), bf16[32,2,16,768]{3,2,1,0:T(8,128)(2,1)S(1)}, u32[]{:S(2)}, u32[]{:S(2)}) async-start(bf16[32,2,16,768]{3,2,1,0:T(8,128)(2,1)} %bitcast.32), calls=%async_computation.1 | async-start | bytes 3145728 | tf_op jit(solution)/shard_map/all_to_all | solution.py:433
  27.7 0.8 copy.32
  28.5 0.7 copy.33
  29.3 0.0 copy-done
  29.3 0.0 copy-done.1
  29.3 0.0 copy-done.2
  29.3 0.0 copy-done.3
  29.3 0.0 copy-start.4
  29.3 0.8 copy-done.4
  30.1 0.0 copy-start.5
  30.1 0.7 copy-done.5
  30.8 0.0 copy-start.6
  30.8 0.7 copy-done.6
  31.5 0.0 copy-start.7
  31.5 0.7 copy-done.7
  32.2 6.2 %plan.1 = (bf16[2,512,512]{2,1,0:T(8,128)(2,1)}, bf16[2,512,512]{2,1,0:T(8,128)(2,1)}, f32[2,1,512]{2,1,0:T(1,128)}, bf16[2,512,64]{2,1,0:T(8,128)(2,1)}, f32[2,...) custom-call(s32[2,32]{1,0:T(2,128)S(1)} %bitcast.31, ...), custom_call_target="tpu_custom_call" | custom-call | flops 200000000 | bytes 10000000 | tf_op jit(solution)/shard_map/plan/pallas_call | solution.py:108
  38.3 11.7 %all-to-all-done.1.fetched_ref = bf16[32,2,16,768]{3,2,1,0:T(8,128)(2,1)S(1)} async-done(((bf16[32,2,16,768]{3,2,1,0:T(8,128)(2,1)}), bf16[32,2,16,768]{3,2,1,0:T(8,128)(2,1)S(1)}, u32[]{:S(2)}, u32[]{:S(2)}) %all-to-all-start.1) | async-done | bytes 1572896 | tf_op jit(solution)/shard_map/all_to_all | solution.py:433
  50.0 8.1 %both_passes.1 = (f32[2,64,153]{2,1,0:T(8,128)}, bf16[960,512]{1,0:T(8,128)(2,1)S(1)}, bf16[2,768,1024]{2,1,0:T(8,128)(2,1)S(1)}, bf16[512,1024]{1,0:T(8,128)(2,1)S(1)}, f32[2,192,512]{2,1,0:T(8,128)S(1)}) custom-call(s32[1]{0:T(128)} %bitcast.core_ref.slot_ref, bf16[32,2,16,768]{3,2,1,0:T(8,128)(2,1)S(1)} %all-to-all-done.1.fetched_ref, ...), custom_call_target="tpu_custom_call" | custom-call | flops 4499999744 | bytes 20000000 | tf_op jit(solution)/shard_map/both_passes/pallas_call | solution.py:281
  58.1 2.1 %collective-permute-start = (bf16[960,512]{1,0:T(8,128)(2,1)S(1)}, bf16[960,512]{1,0:T(8,128)(2,1)S(1)}, u32[]{:S(2)}, u32[]{:S(2)}) collective-permute-start(bf16[960,512]{1,0:T(8,128)(2,1)S(1)} %get-tuple-element.40), channel_id=1, source_target_pairs={{0,8},{8,0},{1,9},{9,1},{2,10},{10,2},{3,11},{11,3},{4,12},{12,4},... | collective-permute-start | bytes 2949128 | tf_op jit(solution)/shard_map/ppermute | solution.py:437
  60.2 1.0 keep_half.1.keep_ref
  61.2 1.2 collective-permute-done.got_ref
  62.4 0.3 add_pair.1
  62.7 19.0 %all_to_all.27.parts_ref = bf16[32,120,128]{2,1,0:T(8,128)(2,1)S(1)} all-to-all(bf16[32,120,128]{2,1,0:T(8,128)(2,1)S(1)} %bitcast.23), channel_id=1, replica_groups=mesh['y'=4,'x'=4,'core'=2,'far'=4,'near'=2] {'x','near','y'}, dimensions={0} | all-to-all | bytes 1966080 | tf_op jit(solution)/shard_map/all_to_all | solution.py:433
  81.7 0.1 sum_parts.1.own_ref
  81.8 3.3 %collective-permute-start.1 = (bf16[120,128]{1,0:T(8,128)(2,1)S(1)}, bf16[120,128]{1,0:T(8,128)(2,1)S(1)}, u32[]{:S(2)}, u32[]{:S(2)}) collective-permute-start(bf16[120,128]{1,0:T(8,128)(2,1)S(1)} %sum_parts.1.own_ref), channel_id=1, source_target_pairs={{0,2},{2,4},{4,6},{6,0},{1,3},{3,5},{5,7},{7,1},{8,10},{10,12},{12... | collective-permute-start | bytes 92168 | tf_op jit(solution)/shard_map/ppermute | solution.py:475
  85.1 4.2 %collective-permute-start.2 = (bf16[120,128]{1,0:T(8,128)(2,1)S(1)}, bf16[120,128]{1,0:T(8,128)(2,1)S(1)}, u32[]{:S(2)}, u32[]{:S(2)}) collective-permute-start(bf16[120,128]{1,0:T(8,128)(2,1)S(1)} %sum_parts.1.own_ref), channel_id=1, source_target_pairs={{0,4},{2,6},{4,0},{6,2},{1,5},{3,7},{5,1},{7,3},{8,12},{10,14},{12... | collective-permute-start | bytes 92168 | tf_op jit(solution)/shard_map/ppermute | solution.py:475
  89.3 2.4 %collective-permute-start.3 = (bf16[120,128]{1,0:T(8,128)(2,1)S(1)}, bf16[120,128]{1,0:T(8,128)(2,1)S(1)}, u32[]{:S(2)}, u32[]{:S(2)}) collective-permute-start(bf16[120,128]{1,0:T(8,128)(2,1)S(1)} %sum_parts.1.own_ref), channel_id=1, source_target_pairs={{0,6},{2,0},{4,2},{6,4},{1,7},{3,1},{5,3},{7,5},{8,14},{10,8},{12,... | collective-permute-start | bytes 92168 | tf_op jit(solution)/shard_map/ppermute | solution.py:475
  91.7 0.0 collective-permute-done.1.next_ref
  91.7 0.1 collective-permute-done.2.across_ref
  91.7 2.2 %collective-permute-done.3.last_ref = bf16[120,128]{1,0:T(8,128)(2,1)S(1)} collective-permute-done((bf16[120,128]{1,0:T(8,128)(2,1)S(1)}, bf16[120,128]{1,0:T(8,128)(2,1)S(1)}, u32[]{:S(2)}, u32[]{:S(2)}) %collective-permute-start.3) | collective-permute-done | bytes 30752 | tf_op jit(solution)/shard_map/ppermute | solution.py:475
  93.9 0.1 total_copies.1
  94.0 17.6 %all_to_all.28 = bf16[32,120,128]{2,1,0:T(8,128)(2,1)S(1)} all-to-all(bf16[32,120,128]{2,1,0:T(8,128)(2,1)S(1)} %total_copies.1), channel_id=1, replica_groups=mesh['y'=4,'x'=4,'core'=2,'far'=4,'near'=2] {'x','near','y'}, dimensions={0} | all-to-all | bytes 1966080 | tf_op jit(solution)/shard_map/all_to_all | solution.py:433
  111.6 3.4 %collective-permute-start.4 = (bf16[4,960,128]{2,1,0:T(8,128)(2,1)S(1)}, bf16[4,960,128]{2,1,0:T(8,128)(2,1)S(1)}, u32[]{:S(2)}, u32[]{:S(2)}) collective-permute-start(bf16[4,960,128]{2,1,0:T(8,128)(2,1)S(1)} %bitcast.21), channel_id=1, source_target_pairs={{0,8},{8,0},{1,9},{9,1},{2,10},{10,2},{3,11},{11,3},{4,12},{12,4},... | collective-permute-start | bytes 2949128 | tf_op jit(solution)/shard_map/ppermute | solution.py:437
  115.0 1.3 %unpack.2 = (f32[768,512]{1,0:T(8,128)}, f32[768,512]{1,0:T(8,128)}, f32[153,512]{1,0:T(8,128)}, f32[153,512]{1,0:T(8,128)}) custom-call(s32[1]{0:T(128)} %bitcast.core_ref.slot_ref, bf16[4,960,128]{2,1,0:T(8,128)(2,1)S(1)} %bitcast.22), custom_call_target="tpu_custom_call" | custom-call | flops 491520 | bytes 2949120 | tf_op jit(solution)/shard_map/unpack/pallas_call | solution.py:415
  116.3 0.9 collective-permute-done.4.half_ref
  117.2 1.3 %unpack.3 = (f32[768,512]{1,0:T(8,128)}, f32[768,512]{1,0:T(8,128)}, f32[153,512]{1,0:T(8,128)}, f32[153,512]{1,0:T(8,128)}) custom-call(s32[1]{0:T(128)S(6)} %sub.3.slot_ref, bf16[4,960,128]{2,1,0:T(8,128)(2,1)S(1)} %collective-permute-done.4.half_ref, ...), custom_call_target="tpu_custom_call", output_to_operand_aliasing={{0}: (2, {}), {1}: (3, {}), {2}: (4, {}), {3}: (5, {})} | custom-call | flops 491520 | bytes 2949120 | tf_op jit(solution)/shard_map/unpack/pallas_call | solution.py:415
Async XLA Ops:
  23.2 6.0 %copy-start = (bf16[768,512]{1,0:T(8,128)(2,1)S(1)}, bf16[768,512]{1,0:T(8,128)(2,1)}, u32[]{:S(2)}) copy-start(bf16[768,512]{1,0:T(8,128)(2,1)} %self_one_ref.1) | copy-start | bytes 2359300
  23.3 6.0 %copy-start.1 = (bf16[768,512]{1,0:T(8,128)(2,1)S(1)}, bf16[768,512]{1,0:T(8,128)(2,1)}, u32[]{:S(2)}) copy-start(bf16[768,512]{1,0:T(8,128)(2,1)} %neigh_one_ref.1) | copy-start | bytes 2359300
  23.3 6.0 %copy-start.2 = (bf16[512,153]{0,1:T(8,128)(2,1)S(1)}, bf16[512,153]{0,1:T(8,128)(2,1)}, u32[]{:S(2)}) copy-start(bf16[512,153]{0,1:T(8,128)(2,1)} %param.15) | copy-start | bytes 470020
  23.3 6.0 %copy-start.3 = (bf16[512,153]{0,1:T(8,128)(2,1)S(1)}, bf16[512,153]{0,1:T(8,128)(2,1)}, u32[]{:S(2)}) copy-start(bf16[512,153]{0,1:T(8,128)(2,1)} %param.16) | copy-start | bytes 470020
  23.3 26.7 %all-to-all-start.1 = ((bf16[32,2,16,768]{3,2,1,0:T(8,128)(2,1)}), bf16[32,2,16,768]{3,2,1,0:T(8,128)(2,1)S(1)}, u32[]{:S(2)}, u32[]{:S(2)}) async-start(bf16[32,2,16,768]{3,2,1,0:T(8,128)(2,1)} %bitcast.32), calls=%async_computation.1 | async-start | bytes 3145728 | tf_op jit(solution)/shard_map/all_to_all | solution.py:433
  29.3 0.8 copy-start.4
  30.1 0.7 copy-start.5
  30.8 0.7 copy-start.6
  31.5 0.7 copy-start.7
  58.1 4.3 %collective-permute-start = (bf16[960,512]{1,0:T(8,128)(2,1)S(1)}, bf16[960,512]{1,0:T(8,128)(2,1)S(1)}, u32[]{:S(2)}, u32[]{:S(2)}) collective-permute-start(bf16[960,512]{1,0:T(8,128)(2,1)S(1)} %get-tuple-element.40), channel_id=1, source_target_pairs={{0,8},{8,0},{1,9},{9,1},{2,10},{10,2},{3,11},{11,3},{4,12},{12,4},... | collective-permute-start | bytes 2949128 | tf_op jit(solution)/shard_map/ppermute | solution.py:437
  81.8 9.8 %collective-permute-start.1 = (bf16[120,128]{1,0:T(8,128)(2,1)S(1)}, bf16[120,128]{1,0:T(8,128)(2,1)S(1)}, u32[]{:S(2)}, u32[]{:S(2)}) collective-permute-start(bf16[120,128]{1,0:T(8,128)(2,1)S(1)} %sum_parts.1.own_ref), channel_id=1, source_target_pairs={{0,2},{2,4},{4,6},{6,0},{1,3},{3,5},{5,7},{7,1},{8,10},{10,12},{12... | collective-permute-start | bytes 92168 | tf_op jit(solution)/shard_map/ppermute | solution.py:475
  85.1 6.7 %collective-permute-start.2 = (bf16[120,128]{1,0:T(8,128)(2,1)S(1)}, bf16[120,128]{1,0:T(8,128)(2,1)S(1)}, u32[]{:S(2)}, u32[]{:S(2)}) collective-permute-start(bf16[120,128]{1,0:T(8,128)(2,1)S(1)} %sum_parts.1.own_ref), channel_id=1, source_target_pairs={{0,4},{2,6},{4,0},{6,2},{1,5},{3,7},{5,1},{7,3},{8,12},{10,14},{12... | collective-permute-start | bytes 92168 | tf_op jit(solution)/shard_map/ppermute | solution.py:475
  89.3 4.6 %collective-permute-start.3 = (bf16[120,128]{1,0:T(8,128)(2,1)S(1)}, bf16[120,128]{1,0:T(8,128)(2,1)S(1)}, u32[]{:S(2)}, u32[]{:S(2)}) collective-permute-start(bf16[120,128]{1,0:T(8,128)(2,1)S(1)} %sum_parts.1.own_ref), channel_id=1, source_target_pairs={{0,6},{2,0},{4,2},{6,4},{1,7},{3,1},{5,3},{7,5},{8,14},{10,8},{12,... | collective-permute-start | bytes 92168 | tf_op jit(solution)/shard_map/ppermute | solution.py:475
  111.6 5.6 %collective-permute-start.4 = (bf16[4,960,128]{2,1,0:T(8,128)(2,1)S(1)}, bf16[4,960,128]{2,1,0:T(8,128)(2,1)S(1)}, u32[]{:S(2)}, u32[]{:S(2)}) collective-permute-start(bf16[4,960,128]{2,1,0:T(8,128)(2,1)S(1)} %bitcast.21), channel_id=1, source_target_pairs={{0,8},{8,0},{1,9},{9,1},{2,10},{10,2},{3,11},{11,3},{4,12},{12,4},... | collective-permute-start | bytes 2949128 | tf_op jit(solution)/shard_map/ppermute | solution.py:437

commit v6 on v5

--- a/solution.py
+++ b/solution.py
@@ -1,3 +1,5 @@
+import functools
+
 import jax
 import jax.numpy as jnp
 from jax import lax
@@ -126,7 +128,9 @@
     )(counts, targets, inner, outer, degree, cot, self_one, neigh_one, self_two, neigh_two)
 
 
-def serve_kernel(asked_ref, rows_ref, out_ref, landed, wide, found, sems, out_sems):
+def serve_kernel(
+    asked_any, rows_ref, out_ref, asked_ref, landed, wide, found, sems, out_sems, asked_sem
+):
     askers, each = asked_ref.shape
     rows, width = rows_ref.shape
     chunks = sems.shape[0]
@@ -137,14 +141,17 @@
         here = pl.ds(c * block, block)
         return pltpu.make_async_copy(rows_ref.at[here, :], landed.at[here, :], sems.at[c])
 
+    asked_load = pltpu.make_async_copy(asked_any, asked_ref, asked_sem)
     for c in range(chunks):
         load(c).start()
+    asked_load.start()
     for c in range(chunks):
         load(c).wait()
         for j in range(pieces):
             piece = landed[pl.ds(c * block, block), j * LANES : (j + 1) * LANES]
             wide[j, pl.ds(SUBLANES + c * block, block), :] = piece.astype(F32)
 
+    asked_load.wait()
     line = lax.broadcasted_iota(jnp.int32, (SUBLANES, LANES), 0)
 
     def one_asker(p, carry):
@@ -183,14 +190,16 @@
     return pl.pallas_call(
         serve_kernel,
         out_shape=pltpu.HBM((count, width), BF),
-        in_specs=[SMEM, ANY],
+        in_specs=[ANY, ANY],
         out_specs=ANY,
         scratch_shapes=[
+            pltpu.SMEM(asked.shape, asked.dtype),
             pltpu.VMEM((rows, width), BF),
             pltpu.VMEM((width // LANES, rows + 2 * SUBLANES, LANES), F32),
             pltpu.VMEM((count, width), BF),
             pltpu.SemaphoreType.DMA((chunks,)),
             pltpu.SemaphoreType.DMA((4,)),
+            pltpu.SemaphoreType.DMA,
         ],
         compiler_params=params(28),
         cost_estimate=cost(count * width, rows * width * 6),
@@ -199,11 +208,11 @@
 
 
 def pass_kernel(
-    core_ref, fetched_ref, own_sel_hbm, sum_sel_hbm, scale_hbm, outer_sel_hbm, outer_scale_hbm,
-    back_hbm, self_t_hbm, neigh_t_hbm, cot_t_hbm, self_two_ref, neigh_two_ref,
+    fetched_ref, own_sel_hbm, sum_sel_hbm, scale_hbm, outer_sel_hbm, outer_scale_hbm,
+    back_hbm, self_t_hbm, neigh_t_hbm, cot_t_hbm, self_two_hbm, neigh_two_hbm,
     logits_ref, send_ref, inputs_t, back_t, second,
     own_sel_ref, sum_sel_ref, scale_ref, outer_sel_ref, outer_scale_ref, back_ref,
-    self_t_ref, neigh_t_ref, cot_t_ref, table_t, sems,
+    self_t_ref, neigh_t_ref, cot_t_ref, self_two_ref, neigh_two_ref, table_t, sems,
 ):
     batches = fetched_ref.shape[1]
     slots, nodes = own_sel_ref.shape[1:]
@@ -213,7 +222,7 @@
         (own_sel_hbm, own_sel_ref), (sum_sel_hbm, sum_sel_ref), (back_hbm, back_ref),
         (scale_hbm, scale_ref), (self_t_hbm, self_t_ref), (neigh_t_hbm, neigh_t_ref),
         (outer_sel_hbm, outer_sel_ref), (outer_scale_hbm, outer_scale_ref),
-        (cot_t_hbm, cot_t_ref),
+        (cot_t_hbm, cot_t_ref), (self_two_hbm, self_two_ref), (neigh_two_hbm, neigh_two_ref),
     )
     split = [
         (source.at[b], target.at[b]) for b in range(batches) for source, target in pairs[:3]
@@ -267,17 +276,18 @@
         else:
             second[0, 0:classes, :] += self_grad
             second[1, 0:classes, :] += neigh_grad
-    sent = 1 - core_ref[0]
+    sent = 1 - lax.axis_index("core")
     send_ref[0:width, :] = nt(inputs_t[sent], back_t[...]).astype(BF)
     send_ref[width:, :] = second[sent].astype(BF)
 
 
-def both_passes(core, fetched, planned, self_two, neigh_two, logit_shape, half_rows):
+def both_passes(fetched, planned, self_two, neigh_two, logit_shape, half_rows):
     batches = fetched.shape[1]
     width = fetched.shape[3]
     hidden = self_two.shape[1]
     nodes = planned[0].shape[2]
     tail = half_rows - width
+    loaded = (*planned, self_two, neigh_two)
     return pl.pallas_call(
         pass_kernel,
         out_shape=(
@@ -287,38 +297,38 @@
             struct((hidden, batches * nodes), BF),
             struct((2, tail, hidden), F32),
         ),
-        in_specs=[SMEM, VMEM] + [ANY] * len(planned) + [VMEM] * 2,
+        in_specs=[VMEM] + [ANY] * len(loaded),
         out_specs=[VMEM] * 5,
-        scratch_shapes=[pltpu.VMEM(value.shape, value.dtype) for value in planned]
+        scratch_shapes=[pltpu.VMEM(value.shape, value.dtype) for value in loaded]
         + [
             pltpu.VMEM((batches, width, nodes), BF),
-            pltpu.SemaphoreType.DMA((len(planned) + 3 * (batches - 1),)),
+            pltpu.SemaphoreType.DMA((len(loaded) + 3 * (batches - 1),)),
         ],
         compiler_params=params(40),
         cost_estimate=cost(4_500_000_000, 20_000_000),
         name="both_passes",
-    )(core, fetched, *[in_hbm(value) for value in planned], self_two, neigh_two)
-
-
-def keep_kernel(core_ref, inputs_t, back_t, second, keep_ref):
-    core = core_ref[0]
+    )(fetched, *[in_hbm(value) for value in loaded])
+
+
+def keep_kernel(inputs_t, back_t, second, keep_ref):
+    core = lax.axis_index("core")
     width = inputs_t.shape[1]
     keep_ref[0:width, :] = nt(inputs_t[core], back_t[...])
     keep_ref[width:, :] = second[core]
 
 
-def keep_half(core, inputs_t, back_t, second):
+def keep_half(inputs_t, back_t, second):
     width, nodes = inputs_t.shape[1:]
     tail, hidden = second.shape[1:]
     return pl.pallas_call(
         keep_kernel,
         out_shape=struct((width + tail, hidden), F32),
-        in_specs=[SMEM] + [VMEM] * 3,
+        in_specs=[VMEM] * 3,
         out_specs=VMEM,
         compiler_params=params(16),
         cost_estimate=cost(2 * width * hidden * nodes, 5_000_000),
         name="keep_half",
-    )(core, inputs_t, back_t, second)
+    )(inputs_t, back_t, second)
 
 
 def add_kernel(keep_ref, got_ref, out_ref):
@@ -378,7 +388,7 @@
     )(own, *got)
 
 
-def unpack_kernel(slot_ref, half_ref, *refs):
+def unpack_kernel(mine, half_ref, *refs):
     self_one, neigh_one, self_two, neigh_two, head, tail, sems = refs[-7:]
     width = head.shape[0]
     classes = tail.shape[0]
@@ -402,31 +412,34 @@
         for copy in copies:
             copy.wait()
 
-    @pl.when(slot_ref[0] == 0)
+    core = lax.axis_index("core")
+    slot = core if mine else 1 - core
+
+    @pl.when(slot == 0)
     def _():
         place(self_one, self_two)
 
-    @pl.when(slot_ref[0] != 0)
+    @pl.when(slot != 0)
     def _():
         place(neigh_one, neigh_two)
 
 
-def unpack(slot, half, one_shape, two_shape, placed=()):
-    return pl.pallas_call(
-        unpack_kernel,
+def unpack(mine, half, one_shape, two_shape, placed=()):
+    return pl.pallas_call(
+        functools.partial(unpack_kernel, mine),
         out_shape=tuple(pltpu.HBM(shape, F32) for shape in (one_shape,) * 2 + (two_shape,) * 2),
-        in_specs=[SMEM, VMEM] + [ANY] * len(placed),
+        in_specs=[VMEM] + [ANY] * len(placed),
         out_specs=[ANY] * 4,
         scratch_shapes=[
             pltpu.VMEM(one_shape, F32),
             pltpu.VMEM(two_shape, F32),
             pltpu.SemaphoreType.DMA((5,)),
         ],
-        input_output_aliases={2 + i: i for i in range(len(placed))},
+        input_output_aliases={1 + i: i for i in range(len(placed))},
         compiler_params=params(5),
         cost_estimate=cost(half.size, half.size * 6),
         name="unpack",
-    )(slot, half, *[in_hbm(value) for value in placed])
+    )(half, *[in_hbm(value) for value in placed])
 
 
 def exchange(value, axes):
@@ -443,7 +456,6 @@
 ):
     batches, _, owners, capacity = request_rows.shape
     width, hidden = self_one.shape
-    core = lax.axis_index("core").reshape(1).astype(jnp.int32)
     wanted = request_rows[:, 0].transpose(1, 0, 2).reshape(owners, batches * capacity)
     asked = exchange(wanted, STORE)
     planned = plan(
@@ -466,10 +478,10 @@
     unit = parties * SUBLANES * LANES // hidden
     half_rows = -(-(width + cotangent.shape[2]) // unit) * unit
     logits, send, inputs_t, back_t, second = both_passes(
-        core, fetched, planned, self_two.T, neigh_two.T, cotangent.shape, half_rows
+        fetched, planned, self_two.T, neigh_two.T, cotangent.shape, half_rows
     )
     got = swap_cores(send)
-    half = add_pair(keep_half(core, inputs_t, back_t, second), got)
+    half = add_pair(keep_half(inputs_t, back_t, second), got)
     own = sum_parts(exchange(half.reshape(parties, -1, LANES), plane))
     got = [
         lax.ppermute(own, "far", [(i, (i + shift) % far) for i in range(far)])
@@ -478,7 +490,7 @@
     mine = exchange(total_copies(own, got, parties), plane).reshape(half.shape)
     other = swap_cores(mine)
     shapes = (self_one.shape, self_two.T.shape)
-    grads = unpack(1 - core, other, *shapes, unpack(core, mine, *shapes))
+    grads = unpack(False, other, *shapes, unpack(True, mine, *shapes))
     return (logits, grads[0], grads[1], grads[2].T, grads[3].T)
 
 

time: 119 us -> 119 us (level)
  waiting for transfers between devices: 15.9 us -> 20 us
  local copies, waits for them, and re-layouts: 5.2 us -> 2.35 us
  starting transfers between devices: 19.8 us -> 18.5 us
    unnamed x18, local copies, waits for them, and re-layouts: 4.41 us -> 1.56 us
    all_to_all x1, waiting for transfers between devices: 11.7 us -> 14.5 us  [exchange(): return lax.all_to_all(value, axes, split_axis=0, concat_axis=0, tiled=True)]
    ppermute x3, starting transfers between devices: 9.85 us -> 8.62 us  [body(): lax.ppermute(own, 'far', [(i, (i + shift) % far) for i in range(far)])]
    ppermute x3, waiting for transfers between devices: 2.21 us -> 3.43 us  [body(): lax.ppermute(own, 'far', [(i, (i + shift) % far) for i in range(far)])]
  transfers between devices with their start and end apart: 6 -> 6, of which waited for: 5 -> 4; matrix products, arithmetic and copies ran while one was open for 1% -> 1% of each run, Pallas kernels for 7% -> 7%
where the time goes in v6:
time: 119 us
  blocking collectives  52.6 us (44%)
  Pallas kernels  24.3 us (20%)
  waiting for transfers between devices  20 us (17%)
  starting transfers between devices  18.5 us (16%)
  local copies, waits for them, and re-layouts  2.35 us (2%)
    all_to_all x3, blocking collectives, exchange(): return lax.all_to_all(value, axes, split_axis=0, concat_axis=0, tiled=True)  52.6 us
    all_to_all x1, waiting for transfers between devices, exchange(): return lax.all_to_all(value, axes, split_axis=0, concat_axis=0, tiled=True)  14.5 us
    ppermute x3, starting transfers between devices, body(): lax.ppermute(own, 'far', [(i, (i + shift) % far) for i in range(far)])  8.62 us
    pallas_call x1, Pallas kernels, both_passes(): pl.pallas_call(pass_kernel, out_shape=(struct(logit_shape, F32), struct((...  8.17 us
    pallas_call x1, Pallas kernels, plan(): pl.pallas_call(plan_kernel, out_shape=(pltpu.HBM((batches, slots, nodes),...  6.18 us
    pallas_call x1, Pallas kernels, serve(): pl.pallas_call(serve_kernel, out_shape=pltpu.HBM((count, width), BF), in_...  5.76 us
    ppermute x2, starting transfers between devices, swap_cores(): return lax.ppermute(value, 'core', [(0, 1), (1, 0)])  5.46 us
    all_to_all x1, starting transfers between devices, exchange(): return lax.all_to_all(value, axes, split_axis=0, concat_axis=0, tiled=True)  4.37 us
  transfers between devices with their start and end apart: 6, of which 4 were waited for; matrix products, arithmetic and copies ran while one was open for 1% of the time, Pallas kernels for 7%

profile of v6, /device:TPU:1, one launch (start us, length us, event | category | flops | bytes accessed | tf_op | source)
XLA Modules:
  0.0 118.7 jit_solution(8535670792897251127)
XLA Ops:
  0.6 0.8 copy.27
  1.4 15.3 %all_to_all.26 = s32[32,1,32]{2,1,0:T(1,128)S(1)} all-to-all(s32[32,1,32]{2,1,0:T(1,128)S(1)} %copy.27), channel_id=1, replica_groups=mesh['y'=4,'x'=4,'core'=2,'far'=4,'near'=2] {'y','x','core'}, dimensions={0} | all-to-all | bytes 8192 | tf_op jit(solution)/shard_map/all_to_all | solution.py:446
  16.7 5.8 %serve.1 = bf16[1024,768]{1,0:T(8,128)(2,1)} custom-call(s32[32,32]{1,0:T(8,128)S(1)} %bitcast.29, bf16[4096,768]{1,0:T(8,128)(2,1)} %rows_ref.1), custom_call_target="tpu_custom_call" | custom-call | flops 786432 | bytes 18874368 | tf_op jit(solution)/shard_map/serve/pallas_call | solution.py:190
  22.5 0.0 copy-start
  22.5 0.0 copy-start.1
  22.5 0.0 copy-start.2
  22.5 0.0 copy-start.3
  22.6 0.0 copy-start.4
  22.6 0.0 copy-start.5
  22.6 0.0 copy-start.6
  22.6 0.0 copy-start.7
  22.6 4.4 %all-to-all-start.1 = ((bf16[32,2,16,768]{3,2,1,0:T(8,128)(2,1)}), bf16[32,2,16,768]{3,2,1,0:T(8,128)(2,1)S(1)}, u32[]{:S(2)}, u32[]{:S(2)}) async-start(bf16[32,2,16,768]{3,2,1,0:T(8,128)(2,1)} %bitcast.31), calls=%async_computation.1 | async-start | bytes 3145728 | tf_op jit(solution)/shard_map/all_to_all | solution.py:446
  27.0 0.7 copy.33
  27.7 0.8 copy.32
  28.5 0.0 copy-done
  28.5 0.0 copy-done.1
  28.5 0.0 copy-done.2
  28.5 0.0 copy-done.3
  28.5 0.0 copy-done.4
  28.5 0.0 copy-done.5
  28.6 0.0 copy-done.6
  28.6 0.0 copy-done.7
  28.6 6.2 %plan.1 = (bf16[2,512,512]{2,1,0:T(8,128)(2,1)}, bf16[2,512,512]{2,1,0:T(8,128)(2,1)}, f32[2,1,512]{2,1,0:T(1,128)}, bf16[2,512,64]{2,1,0:T(8,128)(2,1)}, f32[2,...) custom-call(s32[2,32]{1,0:T(2,128)S(1)} %bitcast.30, ...), custom_call_target="tpu_custom_call" | custom-call | flops 200000000 | bytes 10000000 | tf_op jit(solution)/shard_map/plan/pallas_call | solution.py:110
  34.8 14.5 %all-to-all-done.1.fetched_ref = bf16[32,2,16,768]{3,2,1,0:T(8,128)(2,1)S(1)} async-done(((bf16[32,2,16,768]{3,2,1,0:T(8,128)(2,1)}), bf16[32,2,16,768]{3,2,1,0:T(8,128)(2,1)S(1)}, u32[]{:S(2)}, u32[]{:S(2)}) %all-to-all-start.1) | async-done | bytes 1572896 | tf_op jit(solution)/shard_map/all_to_all | solution.py:446
  49.3 8.2 %both_passes.1 = (f32[2,64,153]{2,1,0:T(8,128)}, bf16[960,512]{1,0:T(8,128)(2,1)S(1)}, bf16[2,768,1024]{2,1,0:T(8,128)(2,1)S(1)}, bf16[512,1024]{1,0:T(8,128)(2,1)S(1)}, f32[2,192,512]{2,1,0:T(8,128)S(1)}) custom-call(bf16[32,2,16,768]{3,2,1,0:T(8,128)(2,1)S(1)} %all-to-all-done.1.fetched_ref, bf16[2,512,512]{2,1,0:T(8,128)(2,1)} %get-tuple-element.27.own_sel_hbm, ...), custom_call_target="tpu_custom_call" | custom-call | flops 4499999744 | bytes 20000000 | tf_op jit(solution)/shard_map/both_passes/pallas_call | solution.py:291
  57.4 2.1 %collective-permute-start = (bf16[960,512]{1,0:T(8,128)(2,1)S(1)}, bf16[960,512]{1,0:T(8,128)(2,1)S(1)}, u32[]{:S(2)}, u32[]{:S(2)}) collective-permute-start(bf16[960,512]{1,0:T(8,128)(2,1)S(1)} %get-tuple-element.40), channel_id=1, source_target_pairs={{0,8},{8,0},{1,9},{9,1},{2,10},{10,2},{3,11},{11,3},{4,12},{12,4},... | collective-permute-start | bytes 2949128 | tf_op jit(solution)/shard_map/ppermute | solution.py:450
  59.6 1.0 keep_half.1.keep_ref
  60.6 1.2 collective-permute-done.got_ref
  61.7 0.3 add_pair.1
  62.0 19.0 %all_to_all.27.parts_ref = bf16[32,120,128]{2,1,0:T(8,128)(2,1)S(1)} all-to-all(bf16[32,120,128]{2,1,0:T(8,128)(2,1)S(1)} %bitcast.22), channel_id=1, replica_groups=mesh['y'=4,'x'=4,'core'=2,'far'=4,'near'=2] {'x','near','y'}, dimensions={0} | all-to-all | bytes 1966080 | tf_op jit(solution)/shard_map/all_to_all | solution.py:446
  81.0 0.1 sum_parts.1.own_ref
  81.2 5.4 %collective-permute-start.3 = (bf16[120,128]{1,0:T(8,128)(2,1)S(1)}, bf16[120,128]{1,0:T(8,128)(2,1)S(1)}, u32[]{:S(2)}, u32[]{:S(2)}) collective-permute-start(bf16[120,128]{1,0:T(8,128)(2,1)S(1)} %sum_parts.1.own_ref), channel_id=1, source_target_pairs={{0,6},{2,0},{4,2},{6,4},{1,7},{3,1},{5,3},{7,5},{8,14},{10,8},{12,... | collective-permute-start | bytes 92168 | tf_op jit(solution)/shard_map/ppermute | solution.py:487
  86.6 1.2 collective-permute-start.2
  87.7 2.1 %collective-permute-start.1 = (bf16[120,128]{1,0:T(8,128)(2,1)S(1)}, bf16[120,128]{1,0:T(8,128)(2,1)S(1)}, u32[]{:S(2)}, u32[]{:S(2)}) collective-permute-start(bf16[120,128]{1,0:T(8,128)(2,1)S(1)} %sum_parts.1.own_ref), channel_id=1, source_target_pairs={{0,2},{2,4},{4,6},{6,0},{1,3},{3,5},{5,7},{7,1},{8,10},{10,12},{12... | collective-permute-start | bytes 92168 | tf_op jit(solution)/shard_map/ppermute | solution.py:487
  89.8 0.0 collective-permute-done.3.last_ref
  89.8 3.4 %collective-permute-done.2.across_ref = bf16[120,128]{1,0:T(8,128)(2,1)S(1)} collective-permute-done((bf16[120,128]{1,0:T(8,128)(2,1)S(1)}, bf16[120,128]{1,0:T(8,128)(2,1)S(1)}, u32[]{:S(2)}, u32[]{:S(2)}) %collective-permute-start.2) | collective-permute-done | bytes 30752 | tf_op jit(solution)/shard_map/ppermute | solution.py:487
  93.2 0.0 collective-permute-done.1.next_ref
  93.2 0.1 total_copies.1
  93.3 18.3 %all_to_all.28 = bf16[32,120,128]{2,1,0:T(8,128)(2,1)S(1)} all-to-all(bf16[32,120,128]{2,1,0:T(8,128)(2,1)S(1)} %total_copies.1), channel_id=1, replica_groups=mesh['y'=4,'x'=4,'core'=2,'far'=4,'near'=2] {'x','near','y'}, dimensions={0} | all-to-all | bytes 1966080 | tf_op jit(solution)/shard_map/all_to_all | solution.py:446
  111.6 3.3 %collective-permute-start.4 = (bf16[4,960,128]{2,1,0:T(8,128)(2,1)S(1)}, bf16[4,960,128]{2,1,0:T(8,128)(2,1)S(1)}, u32[]{:S(2)}, u32[]{:S(2)}) collective-permute-start(bf16[4,960,128]{2,1,0:T(8,128)(2,1)S(1)} %bitcast.20), channel_id=1, source_target_pairs={{0,8},{8,0},{1,9},{9,1},{2,10},{10,2},{3,11},{11,3},{4,12},{12,4},... | collective-permute-start | bytes 2949128 | tf_op jit(solution)/shard_map/ppermute | solution.py:450
  115.0 1.3 %unpack.2 = (f32[768,512]{1,0:T(8,128)}, f32[768,512]{1,0:T(8,128)}, f32[153,512]{1,0:T(8,128)}, f32[153,512]{1,0:T(8,128)}) custom-call(bf16[4,960,128]{2,1,0:T(8,128)(2,1)S(1)} %bitcast.21), custom_call_target="tpu_custom_call" | custom-call | flops 491520 | bytes 2949120 | tf_op jit(solution)/shard_map/unpack/pallas_call | solution.py:428
  116.3 0.9 collective-permute-done.4.half_ref
  117.2 1.3 %unpack.3 = (f32[768,512]{1,0:T(8,128)}, f32[768,512]{1,0:T(8,128)}, f32[153,512]{1,0:T(8,128)}, f32[153,512]{1,0:T(8,128)}) custom-call(bf16[4,960,128]{2,1,0:T(8,128)(2,1)S(1)} %collective-permute-done.4.half_ref, f32[768,512]{1,0:T(8,128)} %get-tuple-element.41.refs_0_, ...), custom_call_target="tpu_custom_call", output_to_operand_aliasing={{0}: (1, {}), {1}: (2, {}), {2}: (3, {}), {3}: (4, {})} | custom-call | flops 491520 | bytes 2949120 | tf_op jit(solution)/shard_map/unpack/pallas_call | solution.py:428
Async XLA Ops:
  22.5 6.0 %copy-start = (bf16[768,512]{1,0:T(8,128)(2,1)S(1)}, bf16[768,512]{1,0:T(8,128)(2,1)}, u32[]{:S(2)}) copy-start(bf16[768,512]{1,0:T(8,128)(2,1)} %self_one_ref.1) | copy-start | bytes 2359300
  22.5 6.0 %copy-start.1 = (bf16[768,512]{1,0:T(8,128)(2,1)S(1)}, bf16[768,512]{1,0:T(8,128)(2,1)}, u32[]{:S(2)}) copy-start(bf16[768,512]{1,0:T(8,128)(2,1)} %neigh_one_ref.1) | copy-start | bytes 2359300
  22.5 6.0 %copy-start.2 = (bf16[512,153]{0,1:T(8,128)(2,1)S(1)}, bf16[512,153]{0,1:T(8,128)(2,1)}, u32[]{:S(2)}) copy-start(bf16[512,153]{0,1:T(8,128)(2,1)} %param.15) | copy-start | bytes 470020
  22.5 6.0 %copy-start.3 = (bf16[512,153]{0,1:T(8,128)(2,1)S(1)}, bf16[512,153]{0,1:T(8,128)(2,1)}, u32[]{:S(2)}) copy-start(bf16[512,153]{0,1:T(8,128)(2,1)} %param.16) | copy-start | bytes 470020
  22.6 6.0 %copy-start.4 = (bf16[2,64,153]{2,1,0:T(8,128)(2,1)S(1)}, bf16[2,64,153]{2,1,0:T(8,128)(2,1)}, u32[]{:S(2)}) copy-start(bf16[2,64,153]{2,1,0:T(8,128)(2,1)} %cot_ref.1) | copy-start | bytes 117508
  22.6 6.0 %copy-start.5 = (s32[2,512]{1,0:T(2,128)S(1)}, s32[2,512]{1,0:T(2,128)}, u32[]{:S(2)}) copy-start(s32[2,512]{1,0:T(2,128)} %targets_ref.1) | copy-start | bytes 12292
  22.6 6.0 %copy-start.6 = (s32[2,1,32]{2,1,0:T(1,128)S(1)}, s32[2,1,32]{2,1,0:T(1,128)}, u32[]{:S(2)}) copy-start(s32[2,1,32]{2,1,0:T(1,128)} %param.17) | copy-start | bytes 772
  22.6 6.0 %copy-start.7 = (s32[2,64]{1,0:T(2,128)S(1)}, s32[2,64]{1,0:T(2,128)}, u32[]{:S(2)}) copy-start(s32[2,64]{1,0:T(2,128)} %degree_ref.1) | copy-start | bytes 1540
  22.6 26.7 %all-to-all-start.1 = ((bf16[32,2,16,768]{3,2,1,0:T(8,128)(2,1)}), bf16[32,2,16,768]{3,2,1,0:T(8,128)(2,1)S(1)}, u32[]{:S(2)}, u32[]{:S(2)}) async-start(bf16[32,2,16,768]{3,2,1,0:T(8,128)(2,1)} %bitcast.31), calls=%async_computation.1 | async-start | bytes 3145728 | tf_op jit(solution)/shard_map/all_to_all | solution.py:446
  57.4 4.3 %collective-permute-start = (bf16[960,512]{1,0:T(8,128)(2,1)S(1)}, bf16[960,512]{1,0:T(8,128)(2,1)S(1)}, u32[]{:S(2)}, u32[]{:S(2)}) collective-permute-start(bf16[960,512]{1,0:T(8,128)(2,1)S(1)} %get-tuple-element.40), channel_id=1, source_target_pairs={{0,8},{8,0},{1,9},{9,1},{2,10},{10,2},{3,11},{11,3},{4,12},{12,4},... | collective-permute-start | bytes 2949128 | tf_op jit(solution)/shard_map/ppermute | solution.py:450
  81.2 8.6 %collective-permute-start.3 = (bf16[120,128]{1,0:T(8,128)(2,1)S(1)}, bf16[120,128]{1,0:T(8,128)(2,1)S(1)}, u32[]{:S(2)}, u32[]{:S(2)}) collective-permute-start(bf16[120,128]{1,0:T(8,128)(2,1)S(1)} %sum_parts.1.own_ref), channel_id=1, source_target_pairs={{0,6},{2,0},{4,2},{6,4},{1,7},{3,1},{5,3},{7,5},{8,14},{10,8},{12,... | collective-permute-start | bytes 92168 | tf_op jit(solution)/shard_map/ppermute | solution.py:487
  86.6 6.7 %collective-permute-start.2 = (bf16[120,128]{1,0:T(8,128)(2,1)S(1)}, bf16[120,128]{1,0:T(8,128)(2,1)S(1)}, u32[]{:S(2)}, u32[]{:S(2)}) collective-permute-start(bf16[120,128]{1,0:T(8,128)(2,1)S(1)} %sum_parts.1.own_ref), channel_id=1, source_target_pairs={{0,4},{2,6},{4,0},{6,2},{1,5},{3,7},{5,1},{7,3},{8,12},{10,14},{12... | collective-permute-start | bytes 92168 | tf_op jit(solution)/shard_map/ppermute | solution.py:487
  87.7 5.5 %collective-permute-start.1 = (bf16[120,128]{1,0:T(8,128)(2,1)S(1)}, bf16[120,128]{1,0:T(8,128)(2,1)S(1)}, u32[]{:S(2)}, u32[]{:S(2)}) collective-permute-start(bf16[120,128]{1,0:T(8,128)(2,1)S(1)} %sum_parts.1.own_ref), channel_id=1, source_target_pairs={{0,2},{2,4},{4,6},{6,0},{1,3},{3,5},{5,7},{7,1},{8,10},{10,12},{12... | collective-permute-start | bytes 92168 | tf_op jit(solution)/shard_map/ppermute | solution.py:487
  111.6 5.5 %collective-permute-start.4 = (bf16[4,960,128]{2,1,0:T(8,128)(2,1)S(1)}, bf16[4,960,128]{2,1,0:T(8,128)(2,1)S(1)}, u32[]{:S(2)}, u32[]{:S(2)}) collective-permute-start(bf16[4,960,128]{2,1,0:T(8,128)(2,1)S(1)} %bitcast.20), channel_id=1, source_target_pairs={{0,8},{8,0},{1,9},{9,1},{2,10},{10,2},{3,11},{11,3},{4,12},{12,4},... | collective-permute-start | bytes 2949128 | tf_op jit(solution)/shard_map/ppermute | solution.py:450

commit v7 on v6

--- a/solution.py
+++ b/solution.py
@@ -209,20 +209,20 @@
 
 def pass_kernel(
     fetched_ref, own_sel_hbm, sum_sel_hbm, scale_hbm, outer_sel_hbm, outer_scale_hbm,
-    back_hbm, self_t_hbm, neigh_t_hbm, cot_t_hbm, self_two_hbm, neigh_two_hbm,
-    logits_ref, send_ref, inputs_t, back_t, second,
+    back_hbm, self_t_hbm, neigh_t_hbm, cot_t_hbm,
+    seeds_t, send_ref, inputs_t, back_t, second,
     own_sel_ref, sum_sel_ref, scale_ref, outer_sel_ref, outer_scale_ref, back_ref,
-    self_t_ref, neigh_t_ref, cot_t_ref, self_two_ref, neigh_two_ref, table_t, sems,
+    self_t_ref, neigh_t_ref, cot_t_ref, table_t, sems,
 ):
     batches = fetched_ref.shape[1]
     slots, nodes = own_sel_ref.shape[1:]
     hidden, width = self_t_ref.shape
-    seeds, classes = logits_ref.shape[1:]
+    classes, seeds = cot_t_ref.shape[1:]
     pairs = (
         (own_sel_hbm, own_sel_ref), (sum_sel_hbm, sum_sel_ref), (back_hbm, back_ref),
         (scale_hbm, scale_ref), (self_t_hbm, self_t_ref), (neigh_t_hbm, neigh_t_ref),
         (outer_sel_hbm, outer_sel_ref), (outer_scale_hbm, outer_scale_ref),
-        (cot_t_hbm, cot_t_ref), (self_two_hbm, self_two_ref), (neigh_two_hbm, neigh_two_ref),
+        (cot_t_hbm, cot_t_ref),
     )
     split = [
         (source.at[b], target.at[b]) for b in range(batches) for source, target in pairs[:3]
@@ -267,7 +267,8 @@
         back_t[:, b * nodes : (b + 1) * nodes] = slope.astype(BF)
         outer_t = (nn(hidden_t, outer_sel_ref[b]) * outer_scale_ref[b]).astype(BF)
         seed_t = hidden_t[:, 0:seeds]
-        logits_ref[b, :, :] = (nn(self_two_ref[...], seed_t) + nn(neigh_two_ref[...], outer_t)).T
+        seeds_t[0, b] = seed_t
+        seeds_t[1, b] = outer_t
         self_grad = nt(cot_t_ref[b], seed_t)
         neigh_grad = nt(cot_t_ref[b], outer_t)
         if b == 0:
@@ -281,54 +282,57 @@
     send_ref[width:, :] = second[sent].astype(BF)
 
 
-def both_passes(fetched, planned, self_two, neigh_two, logit_shape, half_rows):
+def both_passes(fetched, planned, half_rows):
     batches = fetched.shape[1]
     width = fetched.shape[3]
-    hidden = self_two.shape[1]
+    hidden = planned[6].shape[0]
+    seeds = planned[3].shape[2]
     nodes = planned[0].shape[2]
     tail = half_rows - width
-    loaded = (*planned, self_two, neigh_two)
     return pl.pallas_call(
         pass_kernel,
         out_shape=(
-            struct(logit_shape, F32),
+            struct((2, batches, hidden, seeds), BF),
             struct((half_rows, hidden), BF),
             struct((2, width, batches * nodes), BF),
             struct((hidden, batches * nodes), BF),
             struct((2, tail, hidden), F32),
         ),
-        in_specs=[VMEM] + [ANY] * len(loaded),
+        in_specs=[VMEM] + [ANY] * len(planned),
         out_specs=[VMEM] * 5,
-        scratch_shapes=[pltpu.VMEM(value.shape, value.dtype) for value in loaded]
+        scratch_shapes=[pltpu.VMEM(value.shape, value.dtype) for value in planned]
         + [
             pltpu.VMEM((batches, width, nodes), BF),
-            pltpu.SemaphoreType.DMA((len(loaded) + 3 * (batches - 1),)),
+            pltpu.SemaphoreType.DMA((len(planned) + 3 * (batches - 1),)),
         ],
         compiler_params=params(40),
         cost_estimate=cost(4_500_000_000, 20_000_000),
         name="both_passes",
-    )(fetched, *[in_hbm(value) for value in loaded])
-
-
-def keep_kernel(inputs_t, back_t, second, keep_ref):
+    )(fetched, *[in_hbm(value) for value in planned])
+
+
+def keep_kernel(inputs_t, back_t, second, seeds_t, self_two_ref, neigh_two_ref, keep_ref, logits_ref):
     core = lax.axis_index("core")
     width = inputs_t.shape[1]
     keep_ref[0:width, :] = nt(inputs_t[core], back_t[...])
     keep_ref[width:, :] = second[core]
-
-
-def keep_half(inputs_t, back_t, second):
+    for b in range(logits_ref.shape[0]):
+        own = nn(self_two_ref[...], seeds_t[0, b])
+        logits_ref[b, :, :] = (own + nn(neigh_two_ref[...], seeds_t[1, b])).T
+
+
+def keep_half(inputs_t, back_t, second, seeds_t, self_two, neigh_two, logit_shape):
     width, nodes = inputs_t.shape[1:]
     tail, hidden = second.shape[1:]
     return pl.pallas_call(
         keep_kernel,
-        out_shape=struct((width + tail, hidden), F32),
-        in_specs=[VMEM] * 3,
-        out_specs=VMEM,
+        out_shape=(struct((width + tail, hidden), F32), struct(logit_shape, F32)),
+        in_specs=[VMEM] * 6,
+        out_specs=[VMEM] * 2,
         compiler_params=params(16),
         cost_estimate=cost(2 * width * hidden * nodes, 5_000_000),
         name="keep_half",
-    )(inputs_t, back_t, second)
+    )(inputs_t, back_t, second, seeds_t, self_two, neigh_two)
 
 
 def add_kernel(keep_ref, got_ref, out_ref):
@@ -477,11 +481,12 @@
     far = lax.axis_size("far")
     unit = parties * SUBLANES * LANES // hidden
     half_rows = -(-(width + cotangent.shape[2]) // unit) * unit
-    logits, send, inputs_t, back_t, second = both_passes(
-        fetched, planned, self_two.T, neigh_two.T, cotangent.shape, half_rows
+    seeds_t, send, inputs_t, back_t, second = both_passes(fetched, planned, half_rows)
+    got = swap_cores(send)
+    keep, logits = keep_half(
+        inputs_t, back_t, second, seeds_t, self_two.T, neigh_two.T, cotangent.shape
     )
-    got = swap_cores(send)
-    half = add_pair(keep_half(inputs_t, back_t, second), got)
+    half = add_pair(keep, got)
     own = sum_parts(exchange(half.reshape(parties, -1, LANES), plane))
     got = [
         lax.ppermute(own, "far", [(i, (i + shift) % far) for i in range(far)])

time: 119 us -> 118 us (level)
  transfers between devices with their start and end apart: 6 -> 6, of which waited for: 4 -> 4; matrix products, arithmetic and copies ran while one was open for 1% -> 1% of each run, Pallas kernels for 7% -> 8%
where the time goes in v7:
time: 118 us; the launch traced here: 117 us
  blocking collectives  52.6 us (45%)
  Pallas kernels  24 us (20%)
  waiting for transfers between devices  19 us (16%)
  starting transfers between devices  18.5 us (16%)
  local copies, waits for them, and re-layouts  2.35 us (2%)
    all_to_all x3, blocking collectives, exchange(): return lax.all_to_all(value, axes, split_axis=0, concat_axis=0, tiled=True)  52.6 us
    all_to_all x1, waiting for transfers between devices, exchange(): return lax.all_to_all(value, axes, split_axis=0, concat_axis=0, tiled=True)  14.5 us
    ppermute x3, starting transfers between devices, body(): lax.ppermute(own, 'far', [(i, (i + shift) % far) for i in range(far)])  8.46 us
    pallas_call x1, Pallas kernels, both_passes(): pl.pallas_call(pass_kernel, out_shape=(struct((2, batches, hidden, seeds)...  6.97 us
    pallas_call x1, Pallas kernels, plan(): pl.pallas_call(plan_kernel, out_shape=(pltpu.HBM((batches, slots, nodes),...  6.18 us
    pallas_call x1, Pallas kernels, serve(): pl.pallas_call(serve_kernel, out_shape=pltpu.HBM((count, width), BF), in_...  5.73 us
    ppermute x2, starting transfers between devices, swap_cores(): return lax.ppermute(value, 'core', [(0, 1), (1, 0)])  5.64 us
    all_to_all x1, starting transfers between devices, exchange(): return lax.all_to_all(value, axes, split_axis=0, concat_axis=0, tiled=True)  4.39 us
  transfers between devices with their start and end apart: 6, of which 4 were waited for; matrix products, arithmetic and copies ran while one was open for 1% of the time, Pallas kernels for 8%

profile of v7, /device:TPU:1, one launch (start us, length us, event | category | flops | bytes accessed | tf_op | source)
XLA Modules:
  0.0 117.4 jit_solution(17391826207428327370)
XLA Ops:
  0.6 0.8 copy.27
  1.4 15.3 %all_to_all.26 = s32[32,1,32]{2,1,0:T(1,128)S(1)} all-to-all(s32[32,1,32]{2,1,0:T(1,128)S(1)} %copy.27), channel_id=1, replica_groups=mesh['y'=4,'x'=4,'core'=2,'far'=4,'near'=2] {'y','x','core'}, dimensions={0} | all-to-all | bytes 8192 | tf_op jit(solution)/shard_map/all_to_all | solution.py:450
  16.7 5.7 %serve.1 = bf16[1024,768]{1,0:T(8,128)(2,1)} custom-call(s32[32,32]{1,0:T(8,128)S(1)} %bitcast.29, bf16[4096,768]{1,0:T(8,128)(2,1)} %rows_ref.1), custom_call_target="tpu_custom_call" | custom-call | flops 786432 | bytes 18874368 | tf_op jit(solution)/shard_map/serve/pallas_call | solution.py:190
  22.5 0.0 copy-start
  22.5 0.0 copy-start.1
  22.5 0.0 copy-start.2
  22.5 0.0 copy-start.3
  22.5 0.0 copy-start.4
  22.5 0.0 copy-start.5
  22.6 0.0 copy-start.6
  22.6 0.0 copy-start.7
  22.6 4.4 %all-to-all-start.1 = ((bf16[32,2,16,768]{3,2,1,0:T(8,128)(2,1)}), bf16[32,2,16,768]{3,2,1,0:T(8,128)(2,1)S(1)}, u32[]{:S(2)}, u32[]{:S(2)}) async-start(bf16[32,2,16,768]{3,2,1,0:T(8,128)(2,1)} %bitcast.31), calls=%async_computation.1 | async-start | bytes 3145728 | tf_op jit(solution)/shard_map/all_to_all | solution.py:450
  27.0 0.7 copy.33
  27.7 0.8 copy.32
  28.5 0.0 copy-done
  28.5 0.0 copy-done.1
  28.5 0.0 copy-done.2
  28.5 0.0 copy-done.3
  28.5 0.0 copy-done.4
  28.5 0.0 copy-done.5
  28.5 0.0 copy-done.6
  28.6 0.0 copy-done.7
  28.6 6.2 %plan.1 = (bf16[2,512,512]{2,1,0:T(8,128)(2,1)}, bf16[2,512,512]{2,1,0:T(8,128)(2,1)}, f32[2,1,512]{2,1,0:T(1,128)}, bf16[2,512,64]{2,1,0:T(8,128)(2,1)}, f32[2,...) custom-call(s32[2,32]{1,0:T(2,128)S(1)} %bitcast.30, ...), custom_call_target="tpu_custom_call" | custom-call | flops 200000000 | bytes 10000000 | tf_op jit(solution)/shard_map/plan/pallas_call | solution.py:110
  34.7 14.5 %all-to-all-done.1.fetched_ref = bf16[32,2,16,768]{3,2,1,0:T(8,128)(2,1)S(1)} async-done(((bf16[32,2,16,768]{3,2,1,0:T(8,128)(2,1)}), bf16[32,2,16,768]{3,2,1,0:T(8,128)(2,1)S(1)}, u32[]{:S(2)}, u32[]{:S(2)}) %all-to-all-start.1) | async-done | bytes 1572896 | tf_op jit(solution)/shard_map/all_to_all | solution.py:450
  49.2 7.0 %both_passes.1 = (bf16[2,2,512,64]{3,2,1,0:T(8,128)(2,1)S(1)}, bf16[960,512]{1,0:T(8,128)(2,1)S(1)}, bf16[2,768,1024]{2,1,0:T(8,128)(2,1)S(1)}, bf16[512,1024]{1,0:T(8,128)(2,1)S(1)}, f32[2,192,512]{2,1,0:T(8,128)S(1)}) custom-call(bf16[32,2,16,768]{3,2,1,0:T(8,128)(2,1)S(1)} %all-to-all-done.1.fetched_ref, ...), custom_call_target="tpu_custom_call" | custom-call | flops 4499999744 | bytes 20000000 | tf_op jit(solution)/shard_map/both_passes/pallas_call | solution.py:292
  56.2 2.3 %collective-permute-start = (bf16[960,512]{1,0:T(8,128)(2,1)S(1)}, bf16[960,512]{1,0:T(8,128)(2,1)S(1)}, u32[]{:S(2)}, u32[]{:S(2)}) collective-permute-start(bf16[960,512]{1,0:T(8,128)(2,1)S(1)} %get-tuple-element.44), channel_id=1, source_target_pairs={{0,8},{8,0},{1,9},{9,1},{2,10},{10,2},{3,11},{11,3},{4,12},{12,4},... | collective-permute-start | bytes 2949128 | tf_op jit(solution)/shard_map/ppermute | solution.py:454
  58.5 1.9 %keep_half.1 = (f32[960,512]{1,0:T(8,128)S(1)}, f32[2,64,153]{2,1,0:T(8,128)}) custom-call(bf16[2,768,1024]{2,1,0:T(8,128)(2,1)S(1)} %get-tuple-element.38.inputs_t, bf16[512,1024]{1,0:T(8,128)(2,1)S(1)} %get-tuple-element.39.back_t, f32[2,192,512]{2,1,0:T(8,128)S(1)} %get-tuple-element.40.second, bf16[2,2,512,64]{3,2,1,0:T(8,128)(2,1)S(1)} %get-tuple-element.41.seeds_t, ...), custom_call_target="tpu_custom_call" | custom-call | flops 805306368 | bytes 5000000 | tf_op jit(solution)/shard_map/keep_half/pallas_call | solution.py:327
  60.4 0.3 collective-permute-done.got_ref
  60.7 0.3 add_pair.1
  61.0 19.0 %all_to_all.27.parts_ref = bf16[32,120,128]{2,1,0:T(8,128)(2,1)S(1)} all-to-all(bf16[32,120,128]{2,1,0:T(8,128)(2,1)S(1)} %bitcast.22), channel_id=1, replica_groups=mesh['y'=4,'x'=4,'core'=2,'far'=4,'near'=2] {'x','near','y'}, dimensions={0} | all-to-all | bytes 1966080 | tf_op jit(solution)/shard_map/all_to_all | solution.py:450
  80.0 0.1 sum_parts.1.own_ref
  80.1 5.2 %collective-permute-start.3 = (bf16[120,128]{1,0:T(8,128)(2,1)S(1)}, bf16[120,128]{1,0:T(8,128)(2,1)S(1)}, u32[]{:S(2)}, u32[]{:S(2)}) collective-permute-start(bf16[120,128]{1,0:T(8,128)(2,1)S(1)} %sum_parts.1.own_ref), channel_id=1, source_target_pairs={{0,6},{2,0},{4,2},{6,4},{1,7},{3,1},{5,3},{7,5},{8,14},{10,8},{12,... | collective-permute-start | bytes 92168 | tf_op jit(solution)/shard_map/ppermute | solution.py:492
  85.3 1.2 collective-permute-start.2
  86.5 2.1 %collective-permute-start.1 = (bf16[120,128]{1,0:T(8,128)(2,1)S(1)}, bf16[120,128]{1,0:T(8,128)(2,1)S(1)}, u32[]{:S(2)}, u32[]{:S(2)}) collective-permute-start(bf16[120,128]{1,0:T(8,128)(2,1)S(1)} %sum_parts.1.own_ref), channel_id=1, source_target_pairs={{0,2},{2,4},{4,6},{6,0},{1,3},{3,5},{5,7},{7,1},{8,10},{10,12},{12... | collective-permute-start | bytes 92168 | tf_op jit(solution)/shard_map/ppermute | solution.py:492
  88.6 0.0 collective-permute-done.3.last_ref
  88.6 3.4 %collective-permute-done.2.across_ref = bf16[120,128]{1,0:T(8,128)(2,1)S(1)} collective-permute-done((bf16[120,128]{1,0:T(8,128)(2,1)S(1)}, bf16[120,128]{1,0:T(8,128)(2,1)S(1)}, u32[]{:S(2)}, u32[]{:S(2)}) %collective-permute-start.2) | collective-permute-done | bytes 30752 | tf_op jit(solution)/shard_map/ppermute | solution.py:492
  92.0 0.0 collective-permute-done.1.next_ref
  92.0 0.1 total_copies.1
  92.1 18.3 %all_to_all.28 = bf16[32,120,128]{2,1,0:T(8,128)(2,1)S(1)} all-to-all(bf16[32,120,128]{2,1,0:T(8,128)(2,1)S(1)} %total_copies.1), channel_id=1, replica_groups=mesh['y'=4,'x'=4,'core'=2,'far'=4,'near'=2] {'x','near','y'}, dimensions={0} | all-to-all | bytes 1966080 | tf_op jit(solution)/shard_map/all_to_all | solution.py:450
  110.4 3.3 %collective-permute-start.4 = (bf16[4,960,128]{2,1,0:T(8,128)(2,1)S(1)}, bf16[4,960,128]{2,1,0:T(8,128)(2,1)S(1)}, u32[]{:S(2)}, u32[]{:S(2)}) collective-permute-start(bf16[4,960,128]{2,1,0:T(8,128)(2,1)S(1)} %bitcast.20), channel_id=1, source_target_pairs={{0,8},{8,0},{1,9},{9,1},{2,10},{10,2},{3,11},{11,3},{4,12},{12,4},... | collective-permute-start | bytes 2949128 | tf_op jit(solution)/shard_map/ppermute | solution.py:454
  113.8 1.3 %unpack.2 = (f32[768,512]{1,0:T(8,128)}, f32[768,512]{1,0:T(8,128)}, f32[153,512]{1,0:T(8,128)}, f32[153,512]{1,0:T(8,128)}) custom-call(bf16[4,960,128]{2,1,0:T(8,128)(2,1)S(1)} %bitcast.21), custom_call_target="tpu_custom_call" | custom-call | flops 491520 | bytes 2949120 | tf_op jit(solution)/shard_map/unpack/pallas_call | solution.py:432
  115.1 0.9 collective-permute-done.4.half_ref
  116.0 1.3 %unpack.3 = (f32[768,512]{1,0:T(8,128)}, f32[768,512]{1,0:T(8,128)}, f32[153,512]{1,0:T(8,128)}, f32[153,512]{1,0:T(8,128)}) custom-call(bf16[4,960,128]{2,1,0:T(8,128)(2,1)S(1)} %collective-permute-done.4.half_ref, f32[768,512]{1,0:T(8,128)} %get-tuple-element.45.refs_0_, ...), custom_call_target="tpu_custom_call", output_to_operand_aliasing={{0}: (1, {}), {1}: (2, {}), {2}: (3, {}), {3}: (4, {})} | custom-call | flops 491520 | bytes 2949120 | tf_op jit(solution)/shard_map/unpack/pallas_call | solution.py:432
Async XLA Ops:
  22.5 6.0 %copy-start = (bf16[768,512]{1,0:T(8,128)(2,1)S(1)}, bf16[768,512]{1,0:T(8,128)(2,1)}, u32[]{:S(2)}) copy-start(bf16[768,512]{1,0:T(8,128)(2,1)} %self_one_ref.1) | copy-start | bytes 2359300
  22.5 6.0 %copy-start.1 = (bf16[768,512]{1,0:T(8,128)(2,1)S(1)}, bf16[768,512]{1,0:T(8,128)(2,1)}, u32[]{:S(2)}) copy-start(bf16[768,512]{1,0:T(8,128)(2,1)} %neigh_one_ref.1) | copy-start | bytes 2359300
  22.5 6.0 %copy-start.2 = (bf16[512,153]{0,1:T(8,128)(2,1)S(1)}, bf16[512,153]{0,1:T(8,128)(2,1)}, u32[]{:S(2)}) copy-start(bf16[512,153]{0,1:T(8,128)(2,1)} %param.15) | copy-start | bytes 470020
  22.5 6.0 %copy-start.3 = (bf16[512,153]{0,1:T(8,128)(2,1)S(1)}, bf16[512,153]{0,1:T(8,128)(2,1)}, u32[]{:S(2)}) copy-start(bf16[512,153]{0,1:T(8,128)(2,1)} %param.16) | copy-start | bytes 470020
  22.5 6.0 %copy-start.4 = (bf16[2,64,153]{2,1,0:T(8,128)(2,1)S(1)}, bf16[2,64,153]{2,1,0:T(8,128)(2,1)}, u32[]{:S(2)}) copy-start(bf16[2,64,153]{2,1,0:T(8,128)(2,1)} %cot_ref.1) | copy-start | bytes 117508
  22.5 6.0 %copy-start.5 = (s32[2,512]{1,0:T(2,128)S(1)}, s32[2,512]{1,0:T(2,128)}, u32[]{:S(2)}) copy-start(s32[2,512]{1,0:T(2,128)} %targets_ref.1) | copy-start | bytes 12292
  22.6 6.0 %copy-start.6 = (s32[2,1,32]{2,1,0:T(1,128)S(1)}, s32[2,1,32]{2,1,0:T(1,128)}, u32[]{:S(2)}) copy-start(s32[2,1,32]{2,1,0:T(1,128)} %param.17) | copy-start | bytes 772
  22.6 6.0 %copy-start.7 = (s32[2,64]{1,0:T(2,128)S(1)}, s32[2,64]{1,0:T(2,128)}, u32[]{:S(2)}) copy-start(s32[2,64]{1,0:T(2,128)} %degree_ref.1) | copy-start | bytes 1540
  22.6 26.7 %all-to-all-start.1 = ((bf16[32,2,16,768]{3,2,1,0:T(8,128)(2,1)}), bf16[32,2,16,768]{3,2,1,0:T(8,128)(2,1)S(1)}, u32[]{:S(2)}, u32[]{:S(2)}) async-start(bf16[32,2,16,768]{3,2,1,0:T(8,128)(2,1)} %bitcast.31), calls=%async_computation.1 | async-start | bytes 3145728 | tf_op jit(solution)/shard_map/all_to_all | solution.py:450
  56.2 4.5 %collective-permute-start = (bf16[960,512]{1,0:T(8,128)(2,1)S(1)}, bf16[960,512]{1,0:T(8,128)(2,1)S(1)}, u32[]{:S(2)}, u32[]{:S(2)}) collective-permute-start(bf16[960,512]{1,0:T(8,128)(2,1)S(1)} %get-tuple-element.44), channel_id=1, source_target_pairs={{0,8},{8,0},{1,9},{9,1},{2,10},{10,2},{3,11},{11,3},{4,12},{12,4},... | collective-permute-start | bytes 2949128 | tf_op jit(solution)/shard_map/ppermute | solution.py:454
  80.1 8.5 %collective-permute-start.3 = (bf16[120,128]{1,0:T(8,128)(2,1)S(1)}, bf16[120,128]{1,0:T(8,128)(2,1)S(1)}, u32[]{:S(2)}, u32[]{:S(2)}) collective-permute-start(bf16[120,128]{1,0:T(8,128)(2,1)S(1)} %sum_parts.1.own_ref), channel_id=1, source_target_pairs={{0,6},{2,0},{4,2},{6,4},{1,7},{3,1},{5,3},{7,5},{8,14},{10,8},{12,... | collective-permute-start | bytes 92168 | tf_op jit(solution)/shard_map/ppermute | solution.py:492
  85.3 6.7 %collective-permute-start.2 = (bf16[120,128]{1,0:T(8,128)(2,1)S(1)}, bf16[120,128]{1,0:T(8,128)(2,1)S(1)}, u32[]{:S(2)}, u32[]{:S(2)}) collective-permute-start(bf16[120,128]{1,0:T(8,128)(2,1)S(1)} %sum_parts.1.own_ref), channel_id=1, source_target_pairs={{0,4},{2,6},{4,0},{6,2},{1,5},{3,7},{5,1},{7,3},{8,12},{10,14},{12... | collective-permute-start | bytes 92168 | tf_op jit(solution)/shard_map/ppermute | solution.py:492
  86.5 5.5 %collective-permute-start.1 = (bf16[120,128]{1,0:T(8,128)(2,1)S(1)}, bf16[120,128]{1,0:T(8,128)(2,1)S(1)}, u32[]{:S(2)}, u32[]{:S(2)}) collective-permute-start(bf16[120,128]{1,0:T(8,128)(2,1)S(1)} %sum_parts.1.own_ref), channel_id=1, source_target_pairs={{0,2},{2,4},{4,6},{6,0},{1,3},{3,5},{5,7},{7,1},{8,10},{10,12},{12... | collective-permute-start | bytes 92168 | tf_op jit(solution)/shard_map/ppermute | solution.py:492
  110.4 5.5 %collective-permute-start.4 = (bf16[4,960,128]{2,1,0:T(8,128)(2,1)S(1)}, bf16[4,960,128]{2,1,0:T(8,128)(2,1)S(1)}, u32[]{:S(2)}, u32[]{:S(2)}) collective-permute-start(bf16[4,960,128]{2,1,0:T(8,128)(2,1)S(1)} %bitcast.20), channel_id=1, source_target_pairs={{0,8},{8,0},{1,9},{9,1},{2,10},{10,2},{3,11},{11,3},{4,12},{12,4},... | collective-permute-start | bytes 2949128 | tf_op jit(solution)/shard_map/ppermute | solution.py:454
